TPU v7x, 128 devices: a whole 4x4x4 slice. The times are simulated.
128 devices in a mesh: memory: 4 (over z), context: 16 (over x, y), dp: 2 (over core).
Axes of the slice: x: 4, y: 4, z: 4, core: 2. Of those that a mesh axis runs over, the one named last changes fastest.
Arguments:
- hidden: bfloat16 [32, 512, 4096], P(('context', 'dp'), 'memory'), may hold values from -6 to 6
- queries: bfloat16 [32, 512, 2048], P(('context', 'dp'), 'memory'), may hold values from -6 to 6
- route_ids: int32 [32, 512, 2], P(('context', 'dp'), 'memory'), may hold values from 0 to 3, all different within a row; in each aligned block of 128 rows (0 to 127, 128 to 255, ..., all dimensions but the last counted through in order) at most 80 rows name the same one
- router_weight: bfloat16 [4096, 4], replicated, may hold values from -0.09375 to 0.09375
- key_weight: bfloat16 [4, 4096, 2048], P('memory', None, 'dp'), may hold values from -0.09375 to 0.09375
- value_weight: bfloat16 [4, 4096, 2048], P('memory', None, 'dp'), may hold values from -0.09375 to 0.09375
- decay_weight: bfloat16 [4, 4096, 16], P('memory', None, 'dp'), may hold values from -0.046875 to 0.046875
- decay_bias: float32 [4, 16], P('memory', 'dp'), may hold values from 3 to 14
- norm_gain: float32 [2048], replicated, may hold values from 0.5 to 1.5
Outputs:
- mixed: bfloat16 [32, 512, 2048], P(('context', 'dp'), 'memory')
Inputs may be any that keep to these rules, and one draw needn't show every extreme that they name: `route_ids`: each token names 2 different memories. Within the tokens of one device (aligned blocks of 128 tokens in token order) no memory is named by more than 80 tokens, and in some such block one memory is named exactly 80 times.
All inputs are finite; a program needn't handle non-finite values.
Results may differ from a plain program's by a relative error of at most 0.0085.
Values may be sent and summed in bfloat16 or wider, within the bound.
No kernel may reach another device: no remote copies, remote signals or barrier semaphores. Data moves between devices by JAX's collectives and lax.ppermute only.
A program may use at most 128 MiB of HBM per device.

v0:
```python
import jax
import jax.numpy as jnp
from jax import lax
from jax.sharding import PartitionSpec as P

D = 4096
HEAD_DIM = 128
TOP = 2
BLOCK = 64
CAP = 80


HIGHER = lax.Precision.HIGH


def carried_in(shard, axis, combine, identity):
    devices, mine = (lax.axis_size(axis), lax.axis_index(axis))
    everything = jax.tree.map(
        lambda part, kind: lax.all_gather(part.astype(kind), axis),
        shard,
        (jnp.bfloat16, jnp.bfloat16),
    )
    start = jax.tree.map(
        lambda part, zero: jnp.broadcast_to(jnp.asarray(zero, part.dtype), part.shape),
        shard,
        identity,
    )

    def step(k, before):
        reached = k < mine
        new = combine(
            before, jax.tree.map(lambda part, own: part[k].astype(own.dtype), everything, shard)
        )
        return jax.tree.map(lambda a, b: jnp.where(reached, a, b), new, before)

    return lax.fori_loop(0, devices, step, start)


def block_scan(query_all, unit_all, value_all, decay_all):
    seq_len, head_count, head_width = query_all.shape
    block_count = seq_len // BLOCK

    def shaped(tensor):
        return tensor.reshape((block_count, BLOCK) + tensor.shape[1:])

    causal = jnp.arange(BLOCK)[:, None] >= jnp.arange(BLOCK)[None, :]

    def advance(carry, pieces):
        memory_state, running = carry
        query_blk, unit_blk, value_blk, decay_blk = pieces
        cumulative = jnp.cumsum(decay_blk, axis=0)
        spread = cumulative[:, None, :] - cumulative[None, :, :]
        weights = jnp.exp(jnp.where(causal[:, :, None], spread, -1e30))
        scores = (
            jnp.einsum("ihd,jhd->ijh", query_blk, unit_blk, preferred_element_type=jnp.float32)
            * weights
        )
        scores = scores.astype(jnp.bfloat16)
        inner = jnp.einsum("ijh,jhe->ihe", scores, value_blk, preferred_element_type=jnp.float32)
        carried = jnp.exp(cumulative)[:, :, None] * jnp.einsum(
            "ihd,hde->ihe", query_blk.astype(jnp.float32), memory_state, precision=HIGHER
        )
        last_sum = cumulative[-1]
        faded = jnp.exp(last_sum[None, :] - cumulative)[:, :, None] * unit_blk.astype(jnp.float32)
        memory_state = jnp.exp(last_sum)[:, None, None] * memory_state + jnp.einsum(
            "jhd,jhe->hde", faded, value_blk.astype(jnp.float32), precision=HIGHER
        )
        return (
            (memory_state, running + last_sum),
            (inner + carried, running[None, :] + cumulative),
        )

    start_state = jnp.zeros((head_count, head_width, head_width), jnp.float32)
    start_total = jnp.zeros((head_count,), jnp.float32)
    pieces = (shaped(query_all), shaped(unit_all), shaped(value_all), shaped(decay_all))
    (end_state, end_total), (outputs, positions) = lax.scan(
        advance, (start_state, start_total), pieces
    )
    return (
        outputs.reshape(seq_len, head_count, head_width),
        positions.reshape(seq_len, head_count),
        end_state,
        end_total,
    )


def project_rows(hidden_rows, key_matrix, value_matrix, decay_matrix, decay_shift, live_slots):
    seq_len = hidden_rows.shape[0]
    head_count = decay_matrix.shape[1]
    keys_low = jnp.dot(hidden_rows, key_matrix, preferred_element_type=jnp.float32).astype(
        jnp.bfloat16
    )
    values_low = jnp.dot(hidden_rows, value_matrix, preferred_element_type=jnp.float32).astype(
        jnp.bfloat16
    )
    gate_logit = (
        jnp.dot(hidden_rows, decay_matrix, preferred_element_type=jnp.float32)
        + decay_shift[None, :]
    )
    decays = jax.nn.log_sigmoid(gate_logit) * live_slots[:, None]
    keys_full = keys_low.astype(jnp.float32).reshape(seq_len, head_count, HEAD_DIM)
    unit_keys = keys_full * lax.rsqrt(
        jnp.sum(keys_full * keys_full, axis=-1, keepdims=True) + 1e-06
    )
    unit_keys = (unit_keys * live_slots[:, None, None]).astype(jnp.bfloat16)
    values_out = values_low.reshape(seq_len, head_count, HEAD_DIM)
    return (unit_keys, values_out, decays)


def shards(
    hidden,
    queries,
    route_ids,
    router_weight,
    key_weight,
    value_weight,
    decay_weight,
    decay_bias,
    norm_gain,
):
    token_rows = hidden[0]
    query_rows = queries[0]
    route_list = route_ids[0]
    row_count = token_rows.shape[0]
    owner_count = lax.axis_size("memory")
    dp_size = lax.axis_size("dp")
    query_width = query_rows.shape[1]
    half_width = query_width // dp_size
    local_heads = decay_bias.shape[1]
    member = (route_list[:, :, None] == jnp.arange(owner_count)[None, None, :]).astype(jnp.int32)
    per_row = jnp.sum(member, axis=1)
    earlier = jnp.cumsum(per_row, axis=0) - per_row
    slot_place = jnp.sum(member * earlier[:, None, :], axis=-1)
    counts = jnp.sum(per_row, axis=0)
    target = (route_list * CAP + slot_place).reshape(-1)
    send_rows = (
        jnp.zeros((owner_count * CAP, D), jnp.bfloat16)
        .at[target]
        .set(jnp.repeat(token_rows, TOP, axis=0))
        .reshape(owner_count, CAP, D)
    )
    send_query = (
        jnp.zeros((owner_count * CAP, query_width), jnp.bfloat16)
        .at[target]
        .set(jnp.repeat(query_rows, TOP, axis=0))
        .reshape(owner_count, CAP, query_width)
    )
    rows_mid, query_mid, count_mid = (
        lax.all_to_all(send_rows, "memory", split_axis=0, concat_axis=0, tiled=True),
        lax.all_to_all(send_query, "memory", split_axis=0, concat_axis=0, tiled=True),
        lax.all_to_all(counts[:, None], "memory", split_axis=0, concat_axis=0, tiled=True),
    )
    rows_in, count_in = (
        lax.all_gather(rows_mid[None], "dp", axis=0, tiled=True),
        lax.all_gather(count_mid[None], "dp", axis=0, tiled=True),
    )
    count_in = count_in[:, :, 0]
    query_split = query_mid.reshape(owner_count, CAP, dp_size, half_width).transpose(2, 0, 1, 3)
    query_in = lax.all_to_all(query_split, "dp", split_axis=0, concat_axis=0, tiled=True)
    slot_total = dp_size * owner_count * CAP
    live_slots = (
        (jnp.arange(CAP)[None, None, :] < count_in[:, :, None]).reshape(-1).astype(jnp.float32)
    )
    query_local = query_in.reshape(slot_total, local_heads, HEAD_DIM)
    unit_keys, values_out, decays = project_rows(
        rows_in.reshape(slot_total, D),
        key_weight[0],
        value_weight[0],
        decay_weight[0],
        decay_bias[0],
        live_slots,
    )
    outputs, positions, end_state, end_total = block_scan(
        query_local, unit_keys, values_out, decays
    )

    def combine(former, latter):
        return (former[0] + latter[0], jnp.exp(latter[0])[:, None, None] * former[1] + latter[1])

    identity = (jnp.zeros_like(end_total), jnp.zeros_like(end_state))
    entry_state = carried_in((end_total, end_state), "context", combine, identity)[1]
    outputs = outputs + jnp.exp(positions)[:, :, None] * jnp.einsum(
        "lhd,hde->lhe", query_local.astype(jnp.float32), entry_state, precision=HIGHER
    )
    slot_reads = (
        outputs.reshape(slot_total, half_width)
        .astype(jnp.bfloat16)
        .reshape(dp_size, owner_count, CAP, half_width)
    )
    returned = lax.all_to_all(
        lax.all_to_all(slot_reads, "memory", split_axis=1, concat_axis=1, tiled=True),
        "dp",
        split_axis=0,
        concat_axis=3,
        tiled=True,
    )[0]
    picked = (
        returned.reshape(owner_count * CAP, query_width)[target]
        .reshape(row_count, TOP, query_width)
        .astype(jnp.float32)
    )
    router = jnp.dot(token_rows, router_weight, preferred_element_type=jnp.float32)
    chosen = jax.nn.sigmoid(jnp.take_along_axis(router, route_list, axis=1))
    gates = chosen / jnp.sum(chosen, axis=1, keepdims=True)
    mixture = jnp.sum(gates[:, :, None] * picked, axis=1)
    per_head = mixture.reshape(row_count, query_width // HEAD_DIM, HEAD_DIM)
    per_head = per_head * lax.rsqrt(jnp.mean(per_head * per_head, axis=-1, keepdims=True) + 1e-05)
    result = per_head * norm_gain.reshape(query_width // HEAD_DIM, HEAD_DIM)[None]
    return result.reshape(row_count, query_width).astype(jnp.bfloat16)[None]


def solution(mesh):
    in_specs = (
        P(("context", "dp"), "memory", None),
        P(("context", "dp"), "memory", None),
        P(("context", "dp"), "memory", None),
        P(),
        P("memory", None, "dp"),
        P("memory", None, "dp"),
        P("memory", None, "dp"),
        P("memory", "dp"),
        P(),
    )
    out_specs = P(("context", "dp"), "memory", None)
    return jax.shard_map(shards, mesh=mesh, in_specs=in_specs, out_specs=out_specs, check_vma=False)
```

profile of v0, /device:TPU:1, one launch (start us, length us, event | category | flops | bytes accessed | tf_op | source)
XLA Modules:
  0.0 318.4 jit_solution(14469372680665920904)
XLA Ops:
  9.6 3.3 %broadcast_in_dim.52 = bf16[128,2,4096]{2,1,0:T(2,128)(2,1)S(1)} broadcast(bf16[128,4096]{1,0:T(8,128)(2,1)} %bitcast.190), dimensions={0,2} | broadcast | bytes 3145728 | tf_op jit(solution)/shard_map/broadcast_in_dim | solution.py:139
  15.2 5.3 %scatter_custom_fusion = bf16[320,4096]{1,0:T(8,128)(2,1)S(1)} fusion(s32[256]{0:T(256)S(1)} %bitcast.200, bf16[256,4096]{1,0:T(8,128)(2,1)} %reshape.365, bf16[]{:T(256)} %constant.88.clone.1), kind=kCustom, calls=%fused_computation.70 | custom fusion | bytes 2621952 | tf_op jit(solution)/shard_map/scatter | solution.py:139
  20.5 36.8 %all_to_all.44 = bf16[4,80,4096]{2,1,0:T(8,128)(2,1)} all-to-all(bf16[4,80,4096]{2,1,0:T(8,128)(2,1)S(1)} %bitcast.179), channel_id=1, replica_groups=mesh['memory'=4,'context'=16,'dp'=2] {'memory'}, dimensions={0} | all-to-all | bytes 5242880 | tf_op jit(solution)/shard_map/all_to_all | solution.py:149
  58.0 3.2 %all-to-all-start.1 = ((s32[4,1,1]{2,1,0:T(1,128)}), s32[4,1,1]{2,1,0:T(1,128)S(1)}, u32[]{:S(2)}, u32[]{:S(2)}) async-start(s32[4,1,1]{2,1,0:T(1,128)} %copy.211), calls=%async_computation.1 | async-start | bytes 4096 | tf_op jit(solution)/shard_map/all_to_all | solution.py:151
  62.3 3.3 %scatter_custom_fusion.1 = bf16[320,2048]{1,0:T(8,128)(2,1)} fusion(s32[256]{0:T(256)S(1)} %bitcast.201, bf16[256,2048]{1,0:T(8,128)(2,1)S(1)} %reshape.373, bf16[]{:T(256)} %constant.88.clone.1), kind=kCustom, calls=%fused_computation.78 | custom fusion | bytes 1310722 | tf_op jit(solution)/shard_map/scatter | solution.py:145
  65.6 4.2 %all-to-all-start.2 = ((bf16[4,80,2048]{2,1,0:T(8,128)(2,1)}), bf16[4,80,2048]{2,1,0:T(8,128)(2,1)S(1)}, u32[]{:S(2)}, u32[]{:S(2)}) async-start(bf16[4,80,2048]{2,1,0:T(8,128)(2,1)} %bitcast.14), calls=%async_computation.2 | async-start | bytes 2621440 | tf_op jit(solution)/shard_map/all_to_all | solution.py:150
  71.5 3.9 %all-reduce = s32[8]{0:T(128)S(1)} all-reduce(s32[8]{0:T(128)S(1)} %dynamic-update-slice), channel_id=3, replica_groups=mesh['memory'=4,'context'=16,'dp'=2] {'dp'}, use_global_device_ids=true, to_apply=%add | all-reduce | flops 8 | bytes 64
  75.7 9.6 %all-to-all-done.2 = bf16[4,80,2048]{2,1,0:T(8,128)(2,1)S(1)} async-done(((bf16[4,80,2048]{2,1,0:T(8,128)(2,1)}), bf16[4,80,2048]{2,1,0:T(8,128)(2,1)S(1)}, u32[]{:S(2)}, u32[]{:S(2)}) %all-to-all-start.2) | async-done | bytes 1310752 | tf_op jit(solution)/shard_map/all_to_all | solution.py:150
  86.7 7.8 %all_to_all.45 = bf16[2,4,80,1024]{3,2,1,0:T(8,128)(2,1)S(1)} all-to-all(bf16[2,4,80,1024]{3,2,1,0:T(8,128)(2,1)S(1)} %copy.215), channel_id=1, replica_groups=mesh['memory'=4,'context'=16,'dp'=2] {'dp'}, dimensions={0} | all-to-all | bytes 2621440 | tf_op jit(solution)/shard_map/all_to_all | solution.py:159
  96.0 9.5 %fusion.44 = bf16[640,1024]{1,0:T(8,128)(2,1)S(1)} fusion(bf16[640,4096]{1,0:T(8,128)(2,1)} %bitcast.183, bf16[1,4096,1024]{2,1,0:T(8,128)(2,1)} %param.17), kind=kOutput, calls=%fused_computation.66 | convolution fusion | flops 5369364480 | bytes 14942208 | tf_op jit(solution)/shard_map/dot_general | solution.py:90
  114.6 4.0 %fusion.63 = f32[640,8]{0,1:T(8,128)S(1)} fusion(bf16[640,4096]{1,0:T(8,128)(2,1)} %bitcast.184, bf16[1,4096,8]{1,2,0:T(8,128)(2,1)S(1)} %copy-done, f32[640]{0:T(1024)S(1)} %reshape.344, f32[8]{0:T(128)S(1)} %bitcast.204), kind=kOutput, calls=%fused_computation.83 | convolution fusion | flops 41994240 | bytes 5331488 | tf_op jit(solution)/shard_map/dot_general | solution.py:97
  118.7 9.5 %fusion.50 = bf16[80,8,8,128]{3,1,2,0:T(8,128)(2,1)S(1)} fusion(bf16[640,4096]{1,0:T(8,128)(2,1)} %bitcast.185, bf16[1,4096,1024]{2,1,0:T(8,128)(2,1)} %param.18), kind=kOutput, calls=%fused_computation.68 | convolution fusion | flops 5369364480 | bytes 14942208 | tf_op jit(solution)/shard_map/dot_general | solution.py:93
  131.8 58.7 %while.31 = (s32[]{:T(128)}, f32[8,128,128]{2,1,0:T(8,128)S(1)}, f32[8]{0:T(128)S(1)}, f32[10,64,8,128]{3,2,1,0:T(8,128)}, f32[10,64,8]{2,1,0:T(8,128)}, /*index...) while((s32[]{:T(128)}, f32[8,128,128]{2,1,0:T(8,128)S(1)}, ...), condition=%wide.region_10.11_spmd.clone, body=%wide.region_8.10_spmd.clone.sunk | while | flops 118395408 | bytes 4282829 | solution.py:76
  192.8 34.1 %all-reduce.1 = bf16[128]{0:T(256)(128)(2,1)S(1)} all-reduce(bf16[128]{0:T(256)(128)(2,1)S(1)} %dynamic-update-slice.1), channel_id=4, replica_groups=mesh['memory'=4,'context'=16,'dp'=2] {'context'}, use_global_device_ids=true, to_apply=%add.1 | all-reduce | flops 128 | bytes 512
  227.0 2.6 copy.223
  230.7 11.5 %all-gather.9.cloned.1.call-done = bf16[128,128,128]{2,1,0:T(8,128)(2,1)} async-done(((bf16[8,128,128]{2,1,0:T(8,128)(2,1)}), bf16[128,128,128]{2,1,0:T(8,128)(2,1)}) %all-gather.9.cloned.1.call-update) | async-done | bytes 4194320 | tf_op jit(solution)/shard_map/all_gather | solution.py:19
  242.2 18.1 %while.32 = (s32[]{:T(128)}, f32[8,128,128]{2,1,0:T(8,128)S(1)}, s32[]{:T(128)}, bf16[16,8]{1,0:T(8,128)(2,1)S(1)}, bf16[16,8,128,128]{3,2,1,0:T(8,128)(2,1)}, /*index=5*/s32[]{:T(128)}, s32[]{:T(128)}) while((s32[]{:T(128)}, f32[8,128,128]{2,1,0:T(8,128)S(1)}, s32[]{:T(128)}, bf16[16,8]{1,0:T(8,128)(2,1)S(1)}, ...), condition=%wide.region_12.13_spmd.clone, body=%wide.region_11.12_spmd.clone.sunk | while | flops 655372 | bytes 1310905 | solution.py:36
  260.3 3.5 %fusion.41 = bf16[640,8,128]{0,2,1:T(8,128)(2,1)} fusion(f32[640,8,128]{0,2,1:T(8,128)S(1)} %copy.223, f32[8,128,128]{2,1,0:T(8,128)S(1)} %get-tuple-element.158, bf16[640,8,128]{2,1,0:T(8,128)(2,1)} %bitcast.182, f32[640,8]{0,1:T(8,128)S(1)} %copy.220), kind=kOutput, calls=%fused_computation.61 | convolution fusion | flops 505282560 | bytes 5787648 | tf_op jit(solution)/shard_map/lhd,hde->lhe/dot_general | solution.py:182
  263.8 5.5 %reshape.395 = bf16[2,4,80,1024]{2,1,0,3:T(4,128)(2,1)S(1)} reshape(bf16[640,8,128]{0,2,1:T(8,128)(2,1)} %fusion.41) | data formatting | bytes 2621440 | tf_op jit(solution)/shard_map/convert_element_type | solution.py:187
  269.4 2.9 copy.225
  272.3 4.0 %all-to-all-start.4 = ((bf16[2,4,80,1024]{3,2,0,1:T(8,128)(2,1)}), bf16[2,4,80,1024]{3,2,0,1:T(8,128)(2,1)S(1)}, u32[]{:S(2)}, u32[]{:S(2)}) async-start(bf16[2,4,80,1024]{3,2,0,1:T(8,128)(2,1)} %copy.225), calls=%async_computation.4 | async-start | bytes 2621440 | tf_op jit(solution)/shard_map/all_to_all | solution.py:191
  279.8 13.5 %all-to-all-done.4 = bf16[2,4,80,1024]{3,2,0,1:T(8,128)(2,1)S(1)} async-done(((bf16[2,4,80,1024]{3,2,0,1:T(8,128)(2,1)}), bf16[2,4,80,1024]{3,2,0,1:T(8,128)(2,1)S(1)}, u32[]{:S(2)}, u32[]{:S(2)}) %all-to-all-start.4) | async-done | bytes 1310752 | tf_op jit(solution)/shard_map/all_to_all | solution.py:191
  293.4 6.3 %all_to_all.46 = bf16[2,4,80,1024]{3,2,1,0:T(8,128)(2,1)S(1)} all-to-all(bf16[2,4,80,1024]{3,2,1,0:T(8,128)(2,1)S(1)} %copy.226), channel_id=1, replica_groups=mesh['memory'=4,'context'=16,'dp'=2] {'dp'}, dimensions={0} | all-to-all | bytes 2621440 | tf_op jit(solution)/shard_map/all_to_all | solution.py:190
  306.2 3.1 multiply_reduce_fusion
  (291 shorter events, 114.9 us)
Async XLA Ops:
  6.5 108.1 %copy-start = (bf16[1,4096,8]{1,2,0:T(8,128)(2,1)S(1)}, bf16[1,4096,8]{1,2,0:T(8,128)(2,1)}, u32[]{:S(2)}) copy-start(bf16[1,4096,8]{1,2,0:T(8,128)(2,1)} %param.19) | copy-start | bytes 196612
  6.5 89.4 %all-gather.7.cloned.1.call-start = ((), (), s32[]{:S(2)}) async-start(), calls=%async_computation.6 | async-start | bytes 7864320 | tf_op jit(solution)/shard_map/all_gather | solution.py:154
  15.2 47.1 %copy-start.8 = (s32[256,1]{0,1:T(1,128)}, s32[256,1]{0,1:T(1,128)S(1)}, u32[]{:S(2)}) copy-start(s32[256,1]{0,1:T(1,128)S(1)} %compare_select_fusion.1) | copy-start | bytes 3076
  57.3 3.9 %copy-start.4 = (bf16[1,128,2048]{2,1,0:T(8,128)(2,1)S(1)}, bf16[1,128,2048]{2,1,0:T(8,128)(2,1)}, u32[]{:S(2)}) copy-start(bf16[1,128,2048]{2,1,0:T(8,128)(2,1)} %param.14) | copy-start | bytes 1572868
  58.0 7.6 %all-to-all-start.1 = ((s32[4,1,1]{2,1,0:T(1,128)}), s32[4,1,1]{2,1,0:T(1,128)S(1)}, u32[]{:S(2)}, u32[]{:S(2)}) async-start(s32[4,1,1]{2,1,0:T(1,128)} %copy.211), calls=%async_computation.1 | async-start | bytes 4096 | tf_op jit(solution)/shard_map/all_to_all | solution.py:151
  61.9 8.0 %copy-start.12 = (u32[128]{0:T(128)S(1)}, u32[128]{0:T(128)}, u32[]{:S(2)}) copy-start(u32[128]{0:T(128)} %constant.118) | copy-start | bytes 1540
  65.6 19.7 %all-to-all-start.2 = ((bf16[4,80,2048]{2,1,0:T(8,128)(2,1)}), bf16[4,80,2048]{2,1,0:T(8,128)(2,1)S(1)}, u32[]{:S(2)}, u32[]{:S(2)}) async-start(bf16[4,80,2048]{2,1,0:T(8,128)(2,1)} %bitcast.14), calls=%async_computation.2 | async-start | bytes 2621440 | tf_op jit(solution)/shard_map/all_to_all | solution.py:150
  69.8 172.4 %all-gather.9.cloned.1.call-start = ((), (), s32[]{:S(2)}) async-start(), calls=%async_computation.7 | async-start | bytes 4456448 | tf_op jit(solution)/shard_map/all_gather | solution.py:19
  112.4 2.2 copy-start.10
  128.3 1.7 copy-start.2
  131.8 59.4 %copy-start.11 = (u32[128]{0:T(128)S(1)}, u32[128]{0:T(128)}, u32[]{:S(2)}) copy-start(u32[128]{0:T(128)} %constant.123) | copy-start | bytes 1540
  269.4 6.9 %copy-start.6 = (s32[1,128,2]{1,2,0:T(2,128)S(1)}, s32[1,128,2]{1,2,0:T(2,128)}, u32[]{:S(2)}) copy-start(s32[1,128,2]{1,2,0:T(2,128)} %param.15) | copy-start | bytes 3076
  269.4 7.2 %copy-start.3 = (bf16[1,128,4096]{2,1,0:T(8,128)(2,1)S(1)}, bf16[1,128,4096]{2,1,0:T(8,128)(2,1)}, u32[]{:S(2)}) copy-start(bf16[1,128,4096]{2,1,0:T(8,128)(2,1)} %param.13) | copy-start | bytes 3145732
  269.4 7.2 %copy-start.5 = (bf16[4096,4]{0,1:T(4,128)(2,1)S(1)}, bf16[4096,4]{0,1:T(4,128)(2,1)}, u32[]{:S(2)}) copy-start(bf16[4096,4]{0,1:T(4,128)(2,1)} %param.16) | copy-start | bytes 98308
  272.3 21.0 %all-to-all-start.4 = ((bf16[2,4,80,1024]{3,2,0,1:T(8,128)(2,1)}), bf16[2,4,80,1024]{3,2,0,1:T(8,128)(2,1)S(1)}, u32[]{:S(2)}, u32[]{:S(2)}) async-start(bf16[2,4,80,1024]{3,2,0,1:T(8,128)(2,1)} %copy.225), calls=%async_computation.4 | async-start | bytes 2621440 | tf_op jit(solution)/shard_map/all_to_all | solution.py:191
  277.0 2.8 copy-start.9
  309.5 1.1 copy-start.7
  310.1 1.4 copy-start.1
Sparse Core Ops, SparseCore 0:
  57.4 19.0 all-gather.6
  191.4 50.7 all-gather.8
where the time goes:
time: 320 us; the launch traced here: 318 us
  blocking collectives  88.9 us (28%)
  local copies, waits for them, and re-layouts  70.9 us (22%)
  matrix products  57.6 us (18%)
  other arithmetic  38.9 us (12%)
  waiting for transfers between devices  34.6 us (11%)
  between operations  15.2 us (5%)
  starting transfers between devices  11.4 us (4%)
    unnamed x2, blocking collectives  38 us
    all_to_all x1, blocking collectives, shards(): lax.all_to_all(send_rows, 'memory', split_axis=0, concat_axis=0, tiled=True)  36.8 us
    select_n x16, other arithmetic, step(): return jax.tree.map(lambda a, b: jnp.where(reached, a, b), new, before)  17.5 us
    dot_general x10, matrix products, advance(): jnp.einsum('jhd,jhe->hde', faded, value_blk.astype(jnp.float32), precisio...  14.8 us
    all_to_all x1, waiting for transfers between devices, shards(): lax.all_to_all(slot_reads, 'memory', split_axis=1, concat_axis=1, tiled=T...  13.5 us
    dot_general x10, matrix products, advance(): jnp.einsum('ijh,jhe->ihe', scores, value_blk, preferred_element_type=jnp....  13.1 us
    all_gather x1, waiting for transfers between devices, carried_in(): lax.all_gather(part.astype(kind), axis)  11.5 us
    unnamed x39, local copies, waits for them, and re-layouts  10 us
  transfers between devices with their start and end apart: 5, of which 3 were waited for; matrix products, arithmetic and copies ran while one was open for 5% of the time, Pallas kernels for 0%

commit v1 on v0

v1 whole, which is shorter than its diff:
```python
import functools

import jax
import jax.numpy as jnp
from jax import lax
from jax.experimental import pallas as pl
from jax.experimental.pallas import tpu as pltpu
from jax.sharding import PartitionSpec as P

D = 4096
HEAD_DIM = 128
CAP = 80
ROWS = 128
OWNERS = 4
CHUNKS = 8
SLOTS = CHUNKS * CAP
HALF = 1024
HEADS = HALF // HEAD_DIM
CONTEXTS = 16
LIVE = 128
PIECE = HALF // CONTEXTS
TAIL = 16
F32 = jnp.float32
BF16 = jnp.bfloat16
MIB = 1 << 20


def iota(shape, axis):
    return lax.broadcasted_iota(jnp.int32, shape, axis)


def dot(a, b):
    return jnp.dot(a, b, preferred_element_type=F32)


def source(owner, shift):
    return (owner + OWNERS - shift) & (OWNERS - 1)


def position(shift, partner, owner, core):
    return (core ^ partner) * OWNERS + source(owner, shift)


def membership(route):
    lane = iota((ROWS, 128), 1)
    named = ((route[:, 0:1] == lane) | (route[:, 1:2] == lane)).astype(F32)
    before = (iota((ROWS, ROWS), 0) > iota((ROWS, ROWS), 1)).astype(F32).astype(BF16)
    return named, dot(before, named.astype(BF16))


def pick_lane(table, lane_at):
    return jnp.sum(jnp.where(iota(table.shape, 1) == lane_at, table, 0.0), axis=1, keepdims=True)


def one_hot(named, slot, memory):
    live = pick_lane(named, memory) > 0.0
    place = pick_lane(slot, memory)
    match = (iota((ROWS, 128), 1).astype(F32) == place) & live
    return match.astype(F32)


def pack_rows_kernel(route_ref, rows_ref, *out_refs):
    owner = lax.axis_index("memory")
    named, slot = membership(route_ref[...])
    picks = [
        one_hot(named, slot, (owner + shift) & (OWNERS - 1)).T.astype(BF16)[:CAP]
        for shift in range(OWNERS)
    ]
    pick = jnp.concatenate(picks, axis=0)
    width = 512
    for column in range(0, D, width):
        part = dot(pick, rows_ref[:, column : column + width]).astype(BF16)
        for shift in range(OWNERS):
            out_refs[shift][:, column : column + width] = part[shift * CAP : (shift + 1) * CAP]
    live = dot(pick, jnp.ones((ROWS, LIVE), BF16)).astype(BF16)
    for shift in range(OWNERS):
        out_refs[shift][:, D:] = live[shift * CAP : (shift + 1) * CAP]


def pack_rows(route, rows):
    return pl.pallas_call(
        pack_rows_kernel,
        out_shape=[jax.ShapeDtypeStruct((CAP, D + LIVE), BF16)] * OWNERS,
        compiler_params=pltpu.CompilerParams(vmem_limit_bytes=24 * MIB),
        cost_estimate=pl.CostEstimate(
            flops=2 * 320 * 128 * D, bytes_accessed=4 * MIB, transcendentals=0
        ),
        name="pack_rows",
    )(route, rows)


def pack_queries_kernel(
    route_ref, other_route_ref, query_ref, other_query_ref, rows_ref, router_ref, *out_refs
):
    owner, core = lax.axis_index("memory"), lax.axis_index("dp")
    gates_ref = out_refs[OWNERS]
    mine = pl.multiple_of(core * HALF, HALF)
    for place, (routes, queries) in enumerate(
        ((route_ref, query_ref), (other_route_ref, other_query_ref))
    ):
        named, slot = membership(routes[...])
        picks = [
            one_hot(named, slot, (owner + shift) & (OWNERS - 1)).T.astype(BF16)[:CAP]
            for shift in range(OWNERS)
        ]
        pick = jnp.concatenate(picks, axis=0)
        part = dot(pick, queries[:, pl.ds(mine, HALF)]).astype(BF16)
        for shift in range(OWNERS):
            out_refs[shift][core ^ place] = part[shift * CAP : (shift + 1) * CAP]
        if place == 0:
            score = dot(rows_ref[...], router_ref[...])
            chosen = jax.nn.sigmoid(score) * named[:, :OWNERS]
            gates_ref[...] = jnp.zeros((ROWS, 128), F32)
            gates_ref[:, :OWNERS] = chosen / jnp.sum(chosen, axis=1, keepdims=True)


def pack_queries(route, other_route, queries, other_queries, rows, router_weight):
    return pl.pallas_call(
        pack_queries_kernel,
        out_shape=[jax.ShapeDtypeStruct((2, CAP, HALF), BF16)] * OWNERS
        + [jax.ShapeDtypeStruct((ROWS, 128), F32)],
        compiler_params=pltpu.CompilerParams(vmem_limit_bytes=24 * MIB),
        cost_estimate=pl.CostEstimate(
            flops=2 * 640 * 128 * HALF, bytes_accessed=4 * MIB, transcendentals=0
        ),
        name="pack_queries",
    )(route, other_route, queries, other_queries, rows, router_weight)


def log_sigmoid(x):
    small = jnp.exp(-jnp.abs(x))
    near = 1.0 + small
    log1p = jnp.where(near == 1.0, small, jnp.log(near) * (small / jnp.where(near == 1.0, 1.0, near - 1.0)))
    return jnp.minimum(x, 0.0) - log1p


def project_kernel(count, *refs):
    row_refs = refs[:count]
    key_ref, value_ref, decay_ref, bias_ref, unit_out, value_out, decay_out, held = refs[count:]

    @pl.when(pl.program_id(0) == 0)
    def _():
        for at in range(count):
            held[at * CAP : (at + 1) * CAP] = row_refs[at][:, :D]
        gate = dot(held[...], decay_ref[...]) + bias_ref[...]
        decay = log_sigmoid(gate)
        decay_out[...] = jnp.zeros_like(decay_out)
        for at in range(count):
            live = row_refs[at][:, D : D + HEADS].astype(F32)
            decay_out[at, :, :HEADS] = decay[at * CAP : (at + 1) * CAP] * live

    keys = dot(held[...], key_ref[...]).astype(BF16).astype(F32)
    width = keys.shape[1]
    for head in range(width // HEAD_DIM):
        columns = slice(head * HEAD_DIM, (head + 1) * HEAD_DIM)
        key = keys[:, columns]
        unit = key * lax.rsqrt(jnp.sum(key * key, axis=1, keepdims=True) + 1e-06)
        unit_out[:, :, columns] = unit.astype(BF16).reshape(count, CAP, HEAD_DIM)
    values = dot(held[...], value_ref[...]).astype(BF16)
    value_out[...] = values.reshape(count, CAP, width)


def project(row_parts, key_weight, value_weight, decay_weight, decay_bias):
    count = len(row_parts)
    width = 256
    whole = lambda shape: pl.BlockSpec(shape, lambda n: (0,) * len(shape))
    return pl.pallas_call(
        functools.partial(project_kernel, count),
        grid=(HALF // width,),
        in_specs=[whole((CAP, D + LIVE))] * count
        + [
            pl.BlockSpec((D, width), lambda n: (0, n)),
            pl.BlockSpec((D, width), lambda n: (0, n)),
            whole((D, HEADS)),
            whole((1, HEADS)),
        ],
        out_specs=[
            pl.BlockSpec((count, CAP, width), lambda n: (0, 0, n)),
            pl.BlockSpec((count, CAP, width), lambda n: (0, 0, n)),
            whole((count, CAP, 128)),
        ],
        out_shape=[
            jax.ShapeDtypeStruct((count, CAP, HALF), BF16),
            jax.ShapeDtypeStruct((count, CAP, HALF), BF16),
            jax.ShapeDtypeStruct((count, CAP, 128), F32),
        ],
        scratch_shapes=[pltpu.VMEM((count * CAP, D), BF16)],
        compiler_params=pltpu.CompilerParams(vmem_limit_bytes=30 * MIB),
        cost_estimate=pl.CostEstimate(
            flops=2 * count * CAP * D * 2 * HALF, bytes_accessed=18 * MIB, transcendentals=0
        ),
        name=f"project_{count}",
    )(*row_parts, key_weight, value_weight, decay_weight, decay_bias)


GROUPS = (((0, 0), (0, 1)), ((1, 0), (1, 1), (3, 0), (3, 1)), ((2, 0), (2, 1)))


def gather_order(refs, held, columns=slice(None)):
    owner, core = lax.axis_index("memory"), lax.axis_index("dp")
    for group, ref in zip(GROUPS, refs):
        for at, (shift, partner) in enumerate(group):
            held[position(shift, partner, owner, core)] = ref[at, :, columns]


def state_kernel(*refs):
    unit_refs, value_refs, decay_refs = refs[0:3], refs[3:6], refs[6:9]
    message, column_out, row_out, units, values, decays = refs[9:]
    step = pl.program_id(0)

    @pl.when(step == 0)
    def _():
        gather_order(decay_refs, decays)
        total = decays[...].reshape(SLOTS, 128).T[:HEADS]
        lane = iota((HEADS, SLOTS), 1)
        reach = 1
        while reach < SLOTS:
            total = total + jnp.where(lane >= reach, pltpu.roll(total, reach, 1), 0.0)
            reach *= 2
        row_out[...] = total
        column_out[...] = jnp.concatenate(
            [total, jnp.zeros((128 - HEADS, SLOTS), F32)], axis=0
        ).T

    gather_order(unit_refs, units)
    gather_order(value_refs, values)
    for at in range(2):
        head = step * 2 + at
        columns = slice(at * HEAD_DIM, (at + 1) * HEAD_DIM)
        running = pick_lane(column_out[...], head)
        last = running[SLOTS - 1 : SLOTS]
        unit = units[:, :, columns].reshape(SLOTS, HEAD_DIM).astype(F32)
        faded = (unit * jnp.exp(last - running)).astype(BF16)
        value = values[:, :, columns].reshape(SLOTS, HEAD_DIM)
        state = lax.dot_general(
            faded, value, (((0,), (0,)), ((), ())), preferred_element_type=F32
        ).astype(BF16)
        high = jnp.broadcast_to(last, (TAIL, 128)).astype(BF16).astype(F32)
        low = jnp.broadcast_to(last, (TAIL, 128)) - high
        tail = jnp.where(iota((TAIL, 128), 0) < TAIL // 2, high, low).astype(BF16)
        for part in range(2):
            message[at * 2 + part, :PIECE] = state[part * PIECE : (part + 1) * PIECE]
            message[at * 2 + part, PIECE:] = tail


def block_state(units, values, decays):
    whole = lambda shape: pl.BlockSpec(shape, lambda n: (0,) * len(shape))
    chunked = [pl.BlockSpec((len(group), CAP, 256), lambda n: (0, 0, n)) for group in GROUPS]
    return pl.pallas_call(
        state_kernel,
        grid=(HEADS // 2,),
        in_specs=chunked * 2 + [whole((len(group), CAP, 128)) for group in GROUPS],
        out_specs=[
            pl.BlockSpec((4, PIECE + TAIL, 128), lambda n: (n, 0, 0)),
            whole((SLOTS, 128)),
            whole((HEADS, SLOTS)),
        ],
        out_shape=[
            jax.ShapeDtypeStruct((CONTEXTS, PIECE + TAIL, 128), BF16),
            jax.ShapeDtypeStruct((SLOTS, 128), F32),
            jax.ShapeDtypeStruct((HEADS, SLOTS), F32),
        ],
        scratch_shapes=[
            pltpu.VMEM((CHUNKS, CAP, 256), BF16),
            pltpu.VMEM((CHUNKS, CAP, 256), BF16),
            pltpu.VMEM((CHUNKS, CAP, 128), F32),
        ],
        compiler_params=pltpu.CompilerParams(vmem_limit_bytes=24 * MIB),
        cost_estimate=pl.CostEstimate(
            flops=2 * SLOTS * HALF * 128, bytes_accessed=4 * MIB, transcendentals=SLOTS * HEADS
        ),
        name="block_state",
    )(*units, *values, *decays)


def prefix_kernel(message, entry):
    before = jnp.zeros((PIECE, 128), F32)
    for context in range(CONTEXTS):
        entry[context] = before.astype(BF16)
        high = message[context, PIECE : PIECE + 1].astype(F32)
        low = message[context, PIECE + TAIL // 2 : PIECE + TAIL // 2 + 1].astype(F32)
        before = jnp.exp(high + low) * before + message[context, :PIECE].astype(F32)


def prefix(message):
    return pl.pallas_call(
        prefix_kernel,
        out_shape=jax.ShapeDtypeStruct((CONTEXTS, PIECE, 128), BF16),
        cost_estimate=pl.CostEstimate(flops=1 << 20, bytes_accessed=1 << 20, transcendentals=0),
        name="prefix",
    )(message)


def inner_kernel(*refs):
    unit_refs, value_refs, query_refs = refs[0:3], refs[3:6], refs[6:10]
    column_ref, row_ref, inner, units, values, queries = refs[10:]
    step = pl.program_id(0)
    owner = lax.axis_index("memory")
    gather_order(unit_refs, units)
    gather_order(value_refs, values)
    for shift in range(OWNERS):
        for core in range(2):
            queries[core * OWNERS + source(owner, shift)] = query_refs[shift][core]
    tile = 2 * CAP
    for at in range(2):
        head = step * 2 + at
        columns = slice(at * HEAD_DIM, (at + 1) * HEAD_DIM)
        running = pick_lane(column_ref[...], head)
        running_row = row_ref[pl.ds(head, 1), :]
        unit = units[:, :, columns].reshape(SLOTS, HEAD_DIM)
        value = values[:, :, columns].reshape(SLOTS, HEAD_DIM)
        for block in range(SLOTS // tile):
            reach = -(-((block + 1) * tile) // 128) * 128
            query = queries[2 * block : 2 * block + 2, :, columns].reshape(tile, HEAD_DIM)
            score = lax.dot_general(
                query, unit[:reach], (((1,), (1,)), ((), ())), preferred_element_type=F32
            )
            spread = running[block * tile : (block + 1) * tile] - running_row[:, :reach]
            causal = iota((tile, reach), 0) + block * tile >= iota((tile, reach), 1)
            score = (score * jnp.exp(jnp.where(causal, spread, -1e30))).astype(BF16)
            result = dot(score, value[:reach])
            inner[2 * block : 2 * block + 2, :, columns] = result.reshape(2, CAP, HEAD_DIM)


def inner_reads(units, values, queries, column, row):
    whole = lambda shape: pl.BlockSpec(shape, lambda n: (0,) * len(shape))
    chunked = [pl.BlockSpec((len(group), CAP, 256), lambda n: (0, 0, n)) for group in GROUPS]
    return pl.pallas_call(
        inner_kernel,
        grid=(HEADS // 2,),
        in_specs=chunked * 2
        + [pl.BlockSpec((2, CAP, 256), lambda n: (0, 0, n))] * OWNERS
        + [whole((SLOTS, 128)), whole((HEADS, SLOTS))],
        out_specs=pl.BlockSpec((CHUNKS, CAP, 256), lambda n: (0, 0, n)),
        out_shape=jax.ShapeDtypeStruct((CHUNKS, CAP, HALF), F32),
        scratch_shapes=[pltpu.VMEM((CHUNKS, CAP, 256), BF16)] * 3,
        compiler_params=pltpu.CompilerParams(vmem_limit_bytes=24 * MIB),
        cost_estimate=pl.CostEstimate(
            flops=4 * SLOTS * SLOTS * HALF, bytes_accessed=8 * MIB, transcendentals=SLOTS * SLOTS * 4
        ),
        name="inner_reads",
    )(*units, *values, *queries, column, row)


def read_kernel(*refs):
    query_refs = refs[0:4]
    inner, column_ref, entry = refs[4:7]
    out_refs = refs[7:11]
    queries, reads = refs[11:]
    step = pl.program_id(0)
    owner = lax.axis_index("memory")
    for shift in range(OWNERS):
        for core in range(2):
            queries[core * OWNERS + source(owner, shift)] = query_refs[shift][core]
    for at in range(2):
        head = step * 2 + at
        columns = slice(at * HEAD_DIM, (at + 1) * HEAD_DIM)
        fade = jnp.exp(pick_lane(column_ref[...], head))
        carried = dot(queries[:, :, columns].reshape(SLOTS, HEAD_DIM), entry[at])
        result = inner[:, :, columns].reshape(SLOTS, HEAD_DIM) + fade * carried
        reads[:, :, columns] = result.astype(BF16).reshape(CHUNKS, CAP, HEAD_DIM)
    for shift in range(OWNERS):
        for core in range(2):
            out_refs[shift][core] = reads[core * OWNERS + source(owner, shift)]


def read_out(queries, inner, column, entry):
    whole = lambda shape: pl.BlockSpec(shape, lambda n: (0,) * len(shape))
    return pl.pallas_call(
        read_kernel,
        grid=(HEADS // 2,),
        in_specs=[pl.BlockSpec((2, CAP, 256), lambda n: (0, 0, n))] * OWNERS
        + [
            pl.BlockSpec((CHUNKS, CAP, 256), lambda n: (0, 0, n)),
            whole((SLOTS, 128)),
            pl.BlockSpec((2, 128, 128), lambda n: (n, 0, 0)),
        ],
        out_specs=[pl.BlockSpec((2, CAP, 256), lambda n: (0, 0, n))] * OWNERS,
        out_shape=[jax.ShapeDtypeStruct((2, CAP, HALF), BF16)] * OWNERS,
        scratch_shapes=[pltpu.VMEM((CHUNKS, CAP, 256), BF16)] * 2,
        compiler_params=pltpu.CompilerParams(vmem_limit_bytes=24 * MIB),
        cost_estimate=pl.CostEstimate(
            flops=2 * SLOTS * HALF * 128, bytes_accessed=6 * MIB, transcendentals=SLOTS * HEADS
        ),
        name="read_out",
    )(*queries, inner, column, entry)


def mix_kernel(route_ref, gates_ref, gain_ref, *refs):
    own_refs, other_refs, out_ref = refs[0:4], refs[4:8], refs[8]
    owner, core = lax.axis_index("memory"), lax.axis_index("dp")
    named, slot = membership(route_ref[...])
    picks, gates = [], []
    for shift in range(OWNERS):
        memory = (owner + shift) & (OWNERS - 1)
        picks.append(one_hot(named, slot, memory).astype(BF16)[:, :CAP])
        gates.append(pick_lane(gates_ref[...], memory))
    for place, reads in enumerate((own_refs, other_refs)):
        start = (core ^ place) * HALF
        mixture = jnp.zeros((ROWS, HALF), F32)
        for shift in range(OWNERS):
            mixture = mixture + gates[shift] * dot(picks[shift], reads[shift][core])
        for head in range(HEADS):
            columns = pl.ds(pl.multiple_of(start + head * HEAD_DIM, HEAD_DIM), HEAD_DIM)
            mix = mixture[:, head * HEAD_DIM : (head + 1) * HEAD_DIM]
            scale = lax.rsqrt(jnp.mean(mix * mix, axis=1, keepdims=True) + 1e-05)
            out_ref[:, columns] = (mix * scale * gain_ref[:, columns]).astype(BF16)


def mix_reads(route, gates, gain, own, other):
    return pl.pallas_call(
        mix_kernel,
        out_shape=jax.ShapeDtypeStruct((ROWS, 2 * HALF), BF16),
        compiler_params=pltpu.CompilerParams(vmem_limit_bytes=24 * MIB),
        cost_estimate=pl.CostEstimate(
            flops=2 * ROWS * 320 * 2 * HALF, bytes_accessed=4 * MIB, transcendentals=0
        ),
        name="mix_reads",
    )(route, gates, gain, *own, *other)


def hop(array, shift):
    return lax.ppermute(array, "memory", [(i, (i + shift) % OWNERS) for i in range(OWNERS)])


def swap(array):
    return lax.ppermute(array, "dp", [(0, 1), (1, 0)])


def shards(
    hidden,
    queries,
    route_ids,
    router_weight,
    key_weight,
    value_weight,
    decay_weight,
    decay_bias,
    norm_gain,
):
    rows, query_rows, route = hidden[0], queries[0], route_ids[0]
    weights = (key_weight[0], value_weight[0], decay_weight[0], decay_bias)

    packed = pack_rows(route, rows)
    arrived = {0: packed[0]}
    for shift in (1, 3, 2):
        arrived[shift] = hop(packed[shift], shift)
    other_route, other_query = swap(route), swap(query_rows)
    packed_query = pack_queries(route, other_route, query_rows, other_query, rows, router_weight)
    gates = packed_query[OWNERS]

    projected = []
    for group in GROUPS:
        parts = [swap(arrived[shift]) if partner else arrived[shift] for shift, partner in group]
        projected.append(project(parts, *weights))
    units, values, decays = zip(*projected)

    query_in = [packed_query[0]] + [hop(packed_query[shift], shift) for shift in (1, 2, 3)]
    message, column, row = block_state(units, values, decays)
    slices = lax.all_to_all(message, "context", 0, 0, tiled=True)
    entry = lax.all_to_all(prefix(slices), "context", 0, 0, tiled=True)
    inner = inner_reads(units, values, query_in, column, row)
    reads = read_out(query_in, inner, column, entry.reshape(HEADS, HEAD_DIM, HEAD_DIM))

    own = [reads[0]] + [hop(reads[shift], -shift) for shift in (1, 2, 3)]
    other = [swap(part) for part in own]
    return mix_reads(route, gates, norm_gain[None], own, other)[None]


def solution(mesh):
    in_specs = (
        P(("context", "dp"), "memory", None),
        P(("context", "dp"), "memory", None),
        P(("context", "dp"), "memory", None),
        P(),
        P("memory", None, "dp"),
        P("memory", None, "dp"),
        P("memory", None, "dp"),
        P("memory", "dp"),
        P(),
    )
    out_specs = P(("context", "dp"), "memory", None)
    return jax.shard_map(shards, mesh=mesh, in_specs=in_specs, out_specs=out_specs, check_vma=False)
```

time: 320 us -> 170 us (0.53)
  blocking collectives: 88.9 us -> 0 us
  matrix products: 57.6 us -> 0 us
  Pallas kernels: 0 us -> 47.3 us
  other arithmetic: 38.9 us -> 0 us
  local copies, waits for them, and re-layouts: 70.9 us -> 39.4 us
  starting transfers between devices: 11.4 us -> 42.2 us
  between operations: 15.2 us -> 0.34 us
  waiting for transfers between devices: 34.6 us -> 39.5 us
    dot_general x35 -> x0, matrix products: 57.6 us -> none  [the longest x10 14.8 us: advance(): jnp.einsum('jhd,jhe->hde', faded, value_blk.astype(jnp.float32), precisio...]
    all_to_all x3 -> x0, blocking collectives: 50.9 us -> none  [the longest x1 36.8 us: shards(): lax.all_to_all(send_rows, 'memory', split_axis=0, concat_axis=0, tiled=True)]
    pallas_call x0 -> x10, Pallas kernels: none -> 47.3 us  [the longest x3 25.4 us: project(): pl.pallas_call(functools.partial(project_kernel, count), grid=(HALF // wi...]
    ppermute x0 -> x19, waiting for transfers between devices: none -> 39.5 us  [the longest x9 37.8 us: hop(): lax.ppermute(array, 'memory', [(i, (i + shift) % OWNERS) for i in range(O...]
    unnamed x2 -> x0, blocking collectives: 38 us -> none
    unnamed x39 -> x91, local copies, waits for them, and re-layouts: 10 us -> 39.4 us
    ppermute x0 -> x19, starting transfers between devices: none -> 28.5 us  [the longest x10 14.6 us: swap(): return lax.ppermute(array, 'dp', [(0, 1), (1, 0)])]
    all_to_all x3 -> x2, waiting for transfers between devices: 23.1 us -> 0.01 us  [the longest x1 0.01 us: shards(): slices = lax.all_to_all(message, 'context', 0, 0, tiled=True)]
  transfers between devices with their start and end apart: 5 -> 21, of which waited for: 3 -> 7; matrix products, arithmetic and copies ran while one was open for 5% -> 1% of each run, Pallas kernels for 0% -> 24%
where the time goes in v1:
time: 170 us; the launch traced here: 169 us
  Pallas kernels  47.3 us (28%)
  starting transfers between devices  42.2 us (25%)
  waiting for transfers between devices  39.5 us (23%)
  local copies, waits for them, and re-layouts  39.4 us (23%)
    unnamed x91, local copies, waits for them, and re-layouts  39.4 us
    ppermute x9, waiting for transfers between devices, hop(): lax.ppermute(array, 'memory', [(i, (i + shift) % OWNERS) for i in range(O...  37.8 us
    pallas_call x3, Pallas kernels, project(): pl.pallas_call(functools.partial(project_kernel, count), grid=(HALF // wi...  25.4 us
    ppermute x10, starting transfers between devices, swap(): return lax.ppermute(array, 'dp', [(0, 1), (1, 0)])  14.6 us
    ppermute x9, starting transfers between devices, hop(): lax.ppermute(array, 'memory', [(i, (i + shift) % OWNERS) for i in range(O...  13.9 us
    all_to_all x1, starting transfers between devices, shards(): entry = lax.all_to_all(prefix(slices), 'context', 0, 0, tiled=True)  6.89 us
    pallas_call x1, Pallas kernels, inner_reads(): pl.pallas_call(inner_kernel, grid=(HEADS // 2,), in_specs=chunked * 2 + [...  6.82 us
    all_to_all x1, starting transfers between devices, shards(): slices = lax.all_to_all(message, 'context', 0, 0, tiled=True)  6.79 us
  transfers between devices with their start and end apart: 21, of which 7 were waited for; matrix products, arithmetic and copies ran while one was open for 1% of the time, Pallas kernels for 24%

profile of v1, /device:TPU:1, one launch (start us, length us, event | category | flops | bytes accessed | tf_op | source)
XLA Modules:
  0.0 168.6 jit_solution(3075487092090327686)
XLA Ops:
  2.0 2.2 %pack_rows.1 = (bf16[80,4224]{1,0:T(8,128)(2,1)}, bf16[80,4224]{1,0:T(8,128)(2,1)S(1)}, bf16[80,4224]{1,0:T(8,128)(2,1)S(1)}, bf16[80,4224]{1,0:T(8,128)(2,1)S(1)}) custom-call(s32[128,2]{1,0:T(8,128)S(1)} %bitcast.21, bf16[128,4096]{1,0:T(8,128)(2,1)S(1)} %bitcast.18), custom_call_target="tpu_custom_call" | custom-call | flops 335544320 | bytes 4194304 | tf_op jit(solution)/shard_map/pack_rows/pallas_call | solution.py:81
  4.2 4.4 %collective-permute-start.10 = (bf16[80,4224]{1,0:T(8,128)(2,1)S(1)}, bf16[80,4224]{1,0:T(8,128)(2,1)}, u32[]{:S(2)}, u32[]{:S(2)}) collective-permute-start(bf16[80,4224]{1,0:T(8,128)(2,1)S(1)} %get-tuple-element.40), channel_id=1, source_target_pairs={{0,64},{32,96},{64,0},{96,32},{1,65},{33,97},{65,1},{97,33},{2,66}... | collective-permute-start | bytes 2027528 | tf_op jit(solution)/shard_map/ppermute | solution.py:423
  12.8 10.9 %collective-permute-done.10.refs_0_ = bf16[80,4224]{1,0:T(8,128)(2,1)} collective-permute-done((bf16[80,4224]{1,0:T(8,128)(2,1)S(1)}, bf16[80,4224]{1,0:T(8,128)(2,1)}, u32[]{:S(2)}, u32[]{:S(2)}) %collective-permute-start.10) | collective-permute-done | bytes 675872 | tf_op jit(solution)/shard_map/ppermute | solution.py:423
  23.7 2.1 %collective-permute-start.11 = (bf16[80,4224]{1,0:T(8,128)(2,1)}, bf16[80,4224]{1,0:T(8,128)(2,1)}, u32[]{:S(2)}, u32[]{:S(2)}) collective-permute-start(bf16[80,4224]{1,0:T(8,128)(2,1)} %collective-permute-done.10.refs_0_), channel_id=1, source_target_pairs={{0,1},{1,0},{2,3},{3,2},{4,5},{5,4},{6,7},{7,6},{8,9},{9,8},{10,11... | collective-permute-start | bytes 2027528 | tf_op jit(solution)/shard_map/ppermute | solution.py:427
  25.8 13.0 %collective-permute-done.6.refs_0_ = bf16[80,4224]{1,0:T(8,128)(2,1)S(1)} collective-permute-done((bf16[80,4224]{1,0:T(8,128)(2,1)S(1)}, bf16[80,4224]{1,0:T(8,128)(2,1)S(1)}, u32[]{:S(2)}, u32[]{:S(2)}) %collective-permute-start.6) | collective-permute-done | bytes 675872 | tf_op jit(solution)/shard_map/ppermute | solution.py:423
  41.4 3.4 %copy-done = bf16[1,4096,1024]{2,1,0:T(8,128)(2,1)S(1)} copy-done((bf16[1,4096,1024]{2,1,0:T(8,128)(2,1)S(1)}, bf16[1,4096,1024]{2,1,0:T(8,128)(2,1)}, u32[]{:S(2)}) %copy-start) | copy-done | bytes 8388632
  44.8 3.4 %copy-done.2 = bf16[1,4096,1024]{2,1,0:T(8,128)(2,1)S(1)} copy-done((bf16[1,4096,1024]{2,1,0:T(8,128)(2,1)S(1)}, bf16[1,4096,1024]{2,1,0:T(8,128)(2,1)}, u32[]{:S(2)}) %copy-start.2) | copy-done | bytes 8388632
  48.8 7.6 %project_2.2 = (bf16[2,80,1024]{2,1,0:T(8,128)(2,1)S(1)}, bf16[2,80,1024]{2,1,0:T(8,128)(2,1)S(1)}, f32[2,80,128]{2,1,0:T(8,128)S(1)}) custom-call(bf16[80,4224]{1,0:T(8,128)(2,1)} %get-tuple-element.35.refs_0_, bf16[80,4224]{1,0:T(8,128)(2,1)} %collective-permute-done.5.refs_1_, bf16[4096,1024]{1,0:T(8,128)(2,1)S(1)} %bitcast.9, ...), custom_call_target="tpu_custom_call" | custom-call | flops 2684354560 | bytes 18874368 | tf_op jit(solution)/shard_map/project_2/pallas_call | solution.py:167
  56.5 3.6 %copy-done.3 = bf16[1,4096,1024]{2,1,0:T(8,128)(2,1)S(1)} copy-done((bf16[1,4096,1024]{2,1,0:T(8,128)(2,1)S(1)}, bf16[1,4096,1024]{2,1,0:T(8,128)(2,1)}, u32[]{:S(2)}) %copy-start.3) | copy-done | bytes 8388632
  60.0 7.3 %project_2.3 = (bf16[2,80,1024]{2,1,0:T(8,128)(2,1)S(1)}, bf16[2,80,1024]{2,1,0:T(8,128)(2,1)S(1)}, f32[2,80,128]{2,1,0:T(8,128)S(1)}) custom-call(bf16[80,4224]{1,0:T(8,128)(2,1)} %collective-permute-done.10.refs_0_, bf16[80,4224]{1,0:T(8,128)(2,1)} %collective-permute-done.11.refs_1_, bf16[4096,1024]{1,0:T(8,128)(2,1)S(1)} %bitcast.10, ...), custom_call_target="tpu_custom_call" | custom-call | flops 2684354560 | bytes 18874368 | tf_op jit(solution)/shard_map/project_2/pallas_call | solution.py:167
  67.5 10.5 %project_4.1 = (bf16[4,80,1024]{2,1,0:T(8,128)(2,1)S(1)}, bf16[4,80,1024]{2,1,0:T(8,128)(2,1)S(1)}, f32[4,80,128]{2,1,0:T(8,128)S(1)}) custom-call(bf16[80,4224]{1,0:T(8,128)(2,1)S(1)} %collective-permute-done.6.refs_0_, bf16[80,4224]{1,0:T(8,128)(2,1)} %collective-permute-done.7.refs_1_, bf16[80,4224]{1,0:T(8,128)(2,1)S(1)} %copy-done.32, ...), custom_call_target="tpu_custom_call" | custom-call | flops 5368709120 | bytes 18874368 | tf_op jit(solution)/shard_map/project_4/pallas_call | solution.py:167
  78.0 4.2 %block_state.1 = (bf16[16,80,128]{2,1,0:T(8,128)(2,1)}, f32[640,128]{1,0:T(8,128)S(1)}, f32[8,640]{1,0:T(8,128)S(1)}) custom-call(bf16[2,80,1024]{2,1,0:T(8,128)(2,1)S(1)} %get-tuple-element.36.refs_0_, bf16[4,80,1024]{2,1,0:T(8,128)(2,1)S(1)} %get-tuple-element.39.refs_1_, bf16[2,80,1024]{2,1,0:T(8,128)(2,1)S(1)} %get-tuple-element.41.refs_2_, ...), custom_call_target="tpu_custom_call" | custom-call | flops 167772160 | bytes 4194304 | tf_op jit(solution)/shard_map/block_state/pallas_call | solution.py:249
  83.8 6.8 %all-to-all-start = ((bf16[16,80,128]{2,1,0:T(8,128)(2,1)}), bf16[16,80,128]{2,1,0:T(8,128)(2,1)}, u32[]{:S(2)}, u32[]{:S(2)}) async-start(bf16[16,80,128]{2,1,0:T(8,128)(2,1)} %get-tuple-element.50), calls=%async_computation | async-start | bytes 655360 | tf_op jit(solution)/shard_map/all_to_all | solution.py:460
  94.8 2.7 %pack_queries.1 = (bf16[2,80,1024]{2,1,0:T(8,128)(2,1)S(1)}, bf16[2,80,1024]{2,1,0:T(8,128)(2,1)S(1)}, bf16[2,80,1024]{2,1,0:T(8,128)(2,1)S(1)}, bf16[2,80,1024]{2,1,0:T(8,128)(2,1)S(1)}, f32[128,128]{1,0:T(8,128)S(1)}) custom-call(s32[128,2]{1,0:T(8,128)S(1)} %bitcast.23, s32[128,2]{1,0:T(8,128)S(1)} %collective-permute-done.other_route_ref, ...), custom_call_target="tpu_custom_call" | custom-call | flops 167772160 | bytes 4194304 | tf_op jit(solution)/shard_map/pack_queries/pallas_call | solution.py:118
  99.7 2.7 %collective-permute-start.3 = (bf16[2,80,1024]{2,1,0:T(8,128)(2,1)S(1)}, bf16[2,80,1024]{2,1,0:T(8,128)(2,1)S(1)}, u32[]{:S(2)}, u32[]{:S(2)}) collective-permute-start(bf16[2,80,1024]{2,1,0:T(8,128)(2,1)S(1)} %get-tuple-element.33), channel_id=1, source_target_pairs={{0,64},{32,96},{64,0},{96,32},{1,65},{33,97},{65,1},{97,33},{2,66}... | collective-permute-start | bytes 983048 | tf_op jit(solution)/shard_map/ppermute | solution.py:423
  104.6 6.9 %all-to-all-start.1 = ((bf16[16,64,128]{2,1,0:T(8,128)(2,1)}), bf16[16,64,128]{2,1,0:T(8,128)(2,1)S(1)}, u32[]{:S(2)}, u32[]{:S(2)}) async-start(bf16[16,64,128]{2,1,0:T(8,128)(2,1)} %prefix.1), calls=%async_computation.1 | async-start | bytes 524288 | tf_op jit(solution)/shard_map/all_to_all | solution.py:461
  112.2 4.7 %collective-permute-done.3.refs_8_.refs_2_ = bf16[2,80,1024]{2,1,0:T(8,128)(2,1)S(1)} collective-permute-done((bf16[2,80,1024]{2,1,0:T(8,128)(2,1)S(1)}, bf16[2,80,1024]{2,1,0:T(8,128)(2,1)S(1)}, u32[]{:S(2)}, u32[]{:S(2)}) %collective-permute-start.3) | collective-permute-done | bytes 327712 | tf_op jit(solution)/shard_map/ppermute | solution.py:423
  129.0 6.8 %inner_reads.1.refs_4_ = f32[8,80,1024]{2,1,0:T(8,128)S(1)} custom-call(bf16[2,80,1024]{2,1,0:T(8,128)(2,1)S(1)} %copy-done.22, bf16[4,80,1024]{2,1,0:T(8,128)(2,1)S(1)} %get-tuple-element.39.refs_1_, bf16[2,80,1024]{2,1,0:T(8,128)(2,1)S(1)} %copy-done.26, bf16[2,80,1024]{2,1,0:T(8,128)(2,1)S(1)} %copy-done.24, bf16[4,80,1024]{2,1,0:T(8,128)(2,1)S(1)} %copy-done.5, ...), custom_call_target="tpu_custom_call" | custom-call | flops 1677721600 | bytes 8388608 | tf_op jit(solution)/shard_map/inner_reads/pallas_call | solution.py:328
  140.7 2.2 %read_out.1 = (bf16[2,80,1024]{2,1,0:T(8,128)(2,1)S(1)}, bf16[2,80,1024]{2,1,0:T(8,128)(2,1)S(1)}, bf16[2,80,1024]{2,1,0:T(8,128)(2,1)S(1)}, bf16[2,80,1024]{2,1,0:T(8,128)(2,1)S(1)}) custom-call(bf16[2,80,1024]{2,1,0:T(8,128)(2,1)S(1)} %copy-done.11, bf16[2,80,1024]{2,1,0:T(8,128)(2,1)S(1)} %copy-done.14, bf16[2,80,1024]{2,1,0:T(8,128)(2,1)S(1)} %copy-done.17, ...), custom_call_target="tpu_custom_call" | custom-call | flops 167772160 | bytes 6291456 | tf_op jit(solution)/shard_map/read_out/pallas_call | solution.py:369
  142.8 2.2 %collective-permute-start.12 = (bf16[2,80,1024]{2,1,0:T(8,128)(2,1)S(1)}, bf16[2,80,1024]{2,1,0:T(8,128)(2,1)S(1)}, u32[]{:S(2)}, u32[]{:S(2)}) collective-permute-start(bf16[2,80,1024]{2,1,0:T(8,128)(2,1)S(1)} %get-tuple-element.52), channel_id=1, source_target_pairs={{0,96},{32,0},{64,32},{96,64},{1,97},{33,1},{65,33},{97,65},{2,98}... | collective-permute-start | bytes 983048 | tf_op jit(solution)/shard_map/ppermute | solution.py:423
  146.7 6.1 %collective-permute-done.12.refs_1_ = bf16[2,80,1024]{2,1,0:T(8,128)(2,1)S(1)} collective-permute-done((bf16[2,80,1024]{2,1,0:T(8,128)(2,1)S(1)}, bf16[2,80,1024]{2,1,0:T(8,128)(2,1)S(1)}, u32[]{:S(2)}, u32[]{:S(2)}) %collective-permute-start.12) | collective-permute-done | bytes 327712 | tf_op jit(solution)/shard_map/ppermute | solution.py:423
  152.8 7.2 %collective-permute-start.16 = (bf16[2,80,1024]{2,1,0:T(8,128)(2,1)S(1)}, bf16[2,80,1024]{2,1,0:T(8,128)(2,1)S(1)}, u32[]{:S(2)}, u32[]{:S(2)}) collective-permute-start(bf16[2,80,1024]{2,1,0:T(8,128)(2,1)S(1)} %collective-permute-done.12.refs_1_), channel_id=1, source_target_pairs={{0,1},{1,0},{2,3},{3,2},{4,5},{5,4},{6,7},{7,6},{8,9},{9,8},{10,11... | collective-permute-start | bytes 983048 | tf_op jit(solution)/shard_map/ppermute | solution.py:427
  160.0 3.2 %collective-permute-done.14.refs_3_ = bf16[2,80,1024]{2,1,0:T(8,128)(2,1)S(1)} collective-permute-done((bf16[2,80,1024]{2,1,0:T(8,128)(2,1)S(1)}, bf16[2,80,1024]{2,1,0:T(8,128)(2,1)S(1)}, u32[]{:S(2)}, u32[]{:S(2)}) %collective-permute-start.14) | collective-permute-done | bytes 327712 | tf_op jit(solution)/shard_map/ppermute | solution.py:423
  166.6 2.0 %mix_reads.1 = bf16[128,2048]{1,0:T(8,128)(2,1)} custom-call(s32[128,2]{1,0:T(8,128)S(1)} %bitcast.24, f32[128,128]{1,0:T(8,128)S(1)} %copy-done.37, f32[1,2048]{1,0:T(1,128)S(1)} %bitcast.27, bf16[2,80,1024]{2,1,0:T(8,128)(2,1)S(1)} %get-tuple-element.51.refs_0_, bf16[2,80,1024]{2,1,0:T(8,128)(2,1)S(1)} %collective-permute-done.12.refs_1_, ...), custom_call_target="tpu_custom_call" | custom-call | flops 167772160 | bytes 4194304 | tf_op jit(solution)/shard_map/mix_reads/pallas_call | solution.py:411
  (119 shorter events, 42.4 us)
Async XLA Ops:
  0.8 91.8 %copy-start.33 = (s32[1,128,2]{2,1,0:T(8,128)}, s32[1,128,2]{2,1,0:T(8,128)S(1)}, u32[]{:S(2)}) copy-start(s32[1,128,2]{2,1,0:T(8,128)S(1)} %copy.10) | copy-start | bytes 3076
  4.2 19.5 %collective-permute-start.10 = (bf16[80,4224]{1,0:T(8,128)(2,1)S(1)}, bf16[80,4224]{1,0:T(8,128)(2,1)}, u32[]{:S(2)}, u32[]{:S(2)}) collective-permute-start(bf16[80,4224]{1,0:T(8,128)(2,1)S(1)} %get-tuple-element.40), channel_id=1, source_target_pairs={{0,64},{32,96},{64,0},{96,32},{1,65},{33,97},{65,1},{97,33},{2,66}... | collective-permute-start | bytes 2027528 | tf_op jit(solution)/shard_map/ppermute | solution.py:423
  8.7 30.1 %collective-permute-start.6 = (bf16[80,4224]{1,0:T(8,128)(2,1)S(1)}, bf16[80,4224]{1,0:T(8,128)(2,1)S(1)}, u32[]{:S(2)}, u32[]{:S(2)}) collective-permute-start(bf16[80,4224]{1,0:T(8,128)(2,1)S(1)} %get-tuple-element.37), channel_id=1, source_target_pairs={{0,32},{32,64},{64,96},{96,0},{1,33},{33,65},{65,97},{97,1},{2,34}... | collective-permute-start | bytes 2027528 | tf_op jit(solution)/shard_map/ppermute | solution.py:423
  9.4 29.9 %collective-permute-start.8 = (bf16[80,4224]{1,0:T(8,128)(2,1)S(1)}, bf16[80,4224]{1,0:T(8,128)(2,1)S(1)}, u32[]{:S(2)}, u32[]{:S(2)}) collective-permute-start(bf16[80,4224]{1,0:T(8,128)(2,1)S(1)} %get-tuple-element.38), channel_id=1, source_target_pairs={{0,96},{32,0},{64,32},{96,64},{1,97},{33,1},{65,33},{97,65},{2,98}... | collective-permute-start | bytes 2027528 | tf_op jit(solution)/shard_map/ppermute | solution.py:423
  11.3 30.0 %collective-permute-start.5 = (bf16[80,4224]{1,0:T(8,128)(2,1)}, bf16[80,4224]{1,0:T(8,128)(2,1)}, u32[]{:S(2)}, u32[]{:S(2)}) collective-permute-start(bf16[80,4224]{1,0:T(8,128)(2,1)} %get-tuple-element.35.refs_0_), channel_id=1, source_target_pairs={{0,1},{1,0},{2,3},{3,2},{4,5},{5,4},{6,7},{7,6},{8,9},{9,8},{10,11... | collective-permute-start | bytes 2027528 | tf_op jit(solution)/shard_map/ppermute | solution.py:427
  23.7 32.7 %collective-permute-start.11 = (bf16[80,4224]{1,0:T(8,128)(2,1)}, bf16[80,4224]{1,0:T(8,128)(2,1)}, u32[]{:S(2)}, u32[]{:S(2)}) collective-permute-start(bf16[80,4224]{1,0:T(8,128)(2,1)} %collective-permute-done.10.refs_0_), channel_id=1, source_target_pairs={{0,1},{1,0},{2,3},{3,2},{4,5},{5,4},{6,7},{7,6},{8,9},{9,8},{10,11... | collective-permute-start | bytes 2027528 | tf_op jit(solution)/shard_map/ppermute | solution.py:427
  38.8 28.7 %collective-permute-start.7 = (bf16[80,4224]{1,0:T(8,128)(2,1)S(1)}, bf16[80,4224]{1,0:T(8,128)(2,1)}, u32[]{:S(2)}, u32[]{:S(2)}) collective-permute-start(bf16[80,4224]{1,0:T(8,128)(2,1)S(1)} %collective-permute-done.6.refs_0_), channel_id=1, source_target_pairs={{0,1},{1,0},{2,3},{3,2},{4,5},{5,4},{6,7},{7,6},{8,9},{9,8},{10,11... | collective-permute-start | bytes 2027528 | tf_op jit(solution)/shard_map/ppermute | solution.py:427
  39.3 28.2 %collective-permute-start.9 = (bf16[80,4224]{1,0:T(8,128)(2,1)S(1)}, bf16[80,4224]{1,0:T(8,128)(2,1)}, u32[]{:S(2)}, u32[]{:S(2)}) collective-permute-start(bf16[80,4224]{1,0:T(8,128)(2,1)S(1)} %collective-permute-done.8.refs_2_), channel_id=1, source_target_pairs={{0,1},{1,0},{2,3},{3,2},{4,5},{5,4},{6,7},{7,6},{8,9},{9,8},{10,11... | collective-permute-start | bytes 2027528 | tf_op jit(solution)/shard_map/ppermute | solution.py:427
  40.0 52.5 %collective-permute-start.1 = (bf16[128,2048]{1,0:T(8,128)(2,1)}, bf16[128,2048]{1,0:T(8,128)(2,1)}, u32[]{:S(2)}, u32[]{:S(2)}) collective-permute-start(bf16[128,2048]{1,0:T(8,128)(2,1)} %bitcast.25), channel_id=1, source_target_pairs={{0,1},{1,0},{2,3},{3,2},{4,5},{5,4},{6,7},{7,6},{8,9},{9,8},{10,11... | collective-permute-start | bytes 1572872 | tf_op jit(solution)/shard_map/ppermute | solution.py:427
  83.8 34.6 %copy-start.38 = (f32[8,640]{1,0:T(8,128)}, f32[8,640]{1,0:T(8,128)S(1)}, u32[]{:S(2)}) copy-start(f32[8,640]{1,0:T(8,128)S(1)} %get-tuple-element.49.refs_11_) | copy-start | bytes 61444
  83.8 19.0 %all-to-all-start = ((bf16[16,80,128]{2,1,0:T(8,128)(2,1)}), bf16[16,80,128]{2,1,0:T(8,128)(2,1)}, u32[]{:S(2)}, u32[]{:S(2)}) async-start(bf16[16,80,128]{2,1,0:T(8,128)(2,1)} %get-tuple-element.50), calls=%async_computation | async-start | bytes 655360 | tf_op jit(solution)/shard_map/all_to_all | solution.py:460
  90.6 74.3 %copy-start.40 = (f32[2048]{0:T(1024)S(1)}, f32[2048]{0:T(1024)}, u32[]{:S(2)}) copy-start(f32[2048]{0:T(1024)} %param.17) | copy-start | bytes 24580
  90.6 1.9 %collective-permute-start = (s32[128,2]{1,0:T(8,128)S(1)}, s32[128,2]{1,0:T(8,128)S(1)}, u32[]{:S(2)}, u32[]{:S(2)}) collective-permute-start(s32[128,2]{1,0:T(8,128)S(1)} %bitcast.22), channel_id=1, source_target_pairs={{0,1},{1,0},{2,3},{3,2},{4,5},{5,4},{6,7},{7,6},{8,9},{9,8},{10,11... | collective-permute-start | bytes 3080 | tf_op jit(solution)/shard_map/ppermute | solution.py:427
  98.9 12.6 %collective-permute-start.2 = (bf16[2,80,1024]{2,1,0:T(8,128)(2,1)S(1)}, bf16[2,80,1024]{2,1,0:T(8,128)(2,1)S(1)}, u32[]{:S(2)}, u32[]{:S(2)}) collective-permute-start(bf16[2,80,1024]{2,1,0:T(8,128)(2,1)S(1)} %get-tuple-element.32), channel_id=1, source_target_pairs={{0,32},{32,64},{64,96},{96,0},{1,33},{33,65},{65,97},{97,1},{2,34}... | collective-permute-start | bytes 983048 | tf_op jit(solution)/shard_map/ppermute | solution.py:423
  99.7 17.2 %collective-permute-start.3 = (bf16[2,80,1024]{2,1,0:T(8,128)(2,1)S(1)}, bf16[2,80,1024]{2,1,0:T(8,128)(2,1)S(1)}, u32[]{:S(2)}, u32[]{:S(2)}) collective-permute-start(bf16[2,80,1024]{2,1,0:T(8,128)(2,1)S(1)} %get-tuple-element.33), channel_id=1, source_target_pairs={{0,64},{32,96},{64,0},{96,32},{1,65},{33,97},{65,1},{97,33},{2,66}... | collective-permute-start | bytes 983048 | tf_op jit(solution)/shard_map/ppermute | solution.py:423
  102.4 15.2 %collective-permute-start.4 = (bf16[2,80,1024]{2,1,0:T(8,128)(2,1)S(1)}, bf16[2,80,1024]{2,1,0:T(8,128)(2,1)S(1)}, u32[]{:S(2)}, u32[]{:S(2)}) collective-permute-start(bf16[2,80,1024]{2,1,0:T(8,128)(2,1)S(1)} %get-tuple-element.34), channel_id=1, source_target_pairs={{0,96},{32,0},{64,32},{96,64},{1,97},{33,1},{65,33},{97,65},{2,98}... | collective-permute-start | bytes 983048 | tf_op jit(solution)/shard_map/ppermute | solution.py:423
  104.6 31.2 %all-to-all-start.1 = ((bf16[16,64,128]{2,1,0:T(8,128)(2,1)}), bf16[16,64,128]{2,1,0:T(8,128)(2,1)S(1)}, u32[]{:S(2)}, u32[]{:S(2)}) async-start(bf16[16,64,128]{2,1,0:T(8,128)(2,1)} %prefix.1), calls=%async_computation.1 | async-start | bytes 524288 | tf_op jit(solution)/shard_map/all_to_all | solution.py:461
  142.8 9.9 %collective-permute-start.12 = (bf16[2,80,1024]{2,1,0:T(8,128)(2,1)S(1)}, bf16[2,80,1024]{2,1,0:T(8,128)(2,1)S(1)}, u32[]{:S(2)}, u32[]{:S(2)}) collective-permute-start(bf16[2,80,1024]{2,1,0:T(8,128)(2,1)S(1)} %get-tuple-element.52), channel_id=1, source_target_pairs={{0,96},{32,0},{64,32},{96,64},{1,97},{33,1},{65,33},{97,65},{2,98}... | collective-permute-start | bytes 983048 | tf_op jit(solution)/shard_map/ppermute | solution.py:423
  145.0 15.0 %collective-permute-start.13 = (bf16[2,80,1024]{2,1,0:T(8,128)(2,1)S(1)}, bf16[2,80,1024]{2,1,0:T(8,128)(2,1)S(1)}, u32[]{:S(2)}, u32[]{:S(2)}) collective-permute-start(bf16[2,80,1024]{2,1,0:T(8,128)(2,1)S(1)} %get-tuple-element.53), channel_id=1, source_target_pairs={{0,64},{32,96},{64,0},{96,32},{1,65},{33,97},{65,1},{97,33},{2,66}... | collective-permute-start | bytes 983048 | tf_op jit(solution)/shard_map/ppermute | solution.py:423
  145.6 17.5 %collective-permute-start.14 = (bf16[2,80,1024]{2,1,0:T(8,128)(2,1)S(1)}, bf16[2,80,1024]{2,1,0:T(8,128)(2,1)S(1)}, u32[]{:S(2)}, u32[]{:S(2)}) collective-permute-start(bf16[2,80,1024]{2,1,0:T(8,128)(2,1)S(1)} %get-tuple-element.54), channel_id=1, source_target_pairs={{0,32},{32,64},{64,96},{96,0},{1,33},{33,65},{65,97},{97,1},{2,34}... | collective-permute-start | bytes 983048 | tf_op jit(solution)/shard_map/ppermute | solution.py:423
  145.7 18.0 %collective-permute-start.15 = (bf16[2,80,1024]{2,1,0:T(8,128)(2,1)S(1)}, bf16[2,80,1024]{2,1,0:T(8,128)(2,1)S(1)}, u32[]{:S(2)}, u32[]{:S(2)}) collective-permute-start(bf16[2,80,1024]{2,1,0:T(8,128)(2,1)S(1)} %get-tuple-element.51.refs_0_), channel_id=1, source_target_pairs={{0,1},{1,0},{2,3},{3,2},{4,5},{5,4},{6,7},{7,6},{8,9},{9,8},{10,11... | collective-permute-start | bytes 983048 | tf_op jit(solution)/shard_map/ppermute | solution.py:427
  152.8 10.9 %collective-permute-start.16 = (bf16[2,80,1024]{2,1,0:T(8,128)(2,1)S(1)}, bf16[2,80,1024]{2,1,0:T(8,128)(2,1)S(1)}, u32[]{:S(2)}, u32[]{:S(2)}) collective-permute-start(bf16[2,80,1024]{2,1,0:T(8,128)(2,1)S(1)} %collective-permute-done.12.refs_1_), channel_id=1, source_target_pairs={{0,1},{1,0},{2,3},{3,2},{4,5},{5,4},{6,7},{7,6},{8,9},{9,8},{10,11... | collective-permute-start | bytes 983048 | tf_op jit(solution)/shard_map/ppermute | solution.py:427
  160.0 3.7 %collective-permute-start.17 = (bf16[2,80,1024]{2,1,0:T(8,128)(2,1)S(1)}, bf16[2,80,1024]{2,1,0:T(8,128)(2,1)S(1)}, u32[]{:S(2)}, u32[]{:S(2)}) collective-permute-start(bf16[2,80,1024]{2,1,0:T(8,128)(2,1)S(1)} %collective-permute-done.13.refs_2_), channel_id=1, source_target_pairs={{0,1},{1,0},{2,3},{3,2},{4,5},{5,4},{6,7},{7,6},{8,9},{9,8},{10,11... | collective-permute-start | bytes 983048 | tf_op jit(solution)/shard_map/ppermute | solution.py:427
  163.2 1.8 %collective-permute-start.18 = (bf16[2,80,1024]{2,1,0:T(8,128)(2,1)S(1)}, bf16[2,80,1024]{2,1,0:T(8,128)(2,1)S(1)}, u32[]{:S(2)}, u32[]{:S(2)}) collective-permute-start(bf16[2,80,1024]{2,1,0:T(8,128)(2,1)S(1)} %collective-permute-done.14.refs_3_), channel_id=1, source_target_pairs={{0,1},{1,0},{2,3},{3,2},{4,5},{5,4},{6,7},{7,6},{8,9},{9,8},{10,11... | collective-permute-start | bytes 983048 | tf_op jit(solution)/shard_map/ppermute | solution.py:427
  (41 other events, 165.0 us)

commit v2 on v1

--- a/solution.py
+++ b/solution.py
@@ -23,6 +23,7 @@
 F32 = jnp.float32
 BF16 = jnp.bfloat16
 MIB = 1 << 20
+VMEM = 60 * MIB
 
 
 def iota(shape, axis):
@@ -81,7 +82,7 @@
     return pl.pallas_call(
         pack_rows_kernel,
         out_shape=[jax.ShapeDtypeStruct((CAP, D + LIVE), BF16)] * OWNERS,
-        compiler_params=pltpu.CompilerParams(vmem_limit_bytes=24 * MIB),
+        compiler_params=pltpu.CompilerParams(vmem_limit_bytes=VMEM),
         cost_estimate=pl.CostEstimate(
             flops=2 * 320 * 128 * D, bytes_accessed=4 * MIB, transcendentals=0
         ),
@@ -119,7 +120,7 @@
         pack_queries_kernel,
         out_shape=[jax.ShapeDtypeStruct((2, CAP, HALF), BF16)] * OWNERS
         + [jax.ShapeDtypeStruct((ROWS, 128), F32)],
-        compiler_params=pltpu.CompilerParams(vmem_limit_bytes=24 * MIB),
+        compiler_params=pltpu.CompilerParams(vmem_limit_bytes=VMEM),
         cost_estimate=pl.CostEstimate(
             flops=2 * 640 * 128 * HALF, bytes_accessed=4 * MIB, transcendentals=0
         ),
@@ -185,7 +186,7 @@
             jax.ShapeDtypeStruct((count, CAP, 128), F32),
         ],
         scratch_shapes=[pltpu.VMEM((count * CAP, D), BF16)],
-        compiler_params=pltpu.CompilerParams(vmem_limit_bytes=30 * MIB),
+        compiler_params=pltpu.CompilerParams(vmem_limit_bytes=VMEM),
         cost_estimate=pl.CostEstimate(
             flops=2 * count * CAP * D * 2 * HALF, bytes_accessed=18 * MIB, transcendentals=0
         ),
@@ -265,7 +266,7 @@
             pltpu.VMEM((CHUNKS, CAP, 256), BF16),
             pltpu.VMEM((CHUNKS, CAP, 128), F32),
         ],
-        compiler_params=pltpu.CompilerParams(vmem_limit_bytes=24 * MIB),
+        compiler_params=pltpu.CompilerParams(vmem_limit_bytes=VMEM),
         cost_estimate=pl.CostEstimate(
             flops=2 * SLOTS * HALF * 128, bytes_accessed=4 * MIB, transcendentals=SLOTS * HEADS
         ),
@@ -286,6 +287,7 @@
     return pl.pallas_call(
         prefix_kernel,
         out_shape=jax.ShapeDtypeStruct((CONTEXTS, PIECE, 128), BF16),
+        compiler_params=pltpu.CompilerParams(vmem_limit_bytes=VMEM),
         cost_estimate=pl.CostEstimate(flops=1 << 20, bytes_accessed=1 << 20, transcendentals=0),
         name="prefix",
     )(message)
@@ -334,7 +336,7 @@
         out_specs=pl.BlockSpec((CHUNKS, CAP, 256), lambda n: (0, 0, n)),
         out_shape=jax.ShapeDtypeStruct((CHUNKS, CAP, HALF), F32),
         scratch_shapes=[pltpu.VMEM((CHUNKS, CAP, 256), BF16)] * 3,
-        compiler_params=pltpu.CompilerParams(vmem_limit_bytes=24 * MIB),
+        compiler_params=pltpu.CompilerParams(vmem_limit_bytes=VMEM),
         cost_estimate=pl.CostEstimate(
             flops=4 * SLOTS * SLOTS * HALF, bytes_accessed=8 * MIB, transcendentals=SLOTS * SLOTS * 4
         ),
@@ -378,7 +380,7 @@
         out_specs=[pl.BlockSpec((2, CAP, 256), lambda n: (0, 0, n))] * OWNERS,
         out_shape=[jax.ShapeDtypeStruct((2, CAP, HALF), BF16)] * OWNERS,
         scratch_shapes=[pltpu.VMEM((CHUNKS, CAP, 256), BF16)] * 2,
-        compiler_params=pltpu.CompilerParams(vmem_limit_bytes=24 * MIB),
+        compiler_params=pltpu.CompilerParams(vmem_limit_bytes=VMEM),
         cost_estimate=pl.CostEstimate(
             flops=2 * SLOTS * HALF * 128, bytes_accessed=6 * MIB, transcendentals=SLOTS * HEADS
         ),
@@ -411,12 +413,16 @@
     return pl.pallas_call(
         mix_kernel,
         out_shape=jax.ShapeDtypeStruct((ROWS, 2 * HALF), BF16),
-        compiler_params=pltpu.CompilerParams(vmem_limit_bytes=24 * MIB),
+        compiler_params=pltpu.CompilerParams(vmem_limit_bytes=VMEM),
         cost_estimate=pl.CostEstimate(
             flops=2 * ROWS * 320 * 2 * HALF, bytes_accessed=4 * MIB, transcendentals=0
         ),
         name="mix_reads",
     )(route, gates, gain, *own, *other)
+
+
+def after(array, *first):
+    return lax.optimization_barrier((array, *first))[0]
 
 
 def hop(array, shift):
@@ -445,17 +451,24 @@
     arrived = {0: packed[0]}
     for shift in (1, 3, 2):
         arrived[shift] = hop(packed[shift], shift)
+    other = {0: swap(packed[0])}
     other_route, other_query = swap(route), swap(query_rows)
-    packed_query = pack_queries(route, other_route, query_rows, other_query, rows, router_weight)
+    first = project([arrived[0], other[0]], *weights)
+    packed_query = pack_queries(
+        after(route, first[2]), other_route, query_rows, other_query, rows, router_weight
+    )
     gates = packed_query[OWNERS]
-
-    projected = []
-    for group in GROUPS:
-        parts = [swap(arrived[shift]) if partner else arrived[shift] for shift, partner in group]
-        projected.append(project(parts, *weights))
-    units, values, decays = zip(*projected)
-
-    query_in = [packed_query[0]] + [hop(packed_query[shift], shift) for shift in (1, 2, 3)]
+    for shift in (1, 3):
+        arrived[shift] = after(arrived[shift], gates)
+        other[shift] = swap(arrived[shift])
+    second = project([arrived[1], other[1], arrived[3], other[3]], *weights)
+    arrived[2] = after(arrived[2], second[2])
+    other[2] = swap(arrived[2])
+    query_in = [packed_query[0]]
+    query_in += [hop(after(packed_query[shift], arrived[2]), shift) for shift in (1, 2, 3)]
+    third = project([arrived[2], other[2]], *weights)
+    units, values, decays = zip(first, second, third)
+
     message, column, row = block_state(units, values, decays)
     slices = lax.all_to_all(message, "context", 0, 0, tiled=True)
     entry = lax.all_to_all(prefix(slices), "context", 0, 0, tiled=True)
@@ -463,8 +476,8 @@
     reads = read_out(query_in, inner, column, entry.reshape(HEADS, HEAD_DIM, HEAD_DIM))
 
     own = [reads[0]] + [hop(reads[shift], -shift) for shift in (1, 2, 3)]
-    other = [swap(part) for part in own]
-    return mix_reads(route, gates, norm_gain[None], own, other)[None]
+    paired = [swap(part) for part in own]
+    return mix_reads(route, gates, norm_gain[None], own, paired)[None]
 
 
 def solution(mesh):

time: 170 us -> 138 us (0.81)
  local copies, waits for them, and re-layouts: 39.4 us -> 12.7 us
  Pallas kernels: 47.3 us -> 65.4 us
  starting transfers between devices: 42.2 us -> 30.9 us
  waiting for transfers between devices: 39.5 us -> 28.4 us
    unnamed x91 -> x53, local copies, waits for them, and re-layouts: 39.4 us -> 12.7 us
    ppermute x9, waiting for transfers between devices: 37.8 us -> 20.5 us  [hop(): lax.ppermute(array, 'memory', [(i, (i + shift) % OWNERS) for i in range(O...]
    ppermute x10, starting transfers between devices: 14.6 us -> 7.18 us  [swap(): return lax.ppermute(array, 'dp', [(0, 1), (1, 0)])]
    pallas_call x3, Pallas kernels: 25.4 us -> 31.9 us  [project(): pl.pallas_call(functools.partial(project_kernel, count), grid=(HALF // wi...]
    all_to_all x1, waiting for transfers between devices: 0.01 us -> 3.82 us  [shards(): slices = lax.all_to_all(message, 'context', 0, 0, tiled=True)]
    all_to_all x1, starting transfers between devices: 6.89 us -> 4.05 us  [shards(): entry = lax.all_to_all(prefix(slices), 'context', 0, 0, tiled=True)]
    pallas_call x1, Pallas kernels: 2.16 us -> 4.96 us  [read_out(): pl.pallas_call(read_kernel, grid=(HEADS // 2,), in_specs=[pl.BlockSpec((2...]
    ppermute x10, waiting for transfers between devices: 1.65 us -> 4.1 us  [swap(): return lax.ppermute(array, 'dp', [(0, 1), (1, 0)])]
  transfers between devices with their start and end apart: 21 -> 21, of which waited for: 7 -> 9; matrix products, arithmetic and copies ran while one was open for 1% -> 3% of each run, Pallas kernels for 24% -> 27%
where the time goes in v2:
time: 138 us
  Pallas kernels  65.4 us (47%)
  starting transfers between devices  30.9 us (22%)
  waiting for transfers between devices  28.4 us (21%)
  local copies, waits for them, and re-layouts  12.7 us (9%)
    pallas_call x3, Pallas kernels, project(): pl.pallas_call(functools.partial(project_kernel, count), grid=(HALF // wi...  31.9 us
    ppermute x9, waiting for transfers between devices, hop(): lax.ppermute(array, 'memory', [(i, (i + shift) % OWNERS) for i in range(O...  20.5 us
    ppermute x9, starting transfers between devices, hop(): lax.ppermute(array, 'memory', [(i, (i + shift) % OWNERS) for i in range(O...  12.9 us
    unnamed x53, local copies, waits for them, and re-layouts  12.7 us
    pallas_call x1, Pallas kernels, inner_reads(): pl.pallas_call(inner_kernel, grid=(HEADS // 2,), in_specs=chunked * 2 + [...  8.55 us
    ppermute x10, starting transfers between devices, swap(): return lax.ppermute(array, 'dp', [(0, 1), (1, 0)])  7.18 us
    all_to_all x1, starting transfers between devices, shards(): slices = lax.all_to_all(message, 'context', 0, 0, tiled=True)  6.75 us
    pallas_call x1, Pallas kernels, block_state(): pl.pallas_call(state_kernel, grid=(HEADS // 2,), in_specs=chunked * 2 + [...  5.73 us
  transfers between devices with their start and end apart: 21, of which 9 were waited for; matrix products, arithmetic and copies ran while one was open for 3% of the time, Pallas kernels for 27%

profile of v2, /device:TPU:1, one launch (start us, length us, event | category | flops | bytes accessed | tf_op | source)
XLA Modules:
  0.0 137.6 jit_solution(5032385416307056048)
XLA Ops:
  1.4 4.1 %pack_rows.1 = (bf16[80,4224]{1,0:T(8,128)(2,1)}, bf16[80,4224]{1,0:T(8,128)(2,1)}, bf16[80,4224]{1,0:T(8,128)(2,1)}, bf16[80,4224]{1,0:T(8,128)(2,1)}) custom-call(s32[128,2]{1,0:T(8,128)} %bitcast.21, bf16[128,4096]{1,0:T(8,128)(2,1)} %bitcast.18), custom_call_target="tpu_custom_call" | custom-call | flops 335544320 | bytes 4194304 | tf_op jit(solution)/shard_map/pack_rows/pallas_call | solution.py:82
  7.0 3.8 %collective-permute-start.6 = (bf16[80,4224]{1,0:T(8,128)(2,1)}, bf16[80,4224]{1,0:T(8,128)(2,1)S(1)}, u32[]{:S(2)}, u32[]{:S(2)}) collective-permute-start(bf16[80,4224]{1,0:T(8,128)(2,1)} %get-tuple-element.46), channel_id=1, source_target_pairs={{0,96},{32,0},{64,32},{96,64},{1,97},{33,1},{65,33},{97,65},{2,98}... | collective-permute-start | bytes 2027528 | tf_op jit(solution)/shard_map/ppermute | solution.py:429
  11.3 2.1 %copy.12.router_ref = bf16[4096,4]{1,0:T(8,128)(2,1)} copy(bf16[4096,4]{0,1:T(4,128)(2,1)} %param.12) | data formatting | bytes 65536 | tf_op args[3]
  13.5 2.2 %copy.11 = bf16[1,4096,8]{2,1,0:T(8,128)(2,1)} copy(bf16[1,4096,8]{1,2,0:T(8,128)(2,1)} %param.15) | data formatting | bytes 131072 | tf_op args[6]
  16.5 9.9 %project_2.2 = (bf16[2,80,1024]{2,1,0:T(8,128)(2,1)}, bf16[2,80,1024]{2,1,0:T(8,128)(2,1)}, f32[2,80,128]{2,1,0:T(8,128)}) custom-call(bf16[80,4224]{1,0:T(8,128)(2,1)} %get-tuple-element.37.refs_0_, bf16[80,4224]{1,0:T(8,128)(2,1)} %copy-done.8, bf16[4096,1024]{1,0:T(8,128)(2,1)} %bitcast.9, bf16[4096,1024]{1,0:T(8,128)(2,1)} %bitcast.12, ...), custom_call_target="tpu_custom_call" | custom-call | flops 2684354560 | bytes 18874368 | tf_op jit(solution)/shard_map/project_2/pallas_call | solution.py:168
  27.8 4.6 %pack_queries.1 = (bf16[2,80,1024]{2,1,0:T(8,128)(2,1)}, bf16[2,80,1024]{2,1,0:T(8,128)(2,1)}, bf16[2,80,1024]{2,1,0:T(8,128)(2,1)}, bf16[2,80,1024]{2,1,0:T(8,128)(2,1)}, f32[128,128]{1,0:T(8,128)}) custom-call(s32[128,2]{1,0:T(8,128)} %bitcast.23, s32[128,2]{1,0:T(8,128)} %copy-done.20, bf16[128,2048]{1,0:T(8,128)(2,1)} %bitcast.26, ...), custom_call_target="tpu_custom_call" | custom-call | flops 167772160 | bytes 4194304 | tf_op jit(solution)/shard_map/pack_queries/pallas_call | solution.py:119
  36.5 12.3 %project_4.1 = (bf16[4,80,1024]{2,1,0:T(8,128)(2,1)}, bf16[4,80,1024]{2,1,0:T(8,128)(2,1)}, f32[4,80,128]{2,1,0:T(8,128)}) custom-call(bf16[80,4224]{1,0:T(8,128)(2,1)} %copy-done.6, bf16[80,4224]{1,0:T(8,128)(2,1)} %copy-done.9, bf16[80,4224]{1,0:T(8,128)(2,1)} %copy-done.5, bf16[80,4224]{1,0:T(8,128)(2,1)} %copy-done.10, bf16[4096,1024]{1,0:T(8,128)(2,1)} %bitcast.10, ...), custom_call_target="tpu_custom_call" | custom-call | flops 5368709120 | bytes 18874368 | tf_op jit(solution)/shard_map/project_4/pallas_call | solution.py:168
  48.7 2.3 %collective-permute-done.3.refs_0_ = bf16[80,4224]{1,0:T(8,128)(2,1)S(1)} collective-permute-done((bf16[80,4224]{1,0:T(8,128)(2,1)S(1)}, bf16[80,4224]{1,0:T(8,128)(2,1)S(1)}, u32[]{:S(2)}, u32[]{:S(2)}) %collective-permute-start.3) | collective-permute-done | bytes 675872 | tf_op jit(solution)/shard_map/ppermute | solution.py:429
  52.2 1.8 %collective-permute-done.11.refs_1_ = bf16[80,4224]{1,0:T(8,128)(2,1)S(1)} collective-permute-done((bf16[80,4224]{1,0:T(8,128)(2,1)S(1)}, bf16[80,4224]{1,0:T(8,128)(2,1)S(1)}, u32[]{:S(2)}, u32[]{:S(2)}) %collective-permute-start.11) | collective-permute-done | bytes 675872 | tf_op jit(solution)/shard_map/ppermute | solution.py:433
  54.8 9.8 %project_2.3 = (bf16[2,80,1024]{2,1,0:T(8,128)(2,1)}, bf16[2,80,1024]{2,1,0:T(8,128)(2,1)}, f32[2,80,128]{2,1,0:T(8,128)}) custom-call(bf16[80,4224]{1,0:T(8,128)(2,1)} %copy-done.7, bf16[80,4224]{1,0:T(8,128)(2,1)} %copy-done.11, bf16[4096,1024]{1,0:T(8,128)(2,1)} %bitcast.11, bf16[4096,1024]{1,0:T(8,128)(2,1)} %bitcast.14, bf16[4096,8]{1,0:T(8,128)(2,1)} %bitcast.17, ...), custom_call_target="tpu_custom_call" | custom-call | flops 2684354560 | bytes 18874368 | tf_op jit(solution)/shard_map/project_2/pallas_call | solution.py:168
  64.6 5.7 %block_state.1 = (bf16[16,80,128]{2,1,0:T(8,128)(2,1)}, f32[640,128]{1,0:T(8,128)}, f32[8,640]{1,0:T(8,128)}) custom-call(bf16[2,80,1024]{2,1,0:T(8,128)(2,1)} %get-tuple-element.55.refs_0_, bf16[4,80,1024]{2,1,0:T(8,128)(2,1)} %get-tuple-element.56.refs_1_, bf16[2,80,1024]{2,1,0:T(8,128)(2,1)} %get-tuple-element.57.refs_2_, ...), custom_call_target="tpu_custom_call" | custom-call | flops 167772160 | bytes 4194304 | tf_op jit(solution)/shard_map/block_state/pallas_call | solution.py:250
  70.4 6.8 %all-to-all-start = ((bf16[16,80,128]{2,1,0:T(8,128)(2,1)}), bf16[16,80,128]{2,1,0:T(8,128)(2,1)S(1)}, u32[]{:S(2)}, u32[]{:S(2)}) async-start(bf16[16,80,128]{2,1,0:T(8,128)(2,1)} %get-tuple-element.64), calls=%async_computation | async-start | bytes 655360 | tf_op jit(solution)/shard_map/all_to_all | solution.py:473
  77.6 3.6 %collective-permute-start.9 = (bf16[2,80,1024]{2,1,0:T(8,128)(2,1)S(1)}, bf16[2,80,1024]{2,1,0:T(8,128)(2,1)S(1)}, u32[]{:S(2)}, u32[]{:S(2)}) collective-permute-start(bf16[2,80,1024]{2,1,0:T(8,128)(2,1)S(1)} %copy-done.23), channel_id=1, source_target_pairs={{0,64},{32,96},{64,0},{96,32},{1,65},{33,97},{65,1},{97,33},{2,66}... | collective-permute-start | bytes 983048 | tf_op jit(solution)/shard_map/ppermute | solution.py:429
  81.2 3.8 %all-to-all-done.message = bf16[16,80,128]{2,1,0:T(8,128)(2,1)S(1)} async-done(((bf16[16,80,128]{2,1,0:T(8,128)(2,1)}), bf16[16,80,128]{2,1,0:T(8,128)(2,1)S(1)}, u32[]{:S(2)}, u32[]{:S(2)}) %all-to-all-start) | async-done | bytes 327712 | tf_op jit(solution)/shard_map/all_to_all | solution.py:473
  85.8 1.7 %prefix.1 = bf16[16,64,128]{2,1,0:T(8,128)(2,1)} custom-call(bf16[16,80,128]{2,1,0:T(8,128)(2,1)} %copy-done.3), custom_call_target="tpu_custom_call" | custom-call | flops 1048576 | bytes 1048576 | tf_op jit(solution)/shard_map/prefix/pallas_call | solution.py:287
  87.5 4.0 %all-to-all-start.1 = ((bf16[16,64,128]{2,1,0:T(8,128)(2,1)}), bf16[16,64,128]{2,1,0:T(8,128)(2,1)S(1)}, u32[]{:S(2)}, u32[]{:S(2)}) async-start(bf16[16,64,128]{2,1,0:T(8,128)(2,1)} %prefix.1), calls=%async_computation.1 | async-start | bytes 524288 | tf_op jit(solution)/shard_map/all_to_all | solution.py:474
  91.6 3.8 %collective-permute-done.9.refs_8_.refs_2_ = bf16[2,80,1024]{2,1,0:T(8,128)(2,1)S(1)} collective-permute-done((bf16[2,80,1024]{2,1,0:T(8,128)(2,1)S(1)}, bf16[2,80,1024]{2,1,0:T(8,128)(2,1)S(1)}, u32[]{:S(2)}, u32[]{:S(2)}) %collective-permute-start.9) | collective-permute-done | bytes 327712 | tf_op jit(solution)/shard_map/ppermute | solution.py:429
  96.2 8.5 %inner_reads.1.refs_4_ = f32[8,80,1024]{2,1,0:T(8,128)} custom-call(bf16[2,80,1024]{2,1,0:T(8,128)(2,1)} %get-tuple-element.55.refs_0_, bf16[4,80,1024]{2,1,0:T(8,128)(2,1)} %get-tuple-element.56.refs_1_, bf16[2,80,1024]{2,1,0:T(8,128)(2,1)} %get-tuple-element.57.refs_2_, bf16[2,80,1024]{2,1,0:T(8,128)(2,1)} %get-tuple-element.58.refs_3_, ...), custom_call_target="tpu_custom_call" | custom-call | flops 1677721600 | bytes 8388608 | tf_op jit(solution)/shard_map/inner_reads/pallas_call | solution.py:330
  105.5 5.0 %read_out.1 = (bf16[2,80,1024]{2,1,0:T(8,128)(2,1)}, bf16[2,80,1024]{2,1,0:T(8,128)(2,1)}, bf16[2,80,1024]{2,1,0:T(8,128)(2,1)}, bf16[2,80,1024]{2,1,0:T(8,128)(2,1)}) custom-call(bf16[2,80,1024]{2,1,0:T(8,128)(2,1)} %get-tuple-element.41.refs_6_.refs_0_, bf16[2,80,1024]{2,1,0:T(8,128)(2,1)} %copy-done, bf16[2,80,1024]{2,1,0:T(8,128)(2,1)} %copy-done.1, ...), custom_call_target="tpu_custom_call" | custom-call | flops 167772160 | bytes 6291456 | tf_op jit(solution)/shard_map/read_out/pallas_call | solution.py:371
  110.5 2.9 %collective-permute-start.12 = (bf16[2,80,1024]{2,1,0:T(8,128)(2,1)}, bf16[2,80,1024]{2,1,0:T(8,128)(2,1)S(1)}, u32[]{:S(2)}, u32[]{:S(2)}) collective-permute-start(bf16[2,80,1024]{2,1,0:T(8,128)(2,1)} %get-tuple-element.66), channel_id=1, source_target_pairs={{0,96},{32,0},{64,32},{96,64},{1,97},{33,1},{65,33},{97,65},{2,98}... | collective-permute-start | bytes 983048 | tf_op jit(solution)/shard_map/ppermute | solution.py:429
  115.1 12.1 %collective-permute-done.12.refs_1_ = bf16[2,80,1024]{2,1,0:T(8,128)(2,1)S(1)} collective-permute-done((bf16[2,80,1024]{2,1,0:T(8,128)(2,1)}, bf16[2,80,1024]{2,1,0:T(8,128)(2,1)S(1)}, u32[]{:S(2)}, u32[]{:S(2)}) %collective-permute-start.12) | collective-permute-done | bytes 327712 | tf_op jit(solution)/shard_map/ppermute | solution.py:429
  127.1 1.5 %collective-permute-start.16 = (bf16[2,80,1024]{2,1,0:T(8,128)(2,1)S(1)}, bf16[2,80,1024]{2,1,0:T(8,128)(2,1)S(1)}, u32[]{:S(2)}, u32[]{:S(2)}) collective-permute-start(bf16[2,80,1024]{2,1,0:T(8,128)(2,1)S(1)} %collective-permute-done.12.refs_1_), channel_id=1, source_target_pairs={{0,1},{1,0},{2,3},{3,2},{4,5},{5,4},{6,7},{7,6},{8,9},{9,8},{10,11... | collective-permute-start | bytes 983048 | tf_op jit(solution)/shard_map/ppermute | solution.py:433
  128.7 2.4 %collective-permute-done.14.refs_3_ = bf16[2,80,1024]{2,1,0:T(8,128)(2,1)S(1)} collective-permute-done((bf16[2,80,1024]{2,1,0:T(8,128)(2,1)}, bf16[2,80,1024]{2,1,0:T(8,128)(2,1)S(1)}, u32[]{:S(2)}, u32[]{:S(2)}) %collective-permute-start.14) | collective-permute-done | bytes 327712 | tf_op jit(solution)/shard_map/ppermute | solution.py:429
  133.9 3.7 %mix_reads.1 = bf16[128,2048]{1,0:T(8,128)(2,1)} custom-call(s32[128,2]{1,0:T(8,128)} %bitcast.24, f32[128,128]{1,0:T(8,128)} %get-tuple-element.40.gates_ref, f32[1,2048]{1,0:T(1,128)} %bitcast.27, bf16[2,80,1024]{2,1,0:T(8,128)(2,1)} %get-tuple-element.65.refs_0_, bf16[2,80,1024]{2,1,0:T(8,128)(2,1)} %copy-done.13, bf16[2,80,1024]{2,1,0:T(8,128)(2,1)} %copy-done.14, ...), custom_call_target="tpu_custom_call" | custom-call | flops 167772160 | bytes 4194304 | tf_op jit(solution)/shard_map/mix_reads/pallas_call | solution.py:413
  (81 shorter events, 19.1 us)
Async XLA Ops:
  5.6 10.1 %collective-permute-start = (bf16[80,4224]{1,0:T(8,128)(2,1)}, bf16[80,4224]{1,0:T(8,128)(2,1)S(1)}, u32[]{:S(2)}, u32[]{:S(2)}) collective-permute-start(bf16[80,4224]{1,0:T(8,128)(2,1)} %get-tuple-element.37.refs_0_), channel_id=1, source_target_pairs={{0,1},{1,0},{2,3},{3,2},{4,5},{5,4},{6,7},{7,6},{8,9},{9,8},{10,11... | collective-permute-start | bytes 2027528 | tf_op jit(solution)/shard_map/ppermute | solution.py:433
  7.0 25.4 %collective-permute-start.6 = (bf16[80,4224]{1,0:T(8,128)(2,1)}, bf16[80,4224]{1,0:T(8,128)(2,1)S(1)}, u32[]{:S(2)}, u32[]{:S(2)}) collective-permute-start(bf16[80,4224]{1,0:T(8,128)(2,1)} %get-tuple-element.46), channel_id=1, source_target_pairs={{0,96},{32,0},{64,32},{96,64},{1,97},{33,1},{65,33},{97,65},{2,98}... | collective-permute-start | bytes 2027528 | tf_op jit(solution)/shard_map/ppermute | solution.py:429
  10.8 21.6 %collective-permute-start.4 = (bf16[80,4224]{1,0:T(8,128)(2,1)}, bf16[80,4224]{1,0:T(8,128)(2,1)S(1)}, u32[]{:S(2)}, u32[]{:S(2)}) collective-permute-start(bf16[80,4224]{1,0:T(8,128)(2,1)} %get-tuple-element.44), channel_id=1, source_target_pairs={{0,32},{32,64},{64,96},{96,0},{1,33},{33,65},{65,97},{97,1},{2,34}... | collective-permute-start | bytes 2027528 | tf_op jit(solution)/shard_map/ppermute | solution.py:429
  10.8 15.6 %collective-permute-start.2 = (bf16[128,2048]{1,0:T(8,128)(2,1)}, bf16[128,2048]{1,0:T(8,128)(2,1)S(1)}, u32[]{:S(2)}, u32[]{:S(2)}) collective-permute-start(bf16[128,2048]{1,0:T(8,128)(2,1)} %bitcast.25), channel_id=1, source_target_pairs={{0,1},{1,0},{2,3},{3,2},{4,5},{5,4},{6,7},{7,6},{8,9},{9,8},{10,11... | collective-permute-start | bytes 1572872 | tf_op jit(solution)/shard_map/ppermute | solution.py:433
  11.1 15.3 %collective-permute-start.1 = (s32[128,2]{1,0:T(8,128)}, s32[128,2]{1,0:T(8,128)S(1)}, u32[]{:S(2)}, u32[]{:S(2)}) collective-permute-start(s32[128,2]{1,0:T(8,128)} %bitcast.22), channel_id=1, source_target_pairs={{0,1},{1,0},{2,3},{3,2},{4,5},{5,4},{6,7},{7,6},{8,9},{9,8},{10,11... | collective-permute-start | bytes 3080 | tf_op jit(solution)/shard_map/ppermute | solution.py:433
  32.5 2.2 %collective-permute-start.5 = (bf16[80,4224]{1,0:T(8,128)(2,1)S(1)}, bf16[80,4224]{1,0:T(8,128)(2,1)S(1)}, u32[]{:S(2)}, u32[]{:S(2)}) collective-permute-start(bf16[80,4224]{1,0:T(8,128)(2,1)S(1)} %collective-permute-done.4.refs_0_), channel_id=1, source_target_pairs={{0,1},{1,0},{2,3},{3,2},{4,5},{5,4},{6,7},{7,6},{8,9},{9,8},{10,11... | collective-permute-start | bytes 2027528 | tf_op jit(solution)/shard_map/ppermute | solution.py:433
  32.8 2.8 %collective-permute-start.7 = (bf16[80,4224]{1,0:T(8,128)(2,1)S(1)}, bf16[80,4224]{1,0:T(8,128)(2,1)S(1)}, u32[]{:S(2)}, u32[]{:S(2)}) collective-permute-start(bf16[80,4224]{1,0:T(8,128)(2,1)S(1)} %collective-permute-done.6.refs_2_), channel_id=1, source_target_pairs={{0,1},{1,0},{2,3},{3,2},{4,5},{5,4},{6,7},{7,6},{8,9},{9,8},{10,11... | collective-permute-start | bytes 2027528 | tf_op jit(solution)/shard_map/ppermute | solution.py:433
  33.0 18.0 %collective-permute-start.3 = (bf16[80,4224]{1,0:T(8,128)(2,1)S(1)}, bf16[80,4224]{1,0:T(8,128)(2,1)S(1)}, u32[]{:S(2)}, u32[]{:S(2)}) collective-permute-start(bf16[80,4224]{1,0:T(8,128)(2,1)S(1)} %copy-done.21), channel_id=1, source_target_pairs={{0,64},{32,96},{64,0},{96,32},{1,65},{33,97},{65,1},{97,33},{2,66}... | collective-permute-start | bytes 2027528 | tf_op jit(solution)/shard_map/ppermute | solution.py:429
  51.0 26.1 %copy-start.24 = (bf16[2,80,1024]{2,1,0:T(8,128)(2,1)S(1)}, bf16[2,80,1024]{2,1,0:T(8,128)(2,1)}, u32[]{:S(2)}) copy-start(bf16[2,80,1024]{2,1,0:T(8,128)(2,1)} %get-tuple-element.50) | copy-start | bytes 983044
  51.0 26.6 %copy-start.23 = (bf16[2,80,1024]{2,1,0:T(8,128)(2,1)S(1)}, bf16[2,80,1024]{2,1,0:T(8,128)(2,1)}, u32[]{:S(2)}) copy-start(bf16[2,80,1024]{2,1,0:T(8,128)(2,1)} %get-tuple-element.52) | copy-start | bytes 983044
  51.0 30.2 %copy-start.22 = (bf16[2,80,1024]{2,1,0:T(8,128)(2,1)S(1)}, bf16[2,80,1024]{2,1,0:T(8,128)(2,1)}, u32[]{:S(2)}) copy-start(bf16[2,80,1024]{2,1,0:T(8,128)(2,1)} %get-tuple-element.54) | copy-start | bytes 983044
  51.0 2.9 %collective-permute-start.11 = (bf16[80,4224]{1,0:T(8,128)(2,1)S(1)}, bf16[80,4224]{1,0:T(8,128)(2,1)S(1)}, u32[]{:S(2)}, u32[]{:S(2)}) collective-permute-start(bf16[80,4224]{1,0:T(8,128)(2,1)S(1)} %collective-permute-done.3.refs_0_), channel_id=1, source_target_pairs={{0,1},{1,0},{2,3},{3,2},{4,5},{5,4},{6,7},{7,6},{8,9},{9,8},{10,11... | collective-permute-start | bytes 2027528 | tf_op jit(solution)/shard_map/ppermute | solution.py:433
  70.4 14.7 %all-to-all-start = ((bf16[16,80,128]{2,1,0:T(8,128)(2,1)}), bf16[16,80,128]{2,1,0:T(8,128)(2,1)S(1)}, u32[]{:S(2)}, u32[]{:S(2)}) async-start(bf16[16,80,128]{2,1,0:T(8,128)(2,1)} %get-tuple-element.64), calls=%async_computation | async-start | bytes 655360 | tf_op jit(solution)/shard_map/all_to_all | solution.py:473
  77.1 14.4 %collective-permute-start.8 = (bf16[2,80,1024]{2,1,0:T(8,128)(2,1)S(1)}, bf16[2,80,1024]{2,1,0:T(8,128)(2,1)S(1)}, u32[]{:S(2)}, u32[]{:S(2)}) collective-permute-start(bf16[2,80,1024]{2,1,0:T(8,128)(2,1)S(1)} %copy-done.24), channel_id=1, source_target_pairs={{0,32},{32,64},{64,96},{96,0},{1,33},{33,65},{65,97},{97,1},{2,34}... | collective-permute-start | bytes 983048 | tf_op jit(solution)/shard_map/ppermute | solution.py:429
  77.6 17.7 %collective-permute-start.9 = (bf16[2,80,1024]{2,1,0:T(8,128)(2,1)S(1)}, bf16[2,80,1024]{2,1,0:T(8,128)(2,1)S(1)}, u32[]{:S(2)}, u32[]{:S(2)}) collective-permute-start(bf16[2,80,1024]{2,1,0:T(8,128)(2,1)S(1)} %copy-done.23), channel_id=1, source_target_pairs={{0,64},{32,96},{64,0},{96,32},{1,65},{33,97},{65,1},{97,33},{2,66}... | collective-permute-start | bytes 983048 | tf_op jit(solution)/shard_map/ppermute | solution.py:429
  81.2 14.2 %collective-permute-start.10 = (bf16[2,80,1024]{2,1,0:T(8,128)(2,1)S(1)}, bf16[2,80,1024]{2,1,0:T(8,128)(2,1)S(1)}, u32[]{:S(2)}, u32[]{:S(2)}) collective-permute-start(bf16[2,80,1024]{2,1,0:T(8,128)(2,1)S(1)} %copy-done.22), channel_id=1, source_target_pairs={{0,96},{32,0},{64,32},{96,64},{1,97},{33,1},{65,33},{97,65},{2,98}... | collective-permute-start | bytes 983048 | tf_op jit(solution)/shard_map/ppermute | solution.py:429
  87.5 17.3 %all-to-all-start.1 = ((bf16[16,64,128]{2,1,0:T(8,128)(2,1)}), bf16[16,64,128]{2,1,0:T(8,128)(2,1)S(1)}, u32[]{:S(2)}, u32[]{:S(2)}) async-start(bf16[16,64,128]{2,1,0:T(8,128)(2,1)} %prefix.1), calls=%async_computation.1 | async-start | bytes 524288 | tf_op jit(solution)/shard_map/all_to_all | solution.py:474
  110.5 16.6 %collective-permute-start.12 = (bf16[2,80,1024]{2,1,0:T(8,128)(2,1)}, bf16[2,80,1024]{2,1,0:T(8,128)(2,1)S(1)}, u32[]{:S(2)}, u32[]{:S(2)}) collective-permute-start(bf16[2,80,1024]{2,1,0:T(8,128)(2,1)} %get-tuple-element.66), channel_id=1, source_target_pairs={{0,96},{32,0},{64,32},{96,64},{1,97},{33,1},{65,33},{97,65},{2,98}... | collective-permute-start | bytes 983048 | tf_op jit(solution)/shard_map/ppermute | solution.py:429
  113.3 15.3 %collective-permute-start.13 = (bf16[2,80,1024]{2,1,0:T(8,128)(2,1)}, bf16[2,80,1024]{2,1,0:T(8,128)(2,1)S(1)}, u32[]{:S(2)}, u32[]{:S(2)}) collective-permute-start(bf16[2,80,1024]{2,1,0:T(8,128)(2,1)} %get-tuple-element.67), channel_id=1, source_target_pairs={{0,64},{32,96},{64,0},{96,32},{1,65},{33,97},{65,1},{97,33},{2,66}... | collective-permute-start | bytes 983048 | tf_op jit(solution)/shard_map/ppermute | solution.py:429
  113.3 17.7 %collective-permute-start.14 = (bf16[2,80,1024]{2,1,0:T(8,128)(2,1)}, bf16[2,80,1024]{2,1,0:T(8,128)(2,1)S(1)}, u32[]{:S(2)}, u32[]{:S(2)}) collective-permute-start(bf16[2,80,1024]{2,1,0:T(8,128)(2,1)} %get-tuple-element.68), channel_id=1, source_target_pairs={{0,32},{32,64},{64,96},{96,0},{1,33},{33,65},{65,97},{97,1},{2,34}... | collective-permute-start | bytes 983048 | tf_op jit(solution)/shard_map/ppermute | solution.py:429
  114.0 17.9 %collective-permute-start.15 = (bf16[2,80,1024]{2,1,0:T(8,128)(2,1)}, bf16[2,80,1024]{2,1,0:T(8,128)(2,1)S(1)}, u32[]{:S(2)}, u32[]{:S(2)}) collective-permute-start(bf16[2,80,1024]{2,1,0:T(8,128)(2,1)} %get-tuple-element.65.refs_0_), channel_id=1, source_target_pairs={{0,1},{1,0},{2,3},{3,2},{4,5},{5,4},{6,7},{7,6},{8,9},{9,8},{10,11... | collective-permute-start | bytes 983048 | tf_op jit(solution)/shard_map/ppermute | solution.py:433
  127.1 4.8 %collective-permute-start.16 = (bf16[2,80,1024]{2,1,0:T(8,128)(2,1)S(1)}, bf16[2,80,1024]{2,1,0:T(8,128)(2,1)S(1)}, u32[]{:S(2)}, u32[]{:S(2)}) collective-permute-start(bf16[2,80,1024]{2,1,0:T(8,128)(2,1)S(1)} %collective-permute-done.12.refs_1_), channel_id=1, source_target_pairs={{0,1},{1,0},{2,3},{3,2},{4,5},{5,4},{6,7},{7,6},{8,9},{9,8},{10,11... | collective-permute-start | bytes 983048 | tf_op jit(solution)/shard_map/ppermute | solution.py:433
  128.6 3.3 %collective-permute-start.17 = (bf16[2,80,1024]{2,1,0:T(8,128)(2,1)S(1)}, bf16[2,80,1024]{2,1,0:T(8,128)(2,1)S(1)}, u32[]{:S(2)}, u32[]{:S(2)}) collective-permute-start(bf16[2,80,1024]{2,1,0:T(8,128)(2,1)S(1)} %collective-permute-done.13.refs_2_), channel_id=1, source_target_pairs={{0,1},{1,0},{2,3},{3,2},{4,5},{5,4},{6,7},{7,6},{8,9},{9,8},{10,11... | collective-permute-start | bytes 983048 | tf_op jit(solution)/shard_map/ppermute | solution.py:433
  131.1 2.1 %collective-permute-start.18 = (bf16[2,80,1024]{2,1,0:T(8,128)(2,1)S(1)}, bf16[2,80,1024]{2,1,0:T(8,128)(2,1)S(1)}, u32[]{:S(2)}, u32[]{:S(2)}) collective-permute-start(bf16[2,80,1024]{2,1,0:T(8,128)(2,1)S(1)} %collective-permute-done.14.refs_3_), channel_id=1, source_target_pairs={{0,1},{1,0},{2,3},{3,2},{4,5},{5,4},{6,7},{7,6},{8,9},{9,8},{10,11... | collective-permute-start | bytes 983048 | tf_op jit(solution)/shard_map/ppermute | solution.py:433
  (22 other events, 54.9 us)

commit v3 on v2

v3 whole, which is shorter than its diff:
```python
import functools

import jax
import jax.numpy as jnp
from jax import lax
from jax.experimental import pallas as pl
from jax.experimental.pallas import tpu as pltpu
from jax.sharding import PartitionSpec as P

D = 4096
HEAD_DIM = 128
CAP = 80
ROWS = 128
OWNERS = 4
CHUNKS = 8
SLOTS = CHUNKS * CAP
HALF = 1024
HEADS = HALF // HEAD_DIM
CONTEXTS = 16
LIVE = 128
PIECE = HALF // CONTEXTS
TAIL = 16
F32 = jnp.float32
BF16 = jnp.bfloat16
MIB = 1 << 20


def iota(shape, axis):
    return lax.broadcasted_iota(jnp.int32, shape, axis)


def dot(a, b):
    return jnp.dot(a, b, preferred_element_type=F32)


def dot_rows(a, b):
    return lax.dot_general(a, b, (((1,), (1,)), ((), ())), preferred_element_type=F32)


def dot_columns(a, b):
    return lax.dot_general(a, b, (((0,), (0,)), ((), ())), preferred_element_type=F32)


def source(owner, shift):
    return (owner + OWNERS - shift) & (OWNERS - 1)


def position(shift, partner, owner, core):
    return (core ^ partner) * OWNERS + source(owner, shift)


def membership(route):
    memory = iota((8, ROWS), 0)
    named = ((route[0:1] == memory) | (route[1:2] == memory)).astype(F32)
    before = (iota((ROWS, ROWS), 0) < iota((ROWS, ROWS), 1)).astype(F32).astype(BF16)
    slot = dot(named.astype(BF16), before)
    return named, jnp.where(named > 0.0, slot, -1.0)


def one_hot(place, memory, slots=CAP):
    mine = jnp.sum(jnp.where(iota(place.shape, 0) == memory, place, 0.0), axis=0, keepdims=True)
    return (iota((slots, ROWS), 0).astype(F32) == mine).astype(F32)


def kernel_call(kernel, name, out_shape, scratch, limit, cost, *operands, hbm=()):
    spaces = [pltpu.HBM if at in hbm else pltpu.VMEM for at in range(len(operands))]
    return pl.pallas_call(
        kernel,
        out_shape=out_shape,
        in_specs=[pl.BlockSpec(memory_space=space) for space in spaces],
        out_specs=jax.tree.map(lambda _: pl.BlockSpec(memory_space=pltpu.VMEM), out_shape),
        scratch_shapes=scratch,
        compiler_params=pltpu.CompilerParams(vmem_limit_bytes=limit * MIB),
        cost_estimate=pl.CostEstimate(
            flops=cost[0], bytes_accessed=cost[1], transcendentals=0
        ),
        name=name,
    )(*operands)


def pack_rows_kernel(route_ref, rows_ref, *out_refs):
    owner = lax.axis_index("memory")
    place = membership(route_ref[...])[1]
    pick = jnp.concatenate(
        [one_hot(place, (owner + shift) & (OWNERS - 1)) for shift in range(OWNERS)], axis=0
    ).astype(BF16)
    width = 512
    for column in range(0, D, width):
        part = dot(pick, rows_ref[:, column : column + width]).astype(BF16)
        for shift in range(OWNERS):
            out_refs[shift][:, column : column + width] = part[shift * CAP : (shift + 1) * CAP]
    live = dot(pick, jnp.ones((ROWS, LIVE), BF16)).astype(BF16)
    for shift in range(OWNERS):
        out_refs[shift][:, D:] = live[shift * CAP : (shift + 1) * CAP]


def pack_rows(route, rows):
    out = [jax.ShapeDtypeStruct((CAP, D + LIVE), BF16)] * OWNERS
    cost = (2 * 320 * 128 * D, 4 * MIB)
    return kernel_call(pack_rows_kernel, "pack_rows", out, (), 12, cost, route, rows)


def pack_queries_kernel(
    route_ref, other_route_ref, query_ref, other_query_ref, rows_ref, router_ref, *out_refs
):
    owner, core = lax.axis_index("memory"), lax.axis_index("dp")
    gates_ref = out_refs[OWNERS]
    mine = pl.multiple_of(core * HALF, HALF)
    for side, (routes, queries) in enumerate(
        ((route_ref, query_ref), (other_route_ref, other_query_ref))
    ):
        named, place = membership(routes[...])
        pick = jnp.concatenate(
            [one_hot(place, (owner + shift) & (OWNERS - 1)) for shift in range(OWNERS)], axis=0
        ).astype(BF16)
        part = dot(pick, queries[:, pl.ds(mine, HALF)]).astype(BF16)
        for shift in range(OWNERS):
            out_refs[shift][core ^ side] = part[shift * CAP : (shift + 1) * CAP]
        if side == 0:
            score = dot_rows(router_ref[...], rows_ref[...])
            chosen = jax.nn.sigmoid(score) * named[:OWNERS]
            gates = chosen / jnp.sum(chosen, axis=0, keepdims=True)
            gates_ref[...] = jnp.concatenate(
                [gates, jnp.zeros((128 - OWNERS, ROWS), F32)], axis=0
            ).T


def pack_queries(route, other_route, queries, other_queries, rows, router_weight):
    out = [jax.ShapeDtypeStruct((2, CAP, HALF), BF16)] * OWNERS
    out = out + [jax.ShapeDtypeStruct((ROWS, 128), F32)]
    cost = (2 * 640 * 128 * HALF, 4 * MIB)
    operands = (route, other_route, queries, other_queries, rows, router_weight)
    return kernel_call(pack_queries_kernel, "pack_queries", out, (), 12, cost, *operands)


def log_sigmoid(x):
    small = jnp.exp(-jnp.abs(x))
    near = 1.0 + small
    tiny = near == 1.0
    log1p = jnp.where(tiny, small, jnp.log(near) * (small / jnp.where(tiny, 1.0, near - 1.0)))
    return jnp.minimum(x, 0.0) - log1p


WIDTH = 512


def project_parts(row_refs, decay_ref, bias_ref, outs, key_ref, value_ref, held, ready):
    count = len(row_refs)
    unit_out, value_out, decay_out = outs
    for at in range(count):
        held[at * CAP : (at + 1) * CAP] = row_refs[at][:, :D]
    decay = log_sigmoid(dot_rows(held[...], decay_ref[...]) + bias_ref[...])
    decay_out[...] = jnp.zeros_like(decay_out)
    for at in range(count):
        live = row_refs[at][:, D : D + HEADS].astype(F32)
        decay_out[at, :, :HEADS] = decay[at * CAP : (at + 1) * CAP] * live
    for start in range(0, HALF, WIDTH):
        ready(start // WIDTH)
        columns = slice(start, start + WIDTH)
        keys = dot(held[...], key_ref[:, columns]).astype(BF16).astype(F32)
        for head in range(0, WIDTH, HEAD_DIM):
            key = keys[:, head : head + HEAD_DIM]
            unit = key * lax.rsqrt(jnp.sum(key * key, axis=1, keepdims=True) + 1e-06)
            unit_out[:, :, start + head : start + head + HEAD_DIM] = unit.astype(BF16).reshape(
                count, CAP, HEAD_DIM
            )
        values = dot(held[...], value_ref[:, columns]).astype(BF16)
        value_out[:, :, columns] = values.reshape(count, CAP, WIDTH)


def project_first_kernel(count, *refs):
    key_hbm, value_hbm, decay_ref, bias_ref = refs[count : count + 4]
    outs, (key_ref, value_ref, held, sems) = refs[count + 4 : count + 7], refs[count + 7 :]
    copies = []
    for at, start in enumerate(range(0, HALF, WIDTH)):
        columns = slice(start, start + WIDTH)
        for side, (far, near) in enumerate(((key_hbm, key_ref), (value_hbm, value_ref))):
            copies.append(
                pltpu.make_async_copy(far.at[:, columns], near.at[:, columns], sems.at[side, at])
            )
    for copy in copies:
        copy.start()

    def ready(at):
        copies[2 * at].wait()
        copies[2 * at + 1].wait()

    project_parts(refs[:count], decay_ref, bias_ref, outs, key_ref, value_ref, held, ready)


def project_next_kernel(count, *refs):
    key_ref, value_ref, decay_ref, bias_ref = refs[count : count + 4]
    outs, held = refs[count + 4 : count + 7], refs[count + 7]
    project_parts(
        refs[:count], decay_ref, bias_ref, outs, key_ref, value_ref, held, lambda at: None
    )


def project(row_parts, key_weight, value_weight, decay_weight, decay_bias, first=False):
    count = len(row_parts)
    out = [jax.ShapeDtypeStruct((count, CAP, HALF), BF16)] * 2
    out = out + [jax.ShapeDtypeStruct((count, CAP, 128), F32)]
    scratch = [pltpu.VMEM((count * CAP, D), BF16)]
    cost = (2 * count * CAP * D * 2 * HALF, 18 * MIB)
    kernel = project_first_kernel if first else project_next_kernel
    if first:
        out = out + [pltpu.VMEM((D, HALF), BF16)] * 2
        scratch = scratch + [pltpu.SemaphoreType.DMA((2, HALF // WIDTH))]
    return kernel_call(
        functools.partial(kernel, count),
        f"project_{count}",
        out,
        scratch,
        40 if first else 12,
        cost,
        *row_parts,
        key_weight,
        value_weight,
        decay_weight,
        decay_bias,
        hbm=(count, count + 1) if first else (),
    )


GROUPS = (((0, 0), (0, 1)), ((1, 0), (1, 1), (3, 0), (3, 1)), ((2, 0), (2, 1)))


def token_order(refs, held):
    owner, core = lax.axis_index("memory"), lax.axis_index("dp")
    for group, ref in zip(GROUPS, refs):
        for at, (shift, partner) in enumerate(group):
            held[position(shift, partner, owner, core)] = ref[at]


def head_columns(head):
    return slice(head * HEAD_DIM, (head + 1) * HEAD_DIM)


def state_kernel(*refs):
    unit_refs, value_refs, decay_refs = refs[0:3], refs[3:6], refs[6:9]
    message, column_out, row_out, units, values, decays = refs[9:]
    token_order(decay_refs, decays)
    total = decays[...].reshape(SLOTS, 128).T[:HEADS]
    lane = iota((HEADS, SLOTS), 1)
    reach = 1
    while reach < SLOTS:
        total = total + jnp.where(lane >= reach, pltpu.roll(total, reach, 1), 0.0)
        reach *= 2
    row_out[...] = total
    running = jnp.concatenate([total, jnp.zeros((128 - HEADS, SLOTS), F32)], axis=0).T
    column_out[...] = running
    token_order(unit_refs, units)
    token_order(value_refs, values)
    last = running[SLOTS - 1 : SLOTS]
    fade = jnp.exp(last - running)
    for head in range(HEADS):
        unit = units[:, :, head_columns(head)].reshape(SLOTS, HEAD_DIM).astype(F32)
        faded = (unit * fade[:, head : head + 1]).astype(BF16)
        value = values[:, :, head_columns(head)].reshape(SLOTS, HEAD_DIM)
        state = dot_columns(faded, value).astype(BF16)
        ended = jnp.broadcast_to(last[:, head : head + 1], (TAIL, 128))
        high = ended.astype(BF16).astype(F32)
        tail = jnp.where(iota((TAIL, 128), 0) < TAIL // 2, high, ended - high).astype(BF16)
        for part in range(2):
            message[head * 2 + part, :PIECE] = state[part * PIECE : (part + 1) * PIECE]
            message[head * 2 + part, PIECE:] = tail


def block_state(units, values, decays):
    out = [
        jax.ShapeDtypeStruct((CONTEXTS, PIECE + TAIL, 128), BF16),
        jax.ShapeDtypeStruct((SLOTS, 128), F32),
        jax.ShapeDtypeStruct((HEADS, SLOTS), F32),
    ]
    scratch = [
        pltpu.VMEM((CHUNKS, CAP, HALF), BF16),
        pltpu.VMEM((CHUNKS, CAP, HALF), BF16),
        pltpu.VMEM((CHUNKS, CAP, 128), F32),
    ]
    cost = (2 * SLOTS * HALF * 128, 4 * MIB)
    return kernel_call(
        state_kernel, "block_state", out, scratch, 12, cost, *units, *values, *decays
    )


def prefix_kernel(message, entry):
    before = jnp.zeros((PIECE, 128), F32)
    for context in range(CONTEXTS):
        entry[context] = before.astype(BF16)
        high = message[context, PIECE : PIECE + 1].astype(F32)
        low = message[context, PIECE + TAIL // 2 : PIECE + TAIL // 2 + 1].astype(F32)
        before = jnp.exp(high + low) * before + message[context, :PIECE].astype(F32)


def prefix(message):
    out = jax.ShapeDtypeStruct((CONTEXTS, PIECE, 128), BF16)
    return kernel_call(prefix_kernel, "prefix", out, (), 4, (MIB, MIB), message)


def order_queries(query_refs, held):
    owner = lax.axis_index("memory")
    for shift in range(OWNERS):
        for core in range(2):
            held[core * OWNERS + source(owner, shift)] = query_refs[shift][core]


def inner_kernel(*refs):
    unit_refs, value_refs, query_refs = refs[0:3], refs[3:6], refs[6:10]
    column_ref, row_ref, inner, units, values, queries = refs[10:]
    token_order(unit_refs, units)
    token_order(value_refs, values)
    order_queries(query_refs, queries)
    tile = 2 * CAP
    for head in range(HEADS):
        columns = head_columns(head)
        running = column_ref[:, head : head + 1]
        running_row = row_ref[head : head + 1]
        unit = units[:, :, columns].reshape(SLOTS, HEAD_DIM)
        value = values[:, :, columns].reshape(SLOTS, HEAD_DIM)
        for block in range(SLOTS // tile):
            reach = -(-((block + 1) * tile) // 128) * 128
            query = queries[2 * block : 2 * block + 2, :, columns].reshape(tile, HEAD_DIM)
            score = dot_rows(query, unit[:reach])
            spread = running[block * tile : (block + 1) * tile] - running_row[:, :reach]
            causal = iota((tile, reach), 0) + block * tile >= iota((tile, reach), 1)
            score = (score * jnp.exp(jnp.where(causal, spread, -1e30))).astype(BF16)
            result = dot(score, value[:reach])
            inner[2 * block : 2 * block + 2, :, columns] = result.reshape(2, CAP, HEAD_DIM)


def inner_reads(units, values, queries, column, row):
    out = jax.ShapeDtypeStruct((CHUNKS, CAP, HALF), F32)
    scratch = [pltpu.VMEM((CHUNKS, CAP, HALF), BF16)] * 3
    cost = (4 * SLOTS * SLOTS * HALF, 8 * MIB)
    operands = (*units, *values, *queries, column, row)
    return kernel_call(inner_kernel, "inner_reads", out, scratch, 16, cost, *operands)


def read_kernel(*refs):
    query_refs = refs[0:4]
    inner, column_ref, entry = refs[4:7]
    out_refs = refs[7:11]
    queries, reads = refs[11:]
    owner = lax.axis_index("memory")
    order_queries(query_refs, queries)
    fade = jnp.exp(column_ref[...])
    for head in range(HEADS):
        columns = head_columns(head)
        carried = dot(queries[:, :, columns].reshape(SLOTS, HEAD_DIM), entry[head])
        result = inner[:, :, columns].reshape(SLOTS, HEAD_DIM) + fade[:, head : head + 1] * carried
        reads[:, :, columns] = result.astype(BF16).reshape(CHUNKS, CAP, HEAD_DIM)
    for shift in range(OWNERS):
        for core in range(2):
            out_refs[shift][core] = reads[core * OWNERS + source(owner, shift)]


def read_out(queries, inner, column, entry):
    out = [jax.ShapeDtypeStruct((2, CAP, HALF), BF16)] * OWNERS
    scratch = [pltpu.VMEM((CHUNKS, CAP, HALF), BF16)] * 2
    cost = (2 * SLOTS * HALF * 128, 6 * MIB)
    return kernel_call(
        read_kernel, "read_out", out, scratch, 12, cost, *queries, inner, column, entry
    )


def mix_kernel(route_ref, gates_ref, gain_ref, *refs):
    own_refs, other_refs, out_ref = refs[0:4], refs[4:8], refs[8]
    owner, core = lax.axis_index("memory"), lax.axis_index("dp")
    place = membership(route_ref[...])[1]
    picks, gates = [], []
    lane = iota((ROWS, 128), 1)
    for shift in range(OWNERS):
        memory = (owner + shift) & (OWNERS - 1)
        picks.append(one_hot(place, memory, 128).T.astype(BF16)[:, :CAP])
        gate = jnp.where(lane == memory, gates_ref[...], 0.0)
        gates.append(jnp.sum(gate, axis=1, keepdims=True))
    for side, reads in enumerate((own_refs, other_refs)):
        start = (core ^ side) * HALF
        mixture = jnp.zeros((ROWS, HALF), F32)
        for shift in range(OWNERS):
            mixture = mixture + gates[shift] * dot(picks[shift], reads[shift][core])
        for head in range(HEADS):
            columns = pl.ds(pl.multiple_of(start + head * HEAD_DIM, HEAD_DIM), HEAD_DIM)
            mix = mixture[:, head_columns(head)]
            scale = lax.rsqrt(jnp.mean(mix * mix, axis=1, keepdims=True) + 1e-05)
            out_ref[:, columns] = (mix * scale * gain_ref[:, columns]).astype(BF16)


def mix_reads(route, gates, gain, own, other):
    out = jax.ShapeDtypeStruct((ROWS, 2 * HALF), BF16)
    cost = (2 * ROWS * 320 * 2 * HALF, 4 * MIB)
    return kernel_call(
        mix_kernel, "mix_reads", out, (), 12, cost, route, gates, gain, *own, *other
    )


def after(array, *first):
    return lax.optimization_barrier((array, *first))[0]


def hop(array, shift):
    return lax.ppermute(array, "memory", [(i, (i + shift) % OWNERS) for i in range(OWNERS)])


def swap(array):
    return lax.ppermute(array, "dp", [(0, 1), (1, 0)])


def shards(
    hidden,
    queries,
    route_ids,
    router_weight,
    key_weight,
    value_weight,
    decay_weight,
    decay_bias,
    norm_gain,
):
    rows, query_rows, route = hidden[0], queries[0], route_ids[0].T
    weights = (key_weight[0], value_weight[0], decay_weight[0].T, decay_bias)

    packed = pack_rows(route, rows)
    arrived = {0: packed[0]}
    for shift in (1, 3, 2):
        arrived[shift] = hop(packed[shift], shift)
    other = {0: swap(packed[0])}
    other_route, other_query = swap(route), swap(query_rows)
    first = project([arrived[0], other[0]], *weights, first=True)
    weights = (first[3], first[4], *weights[2:])
    packed_query = pack_queries(
        after(route, first[2]), other_route, query_rows, other_query, rows, router_weight.T
    )
    gates = packed_query[OWNERS]
    for shift in (1, 3):
        arrived[shift] = after(arrived[shift], gates)
        other[shift] = swap(arrived[shift])
    second = project([arrived[1], other[1], arrived[3], other[3]], *weights)
    arrived[2] = after(arrived[2], second[2])
    other[2] = swap(arrived[2])
    query_in = [packed_query[0]]
    query_in += [hop(after(packed_query[shift], arrived[2]), shift) for shift in (1, 2, 3)]
    third = project([arrived[2], other[2]], *weights)
    units, values, decays = zip(first[:3], second, third)

    message, column, row = block_state(units, values, decays)
    slices = lax.all_to_all(message, "context", 0, 0, tiled=True)
    entry = lax.all_to_all(prefix(slices), "context", 0, 0, tiled=True)
    inner = inner_reads(units, values, query_in, column, row)
    reads = read_out(query_in, inner, column, entry.reshape(HEADS, HEAD_DIM, HEAD_DIM))

    own = [reads[0]] + [hop(reads[shift], -shift) for shift in (1, 2, 3)]
    paired = [swap(part) for part in own]
    return mix_reads(route, gates, norm_gain[None], own, paired)[None]


def solution(mesh):
    in_specs = (
        P(("context", "dp"), "memory", None),
        P(("context", "dp"), "memory", None),
        P(("context", "dp"), "memory", None),
        P(),
        P("memory", None, "dp"),
        P("memory", None, "dp"),
        P("memory", None, "dp"),
        P("memory", "dp"),
        P(),
    )
    out_specs = P(("context", "dp"), "memory", None)
    return jax.shard_map(shards, mesh=mesh, in_specs=in_specs, out_specs=out_specs, check_vma=False)
```

time: 138 us -> 130 us (0.942)
  Pallas kernels: 65.4 us -> 35.9 us
  local copies, waits for them, and re-layouts: 12.7 us -> 21.9 us
  waiting for transfers between devices: 28.4 us -> 36.1 us
  starting transfers between devices: 30.9 us -> 34.7 us
    pallas_call x10, Pallas kernels: 65.4 us -> 35.9 us  [kernel_call(): pl.pallas_call(kernel, out_shape=out_shape, in_specs=[pl.BlockSpec(memory...]
    unnamed x53 -> x78, local copies, waits for them, and re-layouts: 12.7 us -> 21.9 us
    ppermute x10, starting transfers between devices: 7.18 us -> 14.7 us  [swap(): return lax.ppermute(array, 'dp', [(0, 1), (1, 0)])]
    ppermute x9, waiting for transfers between devices: 20.5 us -> 25.2 us  [hop(): lax.ppermute(array, 'memory', [(i, (i + shift) % OWNERS) for i in range(O...]
    ppermute x9, starting transfers between devices: 12.9 us -> 9.22 us  [hop(): lax.ppermute(array, 'memory', [(i, (i + shift) % OWNERS) for i in range(O...]
    ppermute x10, waiting for transfers between devices: 4.1 us -> 5.73 us  [swap(): return lax.ppermute(array, 'dp', [(0, 1), (1, 0)])]
  transfers between devices with their start and end apart: 21 -> 21, of which waited for: 9 -> 11; matrix products, arithmetic and copies ran while one was open for 3% -> 0% of each run, Pallas kernels for 27% -> 18%
where the time goes in v3:
time: 130 us; the launch traced here: 129 us
  waiting for transfers between devices  36.1 us (28%)
  Pallas kernels  35.9 us (28%)
  starting transfers between devices  34.7 us (27%)
  local copies, waits for them, and re-layouts  21.9 us (17%)
    pallas_call x10, Pallas kernels, kernel_call(): pl.pallas_call(kernel, out_shape=out_shape, in_specs=[pl.BlockSpec(memory...  35.9 us
    ppermute x9, waiting for transfers between devices, hop(): lax.ppermute(array, 'memory', [(i, (i + shift) % OWNERS) for i in range(O...  25.2 us
    unnamed x78, local copies, waits for them, and re-layouts  21.9 us
    ppermute x10, starting transfers between devices, swap(): return lax.ppermute(array, 'dp', [(0, 1), (1, 0)])  14.7 us
    ppermute x9, starting transfers between devices, hop(): lax.ppermute(array, 'memory', [(i, (i + shift) % OWNERS) for i in range(O...  9.22 us
    all_to_all x1, starting transfers between devices, shards(): slices = lax.all_to_all(message, 'context', 0, 0, tiled=True)  6.75 us
    ppermute x10, waiting for transfers between devices, swap(): return lax.ppermute(array, 'dp', [(0, 1), (1, 0)])  5.73 us
    all_to_all x1, waiting for transfers between devices, shards(): slices = lax.all_to_all(message, 'context', 0, 0, tiled=True)  5.19 us
  transfers between devices with their start and end apart: 21, of which 11 were waited for; matrix products, arithmetic and copies ran while one was open for 0% of the time, Pallas kernels for 18%

profile of v3, /device:TPU:1, one launch (start us, length us, event | category | flops | bytes accessed | tf_op | source)
XLA Modules:
  0.0 128.9 jit_solution(7484536491118690982)
XLA Ops:
  1.2 1.7 %pack_rows.1 = (bf16[80,4224]{1,0:T(8,128)(2,1)S(1)}, bf16[80,4224]{1,0:T(8,128)(2,1)S(1)}, bf16[80,4224]{1,0:T(8,128)(2,1)S(1)}, bf16[80,4224]{1,0:T(8,128)(2,1)S(1)}) custom-call(s32[2,128]{1,0:T(2,128)} %bitcast.1.route_ref, bf16[128,4096]{1,0:T(8,128)(2,1)S(1)} %bitcast.14), custom_call_target="tpu_custom_call" | custom-call | flops 335544320 | bytes 4194304 | tf_op jit(solution)/shard_map/pack_rows/pallas_call | solution.py:67
  2.9 1.5 %collective-permute-start = (bf16[80,4224]{1,0:T(8,128)(2,1)S(1)}, bf16[80,4224]{1,0:T(8,128)(2,1)S(1)}, u32[]{:S(2)}, u32[]{:S(2)}) collective-permute-start(bf16[80,4224]{1,0:T(8,128)(2,1)S(1)} %get-tuple-element.39.refs_0_), channel_id=1, source_target_pairs={{0,1},{1,0},{2,3},{3,2},{4,5},{5,4},{6,7},{7,6},{8,9},{9,8},{10,11... | collective-permute-start | bytes 2027528 | tf_op jit(solution)/shard_map/ppermute | solution.py:406
  4.4 3.9 %collective-permute-start.6 = (bf16[80,4224]{1,0:T(8,128)(2,1)S(1)}, bf16[80,4224]{1,0:T(8,128)(2,1)S(1)}, u32[]{:S(2)}, u32[]{:S(2)}) collective-permute-start(bf16[80,4224]{1,0:T(8,128)(2,1)S(1)} %get-tuple-element.48), channel_id=1, source_target_pairs={{0,96},{32,0},{64,32},{96,64},{1,97},{33,1},{65,33},{97,65},{2,98}... | collective-permute-start | bytes 2027528 | tf_op jit(solution)/shard_map/ppermute | solution.py:402
  9.7 9.6 %project_2.2 = (bf16[2,80,1024]{2,1,0:T(8,128)(2,1)}, bf16[2,80,1024]{2,1,0:T(8,128)(2,1)}, f32[2,80,128]{2,1,0:T(8,128)}, bf16[4096,1024]{1,0:T(8,128)(2,1)S(1)}, bf16[4096,1024]{1,0:T(8,128)(2,1)S(1)}) custom-call(bf16[80,4224]{1,0:T(8,128)(2,1)} %copy-done.27, bf16[80,4224]{1,0:T(8,128)(2,1)} %copy-done.38, bf16[4096,1024]{1,0:T(8,128)(2,1)} %bitcast.24, ...), custom_call_target="tpu_custom_call" | custom-call | flops 2684354560 | bytes 18874368 | tf_op jit(solution)/shard_map/project_2/pallas_call | solution.py:67
  19.3 1.7 %pack_queries.1 = (bf16[2,80,1024]{2,1,0:T(8,128)(2,1)S(1)}, bf16[2,80,1024]{2,1,0:T(8,128)(2,1)S(1)}, bf16[2,80,1024]{2,1,0:T(8,128)(2,1)S(1)}, bf16[2,80,1024]{2,1,0:T(8,128)(2,1)S(1)}, f32[128,128]{1,0:T(8,128)S(1)}) custom-call(s32[2,128]{1,0:T(2,128)} %bitcast.1.route_ref, s32[2,128]{1,0:T(2,128)S(1)} %collective-permute-done.1.other_route_ref, ...), custom_call_target="tpu_custom_call" | custom-call | flops 167772160 | bytes 4194304 | tf_op jit(solution)/shard_map/pack_queries/pallas_call | solution.py:67
  21.1 1.7 %collective-permute-done.6.refs_2_ = bf16[80,4224]{1,0:T(8,128)(2,1)S(1)} collective-permute-done((bf16[80,4224]{1,0:T(8,128)(2,1)S(1)}, bf16[80,4224]{1,0:T(8,128)(2,1)S(1)}, u32[]{:S(2)}, u32[]{:S(2)}) %collective-permute-start.6) | collective-permute-done | bytes 675872 | tf_op jit(solution)/shard_map/ppermute | solution.py:402
  22.8 3.1 %collective-permute-done.4.refs_0_ = bf16[80,4224]{1,0:T(8,128)(2,1)S(1)} collective-permute-done((bf16[80,4224]{1,0:T(8,128)(2,1)S(1)}, bf16[80,4224]{1,0:T(8,128)(2,1)S(1)}, u32[]{:S(2)}, u32[]{:S(2)}) %collective-permute-start.4) | collective-permute-done | bytes 675872 | tf_op jit(solution)/shard_map/ppermute | solution.py:402
  27.1 1.7 %collective-permute-done.5.refs_1_ = bf16[80,4224]{1,0:T(8,128)(2,1)S(1)} collective-permute-done((bf16[80,4224]{1,0:T(8,128)(2,1)S(1)}, bf16[80,4224]{1,0:T(8,128)(2,1)S(1)}, u32[]{:S(2)}, u32[]{:S(2)}) %collective-permute-start.5) | collective-permute-done | bytes 675872 | tf_op jit(solution)/shard_map/ppermute | solution.py:406
  29.8 6.3 %project_4.1 = (bf16[4,80,1024]{2,1,0:T(8,128)(2,1)S(1)}, bf16[4,80,1024]{2,1,0:T(8,128)(2,1)S(1)}, f32[4,80,128]{2,1,0:T(8,128)S(1)}) custom-call(bf16[80,4224]{1,0:T(8,128)(2,1)S(1)} %collective-permute-done.4.refs_0_, bf16[80,4224]{1,0:T(8,128)(2,1)S(1)} %collective-permute-done.5.refs_1_, bf16[80,4224]{1,0:T(8,128)(2,1)S(1)} %collective-permute-done.6.refs_2_, ...), custom_call_target="tpu_custom_call" | custom-call | flops 5368709120 | bytes 18874368 | tf_op jit(solution)/shard_map/project_4/pallas_call | solution.py:67
  36.1 8.7 %collective-permute-done.3.refs_0_ = bf16[80,4224]{1,0:T(8,128)(2,1)S(1)} collective-permute-done((bf16[80,4224]{1,0:T(8,128)(2,1)S(1)}, bf16[80,4224]{1,0:T(8,128)(2,1)S(1)}, u32[]{:S(2)}, u32[]{:S(2)}) %collective-permute-start.3) | collective-permute-done | bytes 675872 | tf_op jit(solution)/shard_map/ppermute | solution.py:402
  46.2 1.8 %collective-permute-done.11.refs_1_ = bf16[80,4224]{1,0:T(8,128)(2,1)S(1)} collective-permute-done((bf16[80,4224]{1,0:T(8,128)(2,1)S(1)}, bf16[80,4224]{1,0:T(8,128)(2,1)S(1)}, u32[]{:S(2)}, u32[]{:S(2)}) %collective-permute-start.11) | collective-permute-done | bytes 675872 | tf_op jit(solution)/shard_map/ppermute | solution.py:406
  47.9 3.3 %project_2.3 = (bf16[2,80,1024]{2,1,0:T(8,128)(2,1)S(1)}, bf16[2,80,1024]{2,1,0:T(8,128)(2,1)S(1)}, f32[2,80,128]{2,1,0:T(8,128)S(1)}) custom-call(bf16[80,4224]{1,0:T(8,128)(2,1)S(1)} %collective-permute-done.3.refs_0_, bf16[80,4224]{1,0:T(8,128)(2,1)S(1)} %collective-permute-done.11.refs_1_, bf16[4096,1024]{1,0:T(8,128)(2,1)S(1)} %get-tuple-element.50.refs_4_.refs_2_, ...), custom_call_target="tpu_custom_call" | custom-call | flops 2684354560 | bytes 18874368 | tf_op jit(solution)/shard_map/project_2/pallas_call | solution.py:67
  51.3 3.2 %block_state.1 = (bf16[16,80,128]{2,1,0:T(8,128)(2,1)}, f32[640,128]{1,0:T(8,128)S(1)}, f32[8,640]{1,0:T(8,128)S(1)}) custom-call(bf16[2,80,1024]{2,1,0:T(8,128)(2,1)S(1)} %copy-done.17, bf16[4,80,1024]{2,1,0:T(8,128)(2,1)S(1)} %get-tuple-element.60.refs_1_, bf16[2,80,1024]{2,1,0:T(8,128)(2,1)S(1)} %get-tuple-element.61.refs_2_, ...), custom_call_target="tpu_custom_call" | custom-call | flops 167772160 | bytes 4194304 | tf_op jit(solution)/shard_map/block_state/pallas_call | solution.py:67
  55.8 6.8 %all-to-all-start = ((bf16[16,80,128]{2,1,0:T(8,128)(2,1)}), bf16[16,80,128]{2,1,0:T(8,128)(2,1)S(1)}, u32[]{:S(2)}, u32[]{:S(2)}) async-start(bf16[16,80,128]{2,1,0:T(8,128)(2,1)} %get-tuple-element.68), calls=%async_computation | async-start | bytes 655360 | tf_op jit(solution)/shard_map/all_to_all | solution.py:447
  63.8 1.5 %collective-permute-start.10 = (bf16[2,80,1024]{2,1,0:T(8,128)(2,1)S(1)}, bf16[2,80,1024]{2,1,0:T(8,128)(2,1)S(1)}, u32[]{:S(2)}, u32[]{:S(2)}) collective-permute-start(bf16[2,80,1024]{2,1,0:T(8,128)(2,1)S(1)} %get-tuple-element.58), channel_id=1, source_target_pairs={{0,96},{32,0},{64,32},{96,64},{1,97},{33,1},{65,33},{97,65},{2,98}... | collective-permute-start | bytes 983048 | tf_op jit(solution)/shard_map/ppermute | solution.py:402
  65.3 5.2 %all-to-all-done.message = bf16[16,80,128]{2,1,0:T(8,128)(2,1)S(1)} async-done(((bf16[16,80,128]{2,1,0:T(8,128)(2,1)}), bf16[16,80,128]{2,1,0:T(8,128)(2,1)S(1)}, u32[]{:S(2)}, u32[]{:S(2)}) %all-to-all-start) | async-done | bytes 327712 | tf_op jit(solution)/shard_map/all_to_all | solution.py:447
  71.3 4.0 %all-to-all-start.1 = ((bf16[16,64,128]{2,1,0:T(8,128)(2,1)}), bf16[16,64,128]{2,1,0:T(8,128)(2,1)S(1)}, u32[]{:S(2)}, u32[]{:S(2)}) async-start(bf16[16,64,128]{2,1,0:T(8,128)(2,1)} %prefix.1), calls=%async_computation.1 | async-start | bytes 524288 | tf_op jit(solution)/shard_map/all_to_all | solution.py:448
  75.3 4.1 %collective-permute-done.8.refs_7_.refs_1_ = bf16[2,80,1024]{2,1,0:T(8,128)(2,1)S(1)} collective-permute-done((bf16[2,80,1024]{2,1,0:T(8,128)(2,1)S(1)}, bf16[2,80,1024]{2,1,0:T(8,128)(2,1)S(1)}, u32[]{:S(2)}, u32[]{:S(2)}) %collective-permute-start.8) | collective-permute-done | bytes 327712 | tf_op jit(solution)/shard_map/ppermute | solution.py:402
  92.2 5.4 %inner_reads.1.refs_4_ = f32[8,80,1024]{2,1,0:T(8,128)S(1)} custom-call(bf16[2,80,1024]{2,1,0:T(8,128)(2,1)S(1)} %copy-done.18, bf16[4,80,1024]{2,1,0:T(8,128)(2,1)S(1)} %get-tuple-element.60.refs_1_, bf16[2,80,1024]{2,1,0:T(8,128)(2,1)S(1)} %copy-done.22, bf16[2,80,1024]{2,1,0:T(8,128)(2,1)S(1)} %copy-done.20, bf16[4,80,1024]{2,1,0:T(8,128)(2,1)S(1)} %copy-done.1, ...), custom_call_target="tpu_custom_call" | custom-call | flops 1677721600 | bytes 8388608 | tf_op jit(solution)/shard_map/inner_reads/pallas_call | solution.py:67
  103.9 1.9 %collective-permute-start.12 = (bf16[2,80,1024]{2,1,0:T(8,128)(2,1)S(1)}, bf16[2,80,1024]{2,1,0:T(8,128)(2,1)S(1)}, u32[]{:S(2)}, u32[]{:S(2)}) collective-permute-start(bf16[2,80,1024]{2,1,0:T(8,128)(2,1)S(1)} %get-tuple-element.70), channel_id=1, source_target_pairs={{0,96},{32,0},{64,32},{96,64},{1,97},{33,1},{65,33},{97,65},{2,98}... | collective-permute-start | bytes 983048 | tf_op jit(solution)/shard_map/ppermute | solution.py:402
  107.9 5.0 %collective-permute-done.12.refs_1_ = bf16[2,80,1024]{2,1,0:T(8,128)(2,1)S(1)} collective-permute-done((bf16[2,80,1024]{2,1,0:T(8,128)(2,1)S(1)}, bf16[2,80,1024]{2,1,0:T(8,128)(2,1)S(1)}, u32[]{:S(2)}, u32[]{:S(2)}) %collective-permute-start.12) | collective-permute-done | bytes 327712 | tf_op jit(solution)/shard_map/ppermute | solution.py:402
  112.9 7.9 %collective-permute-start.16 = (bf16[2,80,1024]{2,1,0:T(8,128)(2,1)S(1)}, bf16[2,80,1024]{2,1,0:T(8,128)(2,1)S(1)}, u32[]{:S(2)}, u32[]{:S(2)}) collective-permute-start(bf16[2,80,1024]{2,1,0:T(8,128)(2,1)S(1)} %collective-permute-done.12.refs_1_), channel_id=1, source_target_pairs={{0,1},{1,0},{2,3},{3,2},{4,5},{5,4},{6,7},{7,6},{8,9},{9,8},{10,11... | collective-permute-start | bytes 983048 | tf_op jit(solution)/shard_map/ppermute | solution.py:406
  120.8 2.6 %collective-permute-done.14.refs_3_ = bf16[2,80,1024]{2,1,0:T(8,128)(2,1)S(1)} collective-permute-done((bf16[2,80,1024]{2,1,0:T(8,128)(2,1)S(1)}, bf16[2,80,1024]{2,1,0:T(8,128)(2,1)S(1)}, u32[]{:S(2)}, u32[]{:S(2)}) %collective-permute-start.14) | collective-permute-done | bytes 327712 | tf_op jit(solution)/shard_map/ppermute | solution.py:402
  126.3 2.6 %mix_reads.1 = bf16[128,2048]{1,0:T(8,128)(2,1)} custom-call(s32[2,128]{1,0:T(2,128)} %bitcast.1.route_ref, f32[128,128]{1,0:T(8,128)S(1)} %copy-done.32, f32[1,2048]{1,0:T(1,128)S(1)} %bitcast.23, bf16[2,80,1024]{2,1,0:T(8,128)(2,1)S(1)} %get-tuple-element.69.refs_0_, bf16[2,80,1024]{2,1,0:T(8,128)(2,1)S(1)} %collective-permute-done.12.refs_1_, ...), custom_call_target="tpu_custom_call" | custom-call | flops 167772160 | bytes 4194304 | tf_op jit(solution)/shard_map/mix_reads/pallas_call | solution.py:67
  (106 shorter events, 33.4 us)
Async XLA Ops:
  2.9 5.9 %collective-permute-start = (bf16[80,4224]{1,0:T(8,128)(2,1)S(1)}, bf16[80,4224]{1,0:T(8,128)(2,1)S(1)}, u32[]{:S(2)}, u32[]{:S(2)}) collective-permute-start(bf16[80,4224]{1,0:T(8,128)(2,1)S(1)} %get-tuple-element.39.refs_0_), channel_id=1, source_target_pairs={{0,1},{1,0},{2,3},{3,2},{4,5},{5,4},{6,7},{7,6},{8,9},{9,8},{10,11... | collective-permute-start | bytes 2027528 | tf_op jit(solution)/shard_map/ppermute | solution.py:406
  4.4 18.4 %collective-permute-start.6 = (bf16[80,4224]{1,0:T(8,128)(2,1)S(1)}, bf16[80,4224]{1,0:T(8,128)(2,1)S(1)}, u32[]{:S(2)}, u32[]{:S(2)}) collective-permute-start(bf16[80,4224]{1,0:T(8,128)(2,1)S(1)} %get-tuple-element.48), channel_id=1, source_target_pairs={{0,96},{32,0},{64,32},{96,64},{1,97},{33,1},{65,33},{97,65},{2,98}... | collective-permute-start | bytes 2027528 | tf_op jit(solution)/shard_map/ppermute | solution.py:402
  8.3 17.6 %collective-permute-start.4 = (bf16[80,4224]{1,0:T(8,128)(2,1)S(1)}, bf16[80,4224]{1,0:T(8,128)(2,1)S(1)}, u32[]{:S(2)}, u32[]{:S(2)}) collective-permute-start(bf16[80,4224]{1,0:T(8,128)(2,1)S(1)} %get-tuple-element.46), channel_id=1, source_target_pairs={{0,32},{32,64},{64,96},{96,0},{1,33},{33,65},{65,97},{97,1},{2,34}... | collective-permute-start | bytes 2027528 | tf_op jit(solution)/shard_map/ppermute | solution.py:402
  8.3 11.0 %collective-permute-start.2 = (bf16[128,2048]{1,0:T(8,128)(2,1)}, bf16[128,2048]{1,0:T(8,128)(2,1)S(1)}, u32[]{:S(2)}, u32[]{:S(2)}) collective-permute-start(bf16[128,2048]{1,0:T(8,128)(2,1)} %bitcast.17), channel_id=1, source_target_pairs={{0,1},{1,0},{2,3},{3,2},{4,5},{5,4},{6,7},{7,6},{8,9},{9,8},{10,11... | collective-permute-start | bytes 1572872 | tf_op jit(solution)/shard_map/ppermute | solution.py:406
  8.6 10.7 %collective-permute-start.1 = (s32[2,128]{1,0:T(2,128)}, s32[2,128]{1,0:T(2,128)S(1)}, u32[]{:S(2)}, u32[]{:S(2)}) collective-permute-start(s32[2,128]{1,0:T(2,128)} %bitcast.1.route_ref), channel_id=1, source_target_pairs={{0,1},{1,0},{2,3},{3,2},{4,5},{5,4},{6,7},{7,6},{8,9},{9,8},{10,11... | collective-permute-start | bytes 3080 | tf_op jit(solution)/shard_map/ppermute | solution.py:406
  9.6 20.1 %copy-start.29 = (bf16[1,4096,8]{1,2,0:T(8,128)(2,1)S(1)}, bf16[1,4096,8]{1,2,0:T(8,128)(2,1)}, u32[]{:S(2)}) copy-start(bf16[1,4096,8]{1,2,0:T(8,128)(2,1)} %param.15) | copy-start | bytes 196612
  9.6 20.1 %copy-start.37 = (f32[1,8]{1,0:T(1,128)S(1)}, f32[1,8]{1,0:T(1,128)}, u32[]{:S(2)}) copy-start(f32[1,8]{1,0:T(1,128)} %refs_5_.3) | copy-start | bytes 100
  25.9 2.9 %collective-permute-start.5 = (bf16[80,4224]{1,0:T(8,128)(2,1)S(1)}, bf16[80,4224]{1,0:T(8,128)(2,1)S(1)}, u32[]{:S(2)}, u32[]{:S(2)}) collective-permute-start(bf16[80,4224]{1,0:T(8,128)(2,1)S(1)} %collective-permute-done.4.refs_0_), channel_id=1, source_target_pairs={{0,1},{1,0},{2,3},{3,2},{4,5},{5,4},{6,7},{7,6},{8,9},{9,8},{10,11... | collective-permute-start | bytes 2027528 | tf_op jit(solution)/shard_map/ppermute | solution.py:406
  27.1 2.7 %collective-permute-start.7 = (bf16[80,4224]{1,0:T(8,128)(2,1)S(1)}, bf16[80,4224]{1,0:T(8,128)(2,1)S(1)}, u32[]{:S(2)}, u32[]{:S(2)}) collective-permute-start(bf16[80,4224]{1,0:T(8,128)(2,1)S(1)} %collective-permute-done.6.refs_2_), channel_id=1, source_target_pairs={{0,1},{1,0},{2,3},{3,2},{4,5},{5,4},{6,7},{7,6},{8,9},{9,8},{10,11... | collective-permute-start | bytes 2027528 | tf_op jit(solution)/shard_map/ppermute | solution.py:406
  27.1 17.7 %collective-permute-start.3 = (bf16[80,4224]{1,0:T(8,128)(2,1)S(1)}, bf16[80,4224]{1,0:T(8,128)(2,1)S(1)}, u32[]{:S(2)}, u32[]{:S(2)}) collective-permute-start(bf16[80,4224]{1,0:T(8,128)(2,1)S(1)} %get-tuple-element.45), channel_id=1, source_target_pairs={{0,64},{32,96},{64,0},{96,32},{1,65},{33,97},{65,1},{97,33},{2,66}... | collective-permute-start | bytes 2027528 | tf_op jit(solution)/shard_map/ppermute | solution.py:402
  44.8 3.1 %collective-permute-start.11 = (bf16[80,4224]{1,0:T(8,128)(2,1)S(1)}, bf16[80,4224]{1,0:T(8,128)(2,1)S(1)}, u32[]{:S(2)}, u32[]{:S(2)}) collective-permute-start(bf16[80,4224]{1,0:T(8,128)(2,1)S(1)} %collective-permute-done.3.refs_0_), channel_id=1, source_target_pairs={{0,1},{1,0},{2,3},{3,2},{4,5},{5,4},{6,7},{7,6},{8,9},{9,8},{10,11... | collective-permute-start | bytes 2027528 | tf_op jit(solution)/shard_map/ppermute | solution.py:406
  51.2 74.3 %copy-start.36 = (f32[2048]{0:T(1024)S(1)}, f32[2048]{0:T(1024)}, u32[]{:S(2)}) copy-start(f32[2048]{0:T(1024)} %param.17) | copy-start | bytes 24580
  55.8 14.7 %all-to-all-start = ((bf16[16,80,128]{2,1,0:T(8,128)(2,1)}), bf16[16,80,128]{2,1,0:T(8,128)(2,1)S(1)}, u32[]{:S(2)}, u32[]{:S(2)}) async-start(bf16[16,80,128]{2,1,0:T(8,128)(2,1)} %get-tuple-element.68), calls=%async_computation | async-start | bytes 655360 | tf_op jit(solution)/shard_map/all_to_all | solution.py:447
  62.5 16.9 %collective-permute-start.8 = (bf16[2,80,1024]{2,1,0:T(8,128)(2,1)S(1)}, bf16[2,80,1024]{2,1,0:T(8,128)(2,1)S(1)}, u32[]{:S(2)}, u32[]{:S(2)}) collective-permute-start(bf16[2,80,1024]{2,1,0:T(8,128)(2,1)S(1)} %get-tuple-element.54), channel_id=1, source_target_pairs={{0,32},{32,64},{64,96},{96,0},{1,33},{33,65},{65,97},{97,1},{2,34}... | collective-permute-start | bytes 983048 | tf_op jit(solution)/shard_map/ppermute | solution.py:402
  62.6 17.6 %collective-permute-start.9 = (bf16[2,80,1024]{2,1,0:T(8,128)(2,1)S(1)}, bf16[2,80,1024]{2,1,0:T(8,128)(2,1)S(1)}, u32[]{:S(2)}, u32[]{:S(2)}) collective-permute-start(bf16[2,80,1024]{2,1,0:T(8,128)(2,1)S(1)} %get-tuple-element.56), channel_id=1, source_target_pairs={{0,64},{32,96},{64,0},{96,32},{1,65},{33,97},{65,1},{97,33},{2,66}... | collective-permute-start | bytes 983048 | tf_op jit(solution)/shard_map/ppermute | solution.py:402
  63.8 17.1 %collective-permute-start.10 = (bf16[2,80,1024]{2,1,0:T(8,128)(2,1)S(1)}, bf16[2,80,1024]{2,1,0:T(8,128)(2,1)S(1)}, u32[]{:S(2)}, u32[]{:S(2)}) collective-permute-start(bf16[2,80,1024]{2,1,0:T(8,128)(2,1)S(1)} %get-tuple-element.58), channel_id=1, source_target_pairs={{0,96},{32,0},{64,32},{96,64},{1,97},{33,1},{65,33},{97,65},{2,98}... | collective-permute-start | bytes 983048 | tf_op jit(solution)/shard_map/ppermute | solution.py:402
  71.3 26.4 %all-to-all-start.1 = ((bf16[16,64,128]{2,1,0:T(8,128)(2,1)}), bf16[16,64,128]{2,1,0:T(8,128)(2,1)S(1)}, u32[]{:S(2)}, u32[]{:S(2)}) async-start(bf16[16,64,128]{2,1,0:T(8,128)(2,1)} %prefix.1), calls=%async_computation.1 | async-start | bytes 524288 | tf_op jit(solution)/shard_map/all_to_all | solution.py:448
  103.9 9.0 %collective-permute-start.12 = (bf16[2,80,1024]{2,1,0:T(8,128)(2,1)S(1)}, bf16[2,80,1024]{2,1,0:T(8,128)(2,1)S(1)}, u32[]{:S(2)}, u32[]{:S(2)}) collective-permute-start(bf16[2,80,1024]{2,1,0:T(8,128)(2,1)S(1)} %get-tuple-element.70), channel_id=1, source_target_pairs={{0,96},{32,0},{64,32},{96,64},{1,97},{33,1},{65,33},{97,65},{2,98}... | collective-permute-start | bytes 983048 | tf_op jit(solution)/shard_map/ppermute | solution.py:402
  105.8 15.0 %collective-permute-start.13 = (bf16[2,80,1024]{2,1,0:T(8,128)(2,1)S(1)}, bf16[2,80,1024]{2,1,0:T(8,128)(2,1)S(1)}, u32[]{:S(2)}, u32[]{:S(2)}) collective-permute-start(bf16[2,80,1024]{2,1,0:T(8,128)(2,1)S(1)} %get-tuple-element.71), channel_id=1, source_target_pairs={{0,64},{32,96},{64,0},{96,32},{1,65},{33,97},{65,1},{97,33},{2,66}... | collective-permute-start | bytes 983048 | tf_op jit(solution)/shard_map/ppermute | solution.py:402
  105.8 17.5 %collective-permute-start.14 = (bf16[2,80,1024]{2,1,0:T(8,128)(2,1)S(1)}, bf16[2,80,1024]{2,1,0:T(8,128)(2,1)S(1)}, u32[]{:S(2)}, u32[]{:S(2)}) collective-permute-start(bf16[2,80,1024]{2,1,0:T(8,128)(2,1)S(1)} %get-tuple-element.72), channel_id=1, source_target_pairs={{0,32},{32,64},{64,96},{96,0},{1,33},{33,65},{65,97},{97,1},{2,34}... | collective-permute-start | bytes 983048 | tf_op jit(solution)/shard_map/ppermute | solution.py:402
  106.5 17.7 %collective-permute-start.15 = (bf16[2,80,1024]{2,1,0:T(8,128)(2,1)S(1)}, bf16[2,80,1024]{2,1,0:T(8,128)(2,1)S(1)}, u32[]{:S(2)}, u32[]{:S(2)}) collective-permute-start(bf16[2,80,1024]{2,1,0:T(8,128)(2,1)S(1)} %get-tuple-element.69.refs_0_), channel_id=1, source_target_pairs={{0,1},{1,0},{2,3},{3,2},{4,5},{5,4},{6,7},{7,6},{8,9},{9,8},{10,11... | collective-permute-start | bytes 983048 | tf_op jit(solution)/shard_map/ppermute | solution.py:406
  112.9 11.3 %collective-permute-start.16 = (bf16[2,80,1024]{2,1,0:T(8,128)(2,1)S(1)}, bf16[2,80,1024]{2,1,0:T(8,128)(2,1)S(1)}, u32[]{:S(2)}, u32[]{:S(2)}) collective-permute-start(bf16[2,80,1024]{2,1,0:T(8,128)(2,1)S(1)} %collective-permute-done.12.refs_1_), channel_id=1, source_target_pairs={{0,1},{1,0},{2,3},{3,2},{4,5},{5,4},{6,7},{7,6},{8,9},{9,8},{10,11... | collective-permute-start | bytes 983048 | tf_op jit(solution)/shard_map/ppermute | solution.py:406
  120.8 3.4 %collective-permute-start.17 = (bf16[2,80,1024]{2,1,0:T(8,128)(2,1)S(1)}, bf16[2,80,1024]{2,1,0:T(8,128)(2,1)S(1)}, u32[]{:S(2)}, u32[]{:S(2)}) collective-permute-start(bf16[2,80,1024]{2,1,0:T(8,128)(2,1)S(1)} %collective-permute-done.13.refs_2_), channel_id=1, source_target_pairs={{0,1},{1,0},{2,3},{3,2},{4,5},{5,4},{6,7},{7,6},{8,9},{9,8},{10,11... | collective-permute-start | bytes 983048 | tf_op jit(solution)/shard_map/ppermute | solution.py:406
  123.4 2.1 %collective-permute-start.18 = (bf16[2,80,1024]{2,1,0:T(8,128)(2,1)S(1)}, bf16[2,80,1024]{2,1,0:T(8,128)(2,1)S(1)}, u32[]{:S(2)}, u32[]{:S(2)}) collective-permute-start(bf16[2,80,1024]{2,1,0:T(8,128)(2,1)S(1)} %collective-permute-done.14.refs_3_), channel_id=1, source_target_pairs={{0,1},{1,0},{2,3},{3,2},{4,5},{5,4},{6,7},{7,6},{8,9},{9,8},{10,11... | collective-permute-start | bytes 983048 | tf_op jit(solution)/shard_map/ppermute | solution.py:406
  (36 other events, 128.0 us)

commit v4 on v3

--- a/solution.py
+++ b/solution.py
@@ -16,9 +16,11 @@
 SLOTS = CHUNKS * CAP
 HALF = 1024
 HEADS = HALF // HEAD_DIM
-CONTEXTS = 16
-LIVE = 128
-PIECE = HALF // CONTEXTS
+EMPTY = 64.0
+PAD = 128
+PACKS = 4
+RING = 4
+PIECE = HALF // RING
 TAIL = 16
 F32 = jnp.float32
 BF16 = jnp.bfloat16
@@ -41,12 +43,12 @@
     return lax.dot_general(a, b, (((0,), (0,)), ((), ())), preferred_element_type=F32)
 
 
-def source(owner, shift):
-    return (owner + OWNERS - shift) & (OWNERS - 1)
+def near(shape, dtype):
+    return pltpu.VMEM(shape, dtype)
 
 
 def position(shift, partner, owner, core):
-    return (core ^ partner) * OWNERS + source(owner, shift)
+    return (core ^ partner) * OWNERS + (owner ^ shift)
 
 
 def membership(route):
@@ -62,7 +64,7 @@
     return (iota((slots, ROWS), 0).astype(F32) == mine).astype(F32)
 
 
-def kernel_call(kernel, name, out_shape, scratch, limit, cost, *operands, hbm=()):
+def kernel_call(kernel, name, out_shape, scratch, limit, *operands, hbm=(), moved=1):
     spaces = [pltpu.HBM if at in hbm else pltpu.VMEM for at in range(len(operands))]
     return pl.pallas_call(
         kernel,
@@ -71,33 +73,52 @@
         out_specs=jax.tree.map(lambda _: pl.BlockSpec(memory_space=pltpu.VMEM), out_shape),
         scratch_shapes=scratch,
         compiler_params=pltpu.CompilerParams(vmem_limit_bytes=limit * MIB),
-        cost_estimate=pl.CostEstimate(
-            flops=cost[0], bytes_accessed=cost[1], transcendentals=0
-        ),
+        cost_estimate=pl.CostEstimate(flops=1, bytes_accessed=moved, transcendentals=0),
         name=name,
     )(*operands)
 
 
-def pack_rows_kernel(route_ref, rows_ref, *out_refs):
+def pack_rows_kernel(route_hbm, rows_hbm, *refs):
+    out_refs, (route_ref, rows_ref, sems) = refs[:OWNERS], refs[OWNERS:]
     owner = lax.axis_index("memory")
+    width = D // PACKS
+    route_copy = pltpu.make_async_copy(route_hbm, route_ref, sems.at[PACKS])
+    route_copy.start()
+    copies = []
+    for at in range(PACKS):
+        columns = slice(at * width, (at + 1) * width)
+        copies.append(
+            pltpu.make_async_copy(rows_hbm.at[:, columns], rows_ref.at[:, columns], sems.at[at])
+        )
+        copies[at].start()
+    route_copy.wait()
     place = membership(route_ref[...])[1]
-    pick = jnp.concatenate(
-        [one_hot(place, (owner + shift) & (OWNERS - 1)) for shift in range(OWNERS)], axis=0
-    ).astype(BF16)
-    width = 512
-    for column in range(0, D, width):
-        part = dot(pick, rows_ref[:, column : column + width]).astype(BF16)
+    pick = jnp.concatenate([one_hot(place, owner ^ shift) for shift in range(OWNERS)], axis=0)
+    empty = jnp.sum(pick, axis=1, keepdims=True) == 0.0
+    pick = pick.astype(BF16)
+    first_lane = iota((OWNERS * CAP, HEAD_DIM), 1) == 0
+    for at in range(PACKS):
+        copies[at].wait()
+        part = dot(pick, rows_ref[:, at * width : (at + 1) * width])
+        if at == 0:
+            marked = jnp.where(first_lane & empty, EMPTY, part[:, :HEAD_DIM])
+            part = jnp.concatenate([marked, part[:, HEAD_DIM:]], axis=1)
+        part = part.astype(BF16)
         for shift in range(OWNERS):
-            out_refs[shift][:, column : column + width] = part[shift * CAP : (shift + 1) * CAP]
-    live = dot(pick, jnp.ones((ROWS, LIVE), BF16)).astype(BF16)
-    for shift in range(OWNERS):
-        out_refs[shift][:, D:] = live[shift * CAP : (shift + 1) * CAP]
+            out_refs[shift][:, at * width : (at + 1) * width] = part[
+                shift * CAP : (shift + 1) * CAP
+            ]
+    out_refs[2][:, D:] = jnp.zeros((CAP, PAD), BF16)
 
 
 def pack_rows(route, rows):
-    out = [jax.ShapeDtypeStruct((CAP, D + LIVE), BF16)] * OWNERS
-    cost = (2 * 320 * 128 * D, 4 * MIB)
-    return kernel_call(pack_rows_kernel, "pack_rows", out, (), 12, cost, route, rows)
+    out = [near((CAP, D + PAD * (shift == 2)), BF16) for shift in range(OWNERS)]
+    scratch = [
+        pltpu.VMEM((2, ROWS), jnp.int32),
+        pltpu.VMEM((ROWS, D), BF16),
+        pltpu.SemaphoreType.DMA((PACKS + 1,)),
+    ]
+    return kernel_call(pack_rows_kernel, "pack_rows", out, scratch, 56, route, rows, hbm=(0, 1))
 
 
 def pack_queries_kernel(
@@ -111,7 +132,7 @@
     ):
         named, place = membership(routes[...])
         pick = jnp.concatenate(
-            [one_hot(place, (owner + shift) & (OWNERS - 1)) for shift in range(OWNERS)], axis=0
+            [one_hot(place, owner ^ shift) for shift in range(OWNERS)], axis=0
         ).astype(BF16)
         part = dot(pick, queries[:, pl.ds(mine, HALF)]).astype(BF16)
         for shift in range(OWNERS):
@@ -126,11 +147,12 @@
 
 
 def pack_queries(route, other_route, queries, other_queries, rows, router_weight):
-    out = [jax.ShapeDtypeStruct((2, CAP, HALF), BF16)] * OWNERS
-    out = out + [jax.ShapeDtypeStruct((ROWS, 128), F32)]
-    cost = (2 * 640 * 128 * HALF, 4 * MIB)
+    out = [near((2, CAP, HALF), BF16)] * OWNERS
+    out = out + [near((ROWS, 128), F32)]
     operands = (route, other_route, queries, other_queries, rows, router_weight)
-    return kernel_call(pack_queries_kernel, "pack_queries", out, (), 12, cost, *operands)
+    return kernel_call(
+        pack_queries_kernel, "pack_queries", out, (), 12, *operands, moved=4 * MIB
+    )
 
 
 def log_sigmoid(x):
@@ -147,13 +169,17 @@
 def project_parts(row_refs, decay_ref, bias_ref, outs, key_ref, value_ref, held, ready):
     count = len(row_refs)
     unit_out, value_out, decay_out = outs
+    lives = []
     for at in range(count):
-        held[at * CAP : (at + 1) * CAP] = row_refs[at][:, :D]
+        rows = slice(at * CAP, (at + 1) * CAP)
+        head = row_refs[at][:, :HEAD_DIM].astype(F32)
+        lives.append(head[:, :1] < EMPTY / 2)
+        held[rows, :HEAD_DIM] = jnp.where(lives[at], head, 0.0).astype(BF16)
+        held[rows, HEAD_DIM:] = row_refs[at][:, HEAD_DIM:D]
     decay = log_sigmoid(dot_rows(held[...], decay_ref[...]) + bias_ref[...])
     decay_out[...] = jnp.zeros_like(decay_out)
     for at in range(count):
-        live = row_refs[at][:, D : D + HEADS].astype(F32)
-        decay_out[at, :, :HEADS] = decay[at * CAP : (at + 1) * CAP] * live
+        decay_out[at, :, :HEADS] = jnp.where(lives[at], decay[at * CAP : (at + 1) * CAP], 0.0)
     for start in range(0, HALF, WIDTH):
         ready(start // WIDTH)
         columns = slice(start, start + WIDTH)
@@ -198,13 +224,12 @@
 
 def project(row_parts, key_weight, value_weight, decay_weight, decay_bias, first=False):
     count = len(row_parts)
-    out = [jax.ShapeDtypeStruct((count, CAP, HALF), BF16)] * 2
-    out = out + [jax.ShapeDtypeStruct((count, CAP, 128), F32)]
+    out = [near((count, CAP, HALF), BF16)] * 2
+    out = out + [near((count, CAP, 128), F32)]
     scratch = [pltpu.VMEM((count * CAP, D), BF16)]
-    cost = (2 * count * CAP * D * 2 * HALF, 18 * MIB)
     kernel = project_first_kernel if first else project_next_kernel
     if first:
-        out = out + [pltpu.VMEM((D, HALF), BF16)] * 2
+        out = out + [near((D, HALF), BF16)] * 2
         scratch = scratch + [pltpu.SemaphoreType.DMA((2, HALF // WIDTH))]
     return kernel_call(
         functools.partial(kernel, count),
@@ -212,7 +237,6 @@
         out,
         scratch,
         40 if first else 12,
-        cost,
         *row_parts,
         key_weight,
         value_weight,
@@ -236,9 +260,25 @@
     return slice(head * HEAD_DIM, (head + 1) * HEAD_DIM)
 
 
+def place_in_context():
+    context = lax.axis_index("context")
+    return context >> 2, context & (RING - 1)
+
+
+def two_parts(number):
+    wide = jnp.broadcast_to(number, (TAIL, 128))
+    high = wide.astype(BF16).astype(F32)
+    return jnp.where(iota((TAIL, 128), 0) < TAIL // 2, high, wide - high).astype(BF16)
+
+
+def from_parts(rows):
+    return rows[:1].astype(F32) + rows[TAIL // 2 : TAIL // 2 + 1].astype(F32)
+
+
 def state_kernel(*refs):
     unit_refs, value_refs, decay_refs = refs[0:3], refs[3:6], refs[6:9]
-    message, column_out, row_out, units, values, decays = refs[9:]
+    messages = refs[9:13]
+    column_out, row_out, units, values, decays, quarters = refs[13:]
     token_order(decay_refs, decays)
     total = decays[...].reshape(SLOTS, 128).T[:HEADS]
     lane = iota((HEADS, SLOTS), 1)
@@ -258,60 +298,108 @@
         faded = (unit * fade[:, head : head + 1]).astype(BF16)
         value = values[:, :, head_columns(head)].reshape(SLOTS, HEAD_DIM)
         state = dot_columns(faded, value).astype(BF16)
-        ended = jnp.broadcast_to(last[:, head : head + 1], (TAIL, 128))
-        high = ended.astype(BF16).astype(F32)
-        tail = jnp.where(iota((TAIL, 128), 0) < TAIL // 2, high, ended - high).astype(BF16)
-        for part in range(2):
-            message[head * 2 + part, :PIECE] = state[part * PIECE : (part + 1) * PIECE]
-            message[head * 2 + part, PIECE:] = tail
+        at = head % 2 * HEAD_DIM
+        quarters[head // 2, at : at + HEAD_DIM] = state
+        tail = PIECE + head % 2 * TAIL
+        quarters[head // 2, tail : tail + TAIL] = two_parts(last[:, head : head + 1])
+    _, column = place_in_context()
+    for shift in range(RING):
+        messages[shift][...] = quarters[column ^ shift]
 
 
 def block_state(units, values, decays):
-    out = [
-        jax.ShapeDtypeStruct((CONTEXTS, PIECE + TAIL, 128), BF16),
-        jax.ShapeDtypeStruct((SLOTS, 128), F32),
-        jax.ShapeDtypeStruct((HEADS, SLOTS), F32),
+    out = [near((PIECE + 2 * TAIL, 128), BF16)] * RING + [
+        near((SLOTS, 128), F32),
+        near((HEADS, SLOTS), F32),
+        near((CHUNKS, CAP, HALF), BF16),
+        near((CHUNKS, CAP, HALF), BF16),
     ]
     scratch = [
-        pltpu.VMEM((CHUNKS, CAP, HALF), BF16),
-        pltpu.VMEM((CHUNKS, CAP, HALF), BF16),
         pltpu.VMEM((CHUNKS, CAP, 128), F32),
+        pltpu.VMEM((RING, PIECE + 2 * TAIL, 128), BF16),
     ]
-    cost = (2 * SLOTS * HALF * 128, 4 * MIB)
     return kernel_call(
-        state_kernel, "block_state", out, scratch, 12, cost, *units, *values, *decays
-    )
-
-
-def prefix_kernel(message, entry):
-    before = jnp.zeros((PIECE, 128), F32)
-    for context in range(CONTEXTS):
-        entry[context] = before.astype(BF16)
-        high = message[context, PIECE : PIECE + 1].astype(F32)
-        low = message[context, PIECE + TAIL // 2 : PIECE + TAIL // 2 + 1].astype(F32)
-        before = jnp.exp(high + low) * before + message[context, :PIECE].astype(F32)
-
-
-def prefix(message):
-    out = jax.ShapeDtypeStruct((CONTEXTS, PIECE, 128), BF16)
-    return kernel_call(prefix_kernel, "prefix", out, (), 4, (MIB, MIB), message)
+        state_kernel, "block_state", out, scratch, 12, *units, *values, *decays
+    )
+
+
+def ring_order(refs, held, me):
+    for shift in range(RING):
+        held[me ^ shift] = refs[shift][...]
+
+
+def row_prefix_kernel(*refs):
+    pieces, (whole, before, faded, held) = refs[:RING], refs[RING:]
+    ring_order(pieces, held, place_in_context()[1])
+    for head in range(2):
+        rows = slice(head * HEAD_DIM, (head + 1) * HEAD_DIM)
+        tail = slice(PIECE + head * TAIL, PIECE + (head + 1) * TAIL)
+        state, total = jnp.zeros((HEAD_DIM, 128), F32), jnp.zeros((1, 128), F32)
+        for column in range(RING):
+            before[column, rows] = state
+            faded[column, head * 8 : head * 8 + 8] = jnp.broadcast_to(jnp.exp(total), (8, 128))
+            ended = from_parts(held[column, tail])
+            state = jnp.exp(ended) * state + held[column, rows].astype(F32)
+            total = total + ended
+        whole[rows] = state.astype(BF16)
+        whole[tail] = two_parts(total)
+
+
+def row_prefix(pieces):
+    out = [
+        near((PIECE + 2 * TAIL, 128), BF16),
+        near((RING, PIECE, 128), F32),
+        near((RING, 16, 128), F32),
+    ]
+    scratch = [pltpu.VMEM((RING, PIECE + 2 * TAIL, 128), BF16)]
+    return kernel_call(row_prefix_kernel, "row_prefix", out, scratch, 8, *pieces)
+
+
+def entry_kernel(*refs):
+    pieces, (before, faded) = refs[:RING], refs[RING : RING + 2]
+    out_refs, (held, entries) = refs[RING + 2 : 2 * RING + 2], refs[2 * RING + 2 :]
+    row, mine = place_in_context()
+    ring_order(pieces, held, row)
+    for head in range(2):
+        rows = slice(head * HEAD_DIM, (head + 1) * HEAD_DIM)
+        tail = slice(PIECE + head * TAIL, PIECE + (head + 1) * TAIL)
+        state = jnp.zeros((HEAD_DIM, 128), F32)
+        for earlier in range(RING - 1):
+            kept = jnp.exp(from_parts(held[earlier, tail])) * state
+            kept = kept + held[earlier, rows].astype(F32)
+            state = jnp.where(earlier < row, kept, state)
+        for column in range(RING):
+            fade = faded[column, head * 8 : head * 8 + 1]
+            entries[column, rows] = (before[column, rows] + fade * state).astype(BF16)
+    for shift in range(RING):
+        out_refs[shift][...] = entries[mine ^ shift]
+
+
+def entry_states(pieces, before, faded):
+    out = [near((PIECE, 128), BF16)] * RING
+    scratch = [
+        pltpu.VMEM((RING, PIECE + 2 * TAIL, 128), BF16),
+        pltpu.VMEM((RING, PIECE, 128), BF16),
+    ]
+    return kernel_call(entry_kernel, "entry_states", out, scratch, 8, *pieces, before, faded)
 
 
 def order_queries(query_refs, held):
     owner = lax.axis_index("memory")
     for shift in range(OWNERS):
         for core in range(2):
-            held[core * OWNERS + source(owner, shift)] = query_refs[shift][core]
-
-
-def inner_kernel(*refs):
-    unit_refs, value_refs, query_refs = refs[0:3], refs[3:6], refs[6:10]
-    column_ref, row_ref, inner, units, values, queries = refs[10:]
-    token_order(unit_refs, units)
-    token_order(value_refs, values)
-    order_queries(query_refs, queries)
+            held[core * OWNERS + (owner ^ shift)] = query_refs[shift][core]
+
+
+def inner_kernel(start, *refs):
+    units, values, column_ref, row_ref = refs[0:4]
+    if start == 0:
+        inner, queries = refs[8:10]
+        order_queries(refs[4:8], queries)
+    else:
+        queries, inner = refs[4:6]
     tile = 2 * CAP
-    for head in range(HEADS):
+    for head in range(start, start + HEADS // 2):
         columns = head_columns(head)
         running = column_ref[:, head : head + 1]
         running_row = row_ref[head : head + 1]
@@ -325,41 +413,40 @@
             causal = iota((tile, reach), 0) + block * tile >= iota((tile, reach), 1)
             score = (score * jnp.exp(jnp.where(causal, spread, -1e30))).astype(BF16)
             result = dot(score, value[:reach])
-            inner[2 * block : 2 * block + 2, :, columns] = result.reshape(2, CAP, HEAD_DIM)
-
-
-def inner_reads(units, values, queries, column, row):
-    out = jax.ShapeDtypeStruct((CHUNKS, CAP, HALF), F32)
-    scratch = [pltpu.VMEM((CHUNKS, CAP, HALF), BF16)] * 3
-    cost = (4 * SLOTS * SLOTS * HALF, 8 * MIB)
-    operands = (*units, *values, *queries, column, row)
-    return kernel_call(inner_kernel, "inner_reads", out, scratch, 16, cost, *operands)
+            inner[2 * block : 2 * block + 2, :, head_columns(head - start)] = result.reshape(2, CAP, HEAD_DIM)
+
+
+def inner_reads(start, units, values, column, row, *queries):
+    out = [near((CHUNKS, CAP, HALF // 2), F32)]
+    if start == 0:
+        out = out + [near((CHUNKS, CAP, HALF), BF16)]
+    kernel = functools.partial(inner_kernel, start)
+    operands = (units, values, column, row, *queries)
+    return kernel_call(kernel, f"inner_reads_{start}", out, (), 16, *operands)
 
 
 def read_kernel(*refs):
-    query_refs = refs[0:4]
-    inner, column_ref, entry = refs[4:7]
-    out_refs = refs[7:11]
-    queries, reads = refs[11:]
+    queries, inners, column_ref = refs[0], refs[1:3], refs[3]
+    out_refs, (reads, entries) = refs[8:12], refs[12:]
+    ring_order(refs[4:8], entries, place_in_context()[1])
     owner = lax.axis_index("memory")
-    order_queries(query_refs, queries)
     fade = jnp.exp(column_ref[...])
     for head in range(HEADS):
         columns = head_columns(head)
-        carried = dot(queries[:, :, columns].reshape(SLOTS, HEAD_DIM), entry[head])
-        result = inner[:, :, columns].reshape(SLOTS, HEAD_DIM) + fade[:, head : head + 1] * carried
+        carried = dot(queries[:, :, columns].reshape(SLOTS, HEAD_DIM), entries[head // 2, head % 2 * HEAD_DIM : (head % 2 + 1) * HEAD_DIM])
+        inner = inners[head // 4][:, :, head_columns(head % 4)]
+        result = inner.reshape(SLOTS, HEAD_DIM) + fade[:, head : head + 1] * carried
         reads[:, :, columns] = result.astype(BF16).reshape(CHUNKS, CAP, HEAD_DIM)
     for shift in range(OWNERS):
         for core in range(2):
-            out_refs[shift][core] = reads[core * OWNERS + source(owner, shift)]
-
-
-def read_out(queries, inner, column, entry):
-    out = [jax.ShapeDtypeStruct((2, CAP, HALF), BF16)] * OWNERS
-    scratch = [pltpu.VMEM((CHUNKS, CAP, HALF), BF16)] * 2
-    cost = (2 * SLOTS * HALF * 128, 6 * MIB)
+            out_refs[shift][core] = reads[core * OWNERS + (owner ^ shift)]
+
+
+def read_out(queries, inners, column, entry):
+    out = [near((2, CAP, HALF), BF16)] * OWNERS
+    scratch = [pltpu.VMEM((CHUNKS, CAP, HALF), BF16), pltpu.VMEM((RING, PIECE, 128), BF16)]
     return kernel_call(
-        read_kernel, "read_out", out, scratch, 12, cost, *queries, inner, column, entry
+        read_kernel, "read_out", out, scratch, 12, queries, *inners, column, *entry
     )
 
 
@@ -370,7 +457,7 @@
     picks, gates = [], []
     lane = iota((ROWS, 128), 1)
     for shift in range(OWNERS):
-        memory = (owner + shift) & (OWNERS - 1)
+        memory = owner ^ shift
         picks.append(one_hot(place, memory, 128).T.astype(BF16)[:, :CAP])
         gate = jnp.where(lane == memory, gates_ref[...], 0.0)
         gates.append(jnp.sum(gate, axis=1, keepdims=True))
@@ -388,9 +475,8 @@
 
 def mix_reads(route, gates, gain, own, other):
     out = jax.ShapeDtypeStruct((ROWS, 2 * HALF), BF16)
-    cost = (2 * ROWS * 320 * 2 * HALF, 4 * MIB)
     return kernel_call(
-        mix_kernel, "mix_reads", out, (), 12, cost, route, gates, gain, *own, *other
+        mix_kernel, "mix_reads", out, (), 12, route, gates, gain, *own, *other
     )
 
 
@@ -399,7 +485,15 @@
 
 
 def hop(array, shift):
-    return lax.ppermute(array, "memory", [(i, (i + shift) % OWNERS) for i in range(OWNERS)])
+    return lax.ppermute(array, "memory", [(i, i ^ shift) for i in range(OWNERS)])
+
+
+def exchange(arrays, stride):
+    out = [arrays[0]]
+    for shift in (1, 2, 3):
+        pairs = [(i, i ^ shift * stride) for i in range(RING * RING)]
+        out.append(lax.ppermute(arrays[shift], "context", pairs))
+    return out
 
 
 def swap(array):
@@ -422,7 +516,7 @@
 
     packed = pack_rows(route, rows)
     arrived = {0: packed[0]}
-    for shift in (1, 3, 2):
+    for shift in (1, 3):
         arrived[shift] = hop(packed[shift], shift)
     other = {0: swap(packed[0])}
     other_route, other_query = swap(route), swap(query_rows)
@@ -434,22 +528,27 @@
     gates = packed_query[OWNERS]
     for shift in (1, 3):
         arrived[shift] = after(arrived[shift], gates)
+    arrived[2] = hop(after(packed[2], arrived[1], arrived[3]), 2)
+    for shift in (1, 3):
         other[shift] = swap(arrived[shift])
     second = project([arrived[1], other[1], arrived[3], other[3]], *weights)
     arrived[2] = after(arrived[2], second[2])
     other[2] = swap(arrived[2])
-    query_in = [packed_query[0]]
-    query_in += [hop(after(packed_query[shift], arrived[2]), shift) for shift in (1, 2, 3)]
     third = project([arrived[2], other[2]], *weights)
     units, values, decays = zip(first[:3], second, third)
 
-    message, column, row = block_state(units, values, decays)
-    slices = lax.all_to_all(message, "context", 0, 0, tiled=True)
-    entry = lax.all_to_all(prefix(slices), "context", 0, 0, tiled=True)
-    inner = inner_reads(units, values, query_in, column, row)
-    reads = read_out(query_in, inner, column, entry.reshape(HEADS, HEAD_DIM, HEAD_DIM))
-
-    own = [reads[0]] + [hop(reads[shift], -shift) for shift in (1, 2, 3)]
+    *messages, column, row, units, values = block_state(units, values, decays)
+    query_in = [packed_query[0]]
+    query_in += [hop(after(packed_query[shift], second[2]), shift) for shift in (1, 2, 3)]
+    whole, before, faded = row_prefix(exchange(messages, 1))
+    totals = exchange([whole] * RING, RING)
+    inner_low, ordered = inner_reads(0, units, values, column, row, *query_in)
+    totals[0] = after(totals[0], inner_low)
+    entry = exchange(entry_states(totals, before, faded), 1)
+    (inner_high,) = inner_reads(HEADS // 2, units, values, column, row, ordered)
+    reads = read_out(ordered, (inner_low, inner_high), column, entry)
+
+    own = [reads[0]] + [hop(reads[shift], shift) for shift in (1, 2, 3)]
     paired = [swap(part) for part in own]
     return mix_reads(route, gates, norm_gain[None], own, paired)[None]
 

time: 130 us -> 102 us (0.78); the launches traced: 129 us -> 102 us
  local copies, waits for them, and re-layouts: 21.9 us -> 0.91 us
  waiting for transfers between devices: 36.1 us -> 19.9 us
  starting transfers between devices: 34.7 us -> 48.1 us
  Pallas kernels: 35.9 us -> 33.2 us
    unnamed x78 -> x18, local copies, waits for them, and re-layouts: 21.9 us -> 0.91 us
    ppermute x9 -> x18, starting transfers between devices: 9.22 us -> 25.6 us  [the longest x9 13.8 us: exchange(): out.append(lax.ppermute(arrays[shift], 'context', pairs))]
    all_to_all x2 -> x0, starting transfers between devices: 10.8 us -> none  [the longest x1 6.75 us: shards(): slices = lax.all_to_all(message, 'context', 0, 0, tiled=True)]
    ppermute x9 -> x18, waiting for transfers between devices: 25.2 us -> 16 us  [the longest x9 11.3 us: hop(): lax.ppermute(array, 'memory', [(i, i ^ shift) for i in range(OWNERS)])]
    ppermute x10, starting transfers between devices: 14.7 us -> 22.5 us  [swap(): return lax.ppermute(array, 'dp', [(0, 1), (1, 0)])]
    all_to_all x2 -> x0, waiting for transfers between devices: 5.19 us -> none  [the longest x1 5.19 us: shards(): slices = lax.all_to_all(message, 'context', 0, 0, tiled=True)]
    pallas_call x10 -> x12, Pallas kernels: 35.9 us -> 33.2 us  [kernel_call(): pl.pallas_call(kernel, out_shape=out_shape, in_specs=[pl.BlockSpec(memory...]
    ppermute x10, waiting for transfers between devices: 5.73 us -> 3.92 us  [swap(): return lax.ppermute(array, 'dp', [(0, 1), (1, 0)])]
  transfers between devices with their start and end apart: 21 -> 28, of which waited for: 11 -> 10; matrix products, arithmetic and copies ran while one was open for 0% -> 0% of each run, Pallas kernels for 18% -> 27%
where the time goes in v4:
time: 102 us
  starting transfers between devices  48.1 us (47%)
  Pallas kernels  33.2 us (33%)
  waiting for transfers between devices  19.9 us (20%)
    pallas_call x12, Pallas kernels, kernel_call(): pl.pallas_call(kernel, out_shape=out_shape, in_specs=[pl.BlockSpec(memory...  33.2 us
    ppermute x10, starting transfers between devices, swap(): return lax.ppermute(array, 'dp', [(0, 1), (1, 0)])  22.5 us
    ppermute x9, starting transfers between devices, exchange(): out.append(lax.ppermute(arrays[shift], 'context', pairs))  13.8 us
    ppermute x9, starting transfers between devices, hop(): lax.ppermute(array, 'memory', [(i, i ^ shift) for i in range(OWNERS)])  11.8 us
    ppermute x9, waiting for transfers between devices, hop(): lax.ppermute(array, 'memory', [(i, i ^ shift) for i in range(OWNERS)])  11.3 us
    ppermute x9, waiting for transfers between devices, exchange(): out.append(lax.ppermute(arrays[shift], 'context', pairs))  4.69 us
    ppermute x10, waiting for transfers between devices, swap(): return lax.ppermute(array, 'dp', [(0, 1), (1, 0)])  3.92 us
  transfers between devices with their start and end apart: 28, of which 10 were waited for; matrix products, arithmetic and copies ran while one was open for 0% of the time, Pallas kernels for 27%

profile of v4, /device:TPU:1, one launch (start us, length us, event | category | flops | bytes accessed | tf_op | source)
XLA Modules:
  0.0 102.3 jit_solution(13628999143992068822)
XLA Ops:
  0.0 2.3 %pack_rows.1 = (bf16[80,4096]{1,0:T(8,128)(2,1)S(1)}, bf16[80,4096]{1,0:T(8,128)(2,1)S(1)}, bf16[80,4224]{1,0:T(8,128)(2,1)S(1)}, bf16[80,4096]{1,0:T(8,128)(2,1)S(1)}) custom-call(s32[2,128]{1,0:T(2,128)} %bitcast.21, bf16[128,4096]{1,0:T(8,128)(2,1)} %bitcast.13), custom_call_target="tpu_custom_call" | custom-call | flops 1 | bytes 1 | tf_op jit(solution)/shard_map/pack_rows/pallas_call | solution.py:69
  3.8 3.9 %collective-permute-start.5 = (bf16[80,4096]{1,0:T(8,128)(2,1)S(1)}, bf16[80,4096]{1,0:T(8,128)(2,1)S(1)}, u32[]{:S(2)}, u32[]{:S(2)}) collective-permute-start(bf16[80,4096]{1,0:T(8,128)(2,1)S(1)} %get-tuple-element.62), channel_id=1, source_target_pairs={{0,96},{32,64},{64,32},{96,0},{1,97},{33,65},{65,33},{97,1},{2,98}... | collective-permute-start | bytes 1966088 | tf_op jit(solution)/shard_map/ppermute | solution.py:488
  9.1 8.8 %project_2.2 = (bf16[2,80,1024]{2,1,0:T(8,128)(2,1)S(1)}, bf16[2,80,1024]{2,1,0:T(8,128)(2,1)S(1)}, f32[2,80,128]{2,1,0:T(8,128)S(1)}, bf16[4096,1024]{1,0:T(8,128)(2,1)S(1)}, bf16[4096,1024]{1,0:T(8,128)(2,1)S(1)}) custom-call(bf16[80,4096]{1,0:T(8,128)(2,1)} %copy-done.1, bf16[80,4096]{1,0:T(8,128)(2,1)} %copy-done.8, bf16[4096,1024]{1,0:T(8,128)(2,1)} %bitcast.26, ...), custom_call_target="tpu_custom_call" | custom-call | flops 1 | bytes 1 | tf_op jit(solution)/shard_map/project_2/pallas_call | solution.py:69
  19.0 3.7 %collective-permute-done.5.refs_2_ = bf16[80,4096]{1,0:T(8,128)(2,1)S(1)} collective-permute-done((bf16[80,4096]{1,0:T(8,128)(2,1)S(1)}, bf16[80,4096]{1,0:T(8,128)(2,1)S(1)}, u32[]{:S(2)}, u32[]{:S(2)}) %collective-permute-start.5) | collective-permute-done | bytes 655392 | tf_op jit(solution)/shard_map/ppermute | solution.py:488
  24.9 1.7 %collective-permute-done.4.refs_1_ = bf16[80,4096]{1,0:T(8,128)(2,1)S(1)} collective-permute-done((bf16[80,4096]{1,0:T(8,128)(2,1)S(1)}, bf16[80,4096]{1,0:T(8,128)(2,1)S(1)}, u32[]{:S(2)}, u32[]{:S(2)}) %collective-permute-start.4) | collective-permute-done | bytes 655392 | tf_op jit(solution)/shard_map/ppermute | solution.py:500
  27.6 6.3 %project_4.1 = (bf16[4,80,1024]{2,1,0:T(8,128)(2,1)S(1)}, bf16[4,80,1024]{2,1,0:T(8,128)(2,1)S(1)}, f32[4,80,128]{2,1,0:T(8,128)S(1)}) custom-call(bf16[80,4096]{1,0:T(8,128)(2,1)S(1)} %collective-permute-done.3.refs_0_, bf16[80,4096]{1,0:T(8,128)(2,1)S(1)} %collective-permute-done.4.refs_1_, bf16[80,4096]{1,0:T(8,128)(2,1)S(1)} %collective-permute-done.5.refs_2_, ...), custom_call_target="tpu_custom_call" | custom-call | flops 1 | bytes 1 | tf_op jit(solution)/shard_map/project_4/pallas_call | solution.py:69
  33.9 6.7 %collective-permute-done.7.refs_0_ = bf16[80,4224]{1,0:T(8,128)(2,1)S(1)} collective-permute-done((bf16[80,4224]{1,0:T(8,128)(2,1)S(1)}, bf16[80,4224]{1,0:T(8,128)(2,1)S(1)}, u32[]{:S(2)}, u32[]{:S(2)}) %collective-permute-start.7) | collective-permute-done | bytes 675872 | tf_op jit(solution)/shard_map/ppermute | solution.py:488
  40.6 2.1 %collective-permute-start.8 = (bf16[80,4224]{1,0:T(8,128)(2,1)S(1)}, bf16[80,4224]{1,0:T(8,128)(2,1)S(1)}, u32[]{:S(2)}, u32[]{:S(2)}) collective-permute-start(bf16[80,4224]{1,0:T(8,128)(2,1)S(1)} %collective-permute-done.7.refs_0_), channel_id=1, source_target_pairs={{0,1},{1,0},{2,3},{3,2},{4,5},{5,4},{6,7},{7,6},{8,9},{9,8},{10,11... | collective-permute-start | bytes 2027528 | tf_op jit(solution)/shard_map/ppermute | solution.py:500
  43.0 2.4 %collective-permute-start.10 = (bf16[2,80,1024]{2,1,0:T(8,128)(2,1)S(1)}, bf16[2,80,1024]{2,1,0:T(8,128)(2,1)S(1)}, u32[]{:S(2)}, u32[]{:S(2)}) collective-permute-start(bf16[2,80,1024]{2,1,0:T(8,128)(2,1)S(1)} %get-tuple-element.84), channel_id=1, source_target_pairs={{0,64},{32,96},{64,0},{96,32},{1,65},{33,97},{65,1},{97,33},{2,66}... | collective-permute-start | bytes 983048 | tf_op jit(solution)/shard_map/ppermute | solution.py:488
  46.6 3.3 %project_2.3 = (bf16[2,80,1024]{2,1,0:T(8,128)(2,1)S(1)}, bf16[2,80,1024]{2,1,0:T(8,128)(2,1)S(1)}, f32[2,80,128]{2,1,0:T(8,128)S(1)}) custom-call(bf16[80,4224]{1,0:T(8,128)(2,1)S(1)} %collective-permute-done.7.refs_0_, bf16[80,4224]{1,0:T(8,128)(2,1)S(1)} %collective-permute-done.8.refs_1_, bf16[4096,1024]{1,0:T(8,128)(2,1)S(1)} %get-tuple-element.64.refs_4_.refs_2_, ...), custom_call_target="tpu_custom_call" | custom-call | flops 1 | bytes 1 | tf_op jit(solution)/shard_map/project_2/pallas_call | solution.py:69
  49.9 2.6 %block_state.1 = (bf16[288,128]{1,0:T(8,128)(2,1)S(1)}, bf16[288,128]{1,0:T(8,128)(2,1)S(1)}, bf16[288,128]{1,0:T(8,128)(2,1)S(1)}, bf16[288,128]{1,0:T(8,128)(2...) custom-call(bf16[2,80,1024]{2,1,0:T(8,128)(2,1)S(1)} %get-tuple-elem, ...), custom_call_target="tpu_custom_call" | custom-call | flops 1 | bytes 1 | tf_op jit(solution)/shard_map/block_state/pallas_call | solution.py:69
  54.0 2.6 %collective-permute-start.13 = (bf16[288,128]{1,0:T(8,128)(2,1)S(1)}, bf16[288,128]{1,0:T(8,128)(2,1)S(1)}, u32[]{:S(2)}, u32[]{:S(2)}) collective-permute-start(bf16[288,128]{1,0:T(8,128)(2,1)S(1)} %get-tuple-element.91), channel_id=1, source_target_pairs={{0,4},{2,6},{4,0},{6,2},{8,12},{10,14},{12,8},{14,10},{16,20},{18,... | collective-permute-start | bytes 221192 | tf_op jit(solution)/shard_map/ppermute | solution.py:495
  56.7 2.3 %collective-permute-start.14 = (bf16[288,128]{1,0:T(8,128)(2,1)S(1)}, bf16[288,128]{1,0:T(8,128)(2,1)S(1)}, u32[]{:S(2)}, u32[]{:S(2)}) collective-permute-start(bf16[288,128]{1,0:T(8,128)(2,1)S(1)} %get-tuple-element.92), channel_id=1, source_target_pairs={{0,6},{2,4},{4,2},{6,0},{8,14},{10,12},{12,10},{14,8},{16,22},{18,... | collective-permute-start | bytes 221192 | tf_op jit(solution)/shard_map/ppermute | solution.py:495
  59.7 2.1 %collective-permute-done.14.refs_3_ = bf16[288,128]{1,0:T(8,128)(2,1)S(1)} collective-permute-done((bf16[288,128]{1,0:T(8,128)(2,1)S(1)}, bf16[288,128]{1,0:T(8,128)(2,1)S(1)}, u32[]{:S(2)}, u32[]{:S(2)}) %collective-permute-start.14) | collective-permute-done | bytes 73760 | tf_op jit(solution)/shard_map/ppermute | solution.py:495
  62.0 2.6 %collective-permute-start.17 = (bf16[288,128]{1,0:T(8,128)(2,1)S(1)}, bf16[288,128]{1,0:T(8,128)(2,1)S(1)}, u32[]{:S(2)}, u32[]{:S(2)}) collective-permute-start(bf16[288,128]{1,0:T(8,128)(2,1)S(1)} %get-tuple-element.94.refs_0_), channel_id=1, source_target_pairs={{0,24},{2,26},{4,28},{6,30},{8,16},{10,18},{12,20},{14,22},{16,8},... | collective-permute-start | bytes 221192 | tf_op jit(solution)/shard_map/ppermute | solution.py:495
  65.3 2.8 %inner_reads_0.1 = (f32[8,80,512]{2,1,0:T(8,128)S(1)}, bf16[8,80,1024]{2,1,0:T(8,128)(2,1)S(1)}) custom-call(bf16[8,80,1024]{2,1,0:T(8,128)(2,1)S(1)} %get-tuple-element.76.refs_0_, bf16[8,80,1024]{2,1,0:T(8,128)(2,1)S(1)} %get-tuple-element.77.refs_1_, f32[640,128]{1,0:T(8,128)S(1)} %get-tuple-element.78.refs_2_.refs_3_, ...), custom_call_target="tpu_custom_call" | custom-call | flops 1 | bytes 1 | tf_op jit(solution)/shard_map/inner_reads_0/pallas_call | solution.py:69
  69.6 2.9 %collective-permute-start.19 = (bf16[256,128]{1,0:T(8,128)(2,1)S(1)}, bf16[256,128]{1,0:T(8,128)(2,1)S(1)}, u32[]{:S(2)}, u32[]{:S(2)}) collective-permute-start(bf16[256,128]{1,0:T(8,128)(2,1)S(1)} %get-tuple-element.99), channel_id=1, source_target_pairs={{0,4},{2,6},{4,0},{6,2},{8,12},{10,14},{12,8},{14,10},{16,20},{18,... | collective-permute-start | bytes 196616 | tf_op jit(solution)/shard_map/ppermute | solution.py:495
  73.4 2.8 %inner_reads_4.1.refs_2_ = f32[8,80,512]{2,1,0:T(8,128)S(1)} custom-call(bf16[8,80,1024]{2,1,0:T(8,128)(2,1)S(1)} %get-tuple-element.76.refs_0_, bf16[8,80,1024]{2,1,0:T(8,128)(2,1)S(1)} %get-tuple-element.77.refs_1_, f32[640,128]{1,0:T(8,128)S(1)} %get-tuple-element.78.refs_2_.refs_3_, f32[8,640]{1,0:T(8,128)S(1)} %get-tuple-element.79.refs_3_, ...), custom_call_target="tpu_custom_call" | custom-call | flops 1 | bytes 1 | tf_op jit(solution)/shard_map/inner_reads_4/pallas_call | solution.py:69
  78.0 2.7 %collective-permute-start.22 = (bf16[2,80,1024]{2,1,0:T(8,128)(2,1)S(1)}, bf16[2,80,1024]{2,1,0:T(8,128)(2,1)S(1)}, u32[]{:S(2)}, u32[]{:S(2)}) collective-permute-start(bf16[2,80,1024]{2,1,0:T(8,128)(2,1)S(1)} %get-tuple-element.103), channel_id=1, source_target_pairs={{0,64},{32,96},{64,0},{96,32},{1,65},{33,97},{65,1},{97,33},{2,66}... | collective-permute-start | bytes 983048 | tf_op jit(solution)/shard_map/ppermute | solution.py:488
  81.9 6.8 %collective-permute-start.24 = (bf16[2,80,1024]{2,1,0:T(8,128)(2,1)S(1)}, bf16[2,80,1024]{2,1,0:T(8,128)(2,1)S(1)}, u32[]{:S(2)}, u32[]{:S(2)}) collective-permute-start(bf16[2,80,1024]{2,1,0:T(8,128)(2,1)S(1)} %get-tuple-element.101.refs_0_), channel_id=1, source_target_pairs={{0,1},{1,0},{2,3},{3,2},{4,5},{5,4},{6,7},{7,6},{8,9},{9,8},{10,11... | collective-permute-start | bytes 983048 | tf_op jit(solution)/shard_map/ppermute | solution.py:500
  88.7 3.0 %collective-permute-start.25 = (bf16[2,80,1024]{2,1,0:T(8,128)(2,1)S(1)}, bf16[2,80,1024]{2,1,0:T(8,128)(2,1)S(1)}, u32[]{:S(2)}, u32[]{:S(2)}) collective-permute-start(bf16[2,80,1024]{2,1,0:T(8,128)(2,1)S(1)} %collective-permute-done.21.refs_1_), channel_id=1, source_target_pairs={{0,1},{1,0},{2,3},{3,2},{4,5},{5,4},{6,7},{7,6},{8,9},{9,8},{10,11... | collective-permute-start | bytes 983048 | tf_op jit(solution)/shard_map/ppermute | solution.py:500
  91.7 4.9 %collective-permute-start.26 = (bf16[2,80,1024]{2,1,0:T(8,128)(2,1)S(1)}, bf16[2,80,1024]{2,1,0:T(8,128)(2,1)S(1)}, u32[]{:S(2)}, u32[]{:S(2)}) collective-permute-start(bf16[2,80,1024]{2,1,0:T(8,128)(2,1)S(1)} %collective-permute-done.22.refs_2_), channel_id=1, source_target_pairs={{0,1},{1,0},{2,3},{3,2},{4,5},{5,4},{6,7},{7,6},{8,9},{9,8},{10,11... | collective-permute-start | bytes 983048 | tf_op jit(solution)/shard_map/ppermute | solution.py:500
  96.6 2.5 %collective-permute-start.27 = (bf16[2,80,1024]{2,1,0:T(8,128)(2,1)S(1)}, bf16[2,80,1024]{2,1,0:T(8,128)(2,1)S(1)}, u32[]{:S(2)}, u32[]{:S(2)}) collective-permute-start(bf16[2,80,1024]{2,1,0:T(8,128)(2,1)S(1)} %collective-permute-done.23.refs_3_), channel_id=1, source_target_pairs={{0,1},{1,0},{2,3},{3,2},{4,5},{5,4},{6,7},{7,6},{8,9},{9,8},{10,11... | collective-permute-start | bytes 983048 | tf_op jit(solution)/shard_map/ppermute | solution.py:500
  100.4 2.0 %mix_reads.1 = bf16[128,2048]{1,0:T(8,128)(2,1)} custom-call(s32[2,128]{1,0:T(2,128)S(1)} %bitcast.24, f32[128,128]{1,0:T(8,128)S(1)} %get-tuple-element.58.gates_ref, f32[1,2048]{1,0:T(1,128)S(1)} %bitcast.25, bf16[2,80,1024]{2,1,0:T(8,128)(2,1)S(1)} %get-tuple-element.101.refs_0_, bf16[2,80,1024]{2,1,0:T(8,128)(2,1)S(1)} %collective-permute-done.21.refs_1_, ...), custom_call_target="tpu_custom_call" | custom-call | flops 1 | bytes 1 | tf_op jit(solution)/shard_map/mix_reads/pallas_call | solution.py:69
  (62 shorter events, 18.3 us)
Async XLA Ops:
  2.3 5.9 %collective-permute-start = (bf16[80,4096]{1,0:T(8,128)(2,1)S(1)}, bf16[80,4096]{1,0:T(8,128)(2,1)S(1)}, u32[]{:S(2)}, u32[]{:S(2)}) collective-permute-start(bf16[80,4096]{1,0:T(8,128)(2,1)S(1)} %get-tuple-element.55.refs_0_), channel_id=1, source_target_pairs={{0,1},{1,0},{2,3},{3,2},{4,5},{5,4},{6,7},{7,6},{8,9},{9,8},{10,11... | collective-permute-start | bytes 1966088 | tf_op jit(solution)/shard_map/ppermute | solution.py:500
  3.8 18.9 %collective-permute-start.5 = (bf16[80,4096]{1,0:T(8,128)(2,1)S(1)}, bf16[80,4096]{1,0:T(8,128)(2,1)S(1)}, u32[]{:S(2)}, u32[]{:S(2)}) collective-permute-start(bf16[80,4096]{1,0:T(8,128)(2,1)S(1)} %get-tuple-element.62), channel_id=1, source_target_pairs={{0,96},{32,64},{64,32},{96,0},{1,97},{33,65},{65,33},{97,1},{2,98}... | collective-permute-start | bytes 1966088 | tf_op jit(solution)/shard_map/ppermute | solution.py:488
  7.7 16.0 %collective-permute-start.3 = (bf16[80,4096]{1,0:T(8,128)(2,1)S(1)}, bf16[80,4096]{1,0:T(8,128)(2,1)S(1)}, u32[]{:S(2)}, u32[]{:S(2)}) collective-permute-start(bf16[80,4096]{1,0:T(8,128)(2,1)S(1)} %get-tuple-element.60), channel_id=1, source_target_pairs={{0,32},{32,0},{64,96},{96,64},{1,33},{33,1},{65,97},{97,65},{2,34}... | collective-permute-start | bytes 1966088 | tf_op jit(solution)/shard_map/ppermute | solution.py:488
  7.7 10.3 %collective-permute-start.2 = (bf16[128,2048]{1,0:T(8,128)(2,1)}, bf16[128,2048]{1,0:T(8,128)(2,1)S(1)}, u32[]{:S(2)}, u32[]{:S(2)}) collective-permute-start(bf16[128,2048]{1,0:T(8,128)(2,1)} %bitcast.18), channel_id=1, source_target_pairs={{0,1},{1,0},{2,3},{3,2},{4,5},{5,4},{6,7},{7,6},{8,9},{9,8},{10,11... | collective-permute-start | bytes 1572872 | tf_op jit(solution)/shard_map/ppermute | solution.py:500
  8.0 9.9 %collective-permute-start.1 = (s32[2,128]{1,0:T(2,128)}, s32[2,128]{1,0:T(2,128)S(1)}, u32[]{:S(2)}, u32[]{:S(2)}) collective-permute-start(s32[2,128]{1,0:T(2,128)} %bitcast.22), channel_id=1, source_target_pairs={{0,1},{1,0},{2,3},{3,2},{4,5},{5,4},{6,7},{7,6},{8,9},{9,8},{10,11... | collective-permute-start | bytes 3080 | tf_op jit(solution)/shard_map/ppermute | solution.py:500
  23.6 17.0 %collective-permute-start.7 = (bf16[80,4224]{1,0:T(8,128)(2,1)S(1)}, bf16[80,4224]{1,0:T(8,128)(2,1)S(1)}, u32[]{:S(2)}, u32[]{:S(2)}) collective-permute-start(bf16[80,4224]{1,0:T(8,128)(2,1)S(1)} %get-tuple-element.68), channel_id=1, source_target_pairs={{0,64},{32,96},{64,0},{96,32},{1,65},{33,97},{65,1},{97,33},{2,66}... | collective-permute-start | bytes 2027528 | tf_op jit(solution)/shard_map/ppermute | solution.py:488
  40.6 6.0 %collective-permute-start.8 = (bf16[80,4224]{1,0:T(8,128)(2,1)S(1)}, bf16[80,4224]{1,0:T(8,128)(2,1)S(1)}, u32[]{:S(2)}, u32[]{:S(2)}) collective-permute-start(bf16[80,4224]{1,0:T(8,128)(2,1)S(1)} %collective-permute-done.7.refs_0_), channel_id=1, source_target_pairs={{0,1},{1,0},{2,3},{3,2},{4,5},{5,4},{6,7},{7,6},{8,9},{9,8},{10,11... | collective-permute-start | bytes 2027528 | tf_op jit(solution)/shard_map/ppermute | solution.py:500
  42.7 22.3 %collective-permute-start.9 = (bf16[2,80,1024]{2,1,0:T(8,128)(2,1)S(1)}, bf16[2,80,1024]{2,1,0:T(8,128)(2,1)S(1)}, u32[]{:S(2)}, u32[]{:S(2)}) collective-permute-start(bf16[2,80,1024]{2,1,0:T(8,128)(2,1)S(1)} %get-tuple-element.82), channel_id=1, source_target_pairs={{0,32},{32,0},{64,96},{96,64},{1,33},{33,1},{65,97},{97,65},{2,34}... | collective-permute-start | bytes 983048 | tf_op jit(solution)/shard_map/ppermute | solution.py:488
  43.0 22.3 %collective-permute-start.10 = (bf16[2,80,1024]{2,1,0:T(8,128)(2,1)S(1)}, bf16[2,80,1024]{2,1,0:T(8,128)(2,1)S(1)}, u32[]{:S(2)}, u32[]{:S(2)}) collective-permute-start(bf16[2,80,1024]{2,1,0:T(8,128)(2,1)S(1)} %get-tuple-element.84), channel_id=1, source_target_pairs={{0,64},{32,96},{64,0},{96,32},{1,65},{33,97},{65,1},{97,33},{2,66}... | collective-permute-start | bytes 983048 | tf_op jit(solution)/shard_map/ppermute | solution.py:488
  45.4 19.9 %collective-permute-start.11 = (bf16[2,80,1024]{2,1,0:T(8,128)(2,1)S(1)}, bf16[2,80,1024]{2,1,0:T(8,128)(2,1)S(1)}, u32[]{:S(2)}, u32[]{:S(2)}) collective-permute-start(bf16[2,80,1024]{2,1,0:T(8,128)(2,1)S(1)} %get-tuple-element.86), channel_id=1, source_target_pairs={{0,96},{32,64},{64,32},{96,0},{1,97},{33,65},{65,33},{97,1},{2,98}... | collective-permute-start | bytes 983048 | tf_op jit(solution)/shard_map/ppermute | solution.py:488
  54.0 5.7 %collective-permute-start.13 = (bf16[288,128]{1,0:T(8,128)(2,1)S(1)}, bf16[288,128]{1,0:T(8,128)(2,1)S(1)}, u32[]{:S(2)}, u32[]{:S(2)}) collective-permute-start(bf16[288,128]{1,0:T(8,128)(2,1)S(1)} %get-tuple-element.91), channel_id=1, source_target_pairs={{0,4},{2,6},{4,0},{6,2},{8,12},{10,14},{12,8},{14,10},{16,20},{18,... | collective-permute-start | bytes 221192 | tf_op jit(solution)/shard_map/ppermute | solution.py:495
  56.7 5.2 %collective-permute-start.14 = (bf16[288,128]{1,0:T(8,128)(2,1)S(1)}, bf16[288,128]{1,0:T(8,128)(2,1)S(1)}, u32[]{:S(2)}, u32[]{:S(2)}) collective-permute-start(bf16[288,128]{1,0:T(8,128)(2,1)S(1)} %get-tuple-element.92), channel_id=1, source_target_pairs={{0,6},{2,4},{4,2},{6,0},{8,14},{10,12},{12,10},{14,8},{16,22},{18,... | collective-permute-start | bytes 221192 | tf_op jit(solution)/shard_map/ppermute | solution.py:495
  62.0 6.2 %collective-permute-start.17 = (bf16[288,128]{1,0:T(8,128)(2,1)S(1)}, bf16[288,128]{1,0:T(8,128)(2,1)S(1)}, u32[]{:S(2)}, u32[]{:S(2)}) collective-permute-start(bf16[288,128]{1,0:T(8,128)(2,1)S(1)} %get-tuple-element.94.refs_0_), channel_id=1, source_target_pairs={{0,24},{2,26},{4,28},{6,30},{8,16},{10,18},{12,20},{14,22},{16,8},... | collective-permute-start | bytes 221192 | tf_op jit(solution)/shard_map/ppermute | solution.py:495
  64.5 4.8 %collective-permute-start.16 = (bf16[288,128]{1,0:T(8,128)(2,1)S(1)}, bf16[288,128]{1,0:T(8,128)(2,1)S(1)}, u32[]{:S(2)}, u32[]{:S(2)}) collective-permute-start(bf16[288,128]{1,0:T(8,128)(2,1)S(1)} %get-tuple-element.94.refs_0_), channel_id=1, source_target_pairs={{0,16},{2,18},{4,20},{6,22},{8,24},{10,26},{12,28},{14,30},{16,0},... | collective-permute-start | bytes 221192 | tf_op jit(solution)/shard_map/ppermute | solution.py:495
  65.1 4.3 %collective-permute-start.15 = (bf16[288,128]{1,0:T(8,128)(2,1)S(1)}, bf16[288,128]{1,0:T(8,128)(2,1)S(1)}, u32[]{:S(2)}, u32[]{:S(2)}) collective-permute-start(bf16[288,128]{1,0:T(8,128)(2,1)S(1)} %get-tuple-element.94.refs_0_), channel_id=1, source_target_pairs={{0,8},{2,10},{4,12},{6,14},{8,0},{10,2},{12,4},{14,6},{16,24},{18,... | collective-permute-start | bytes 221192 | tf_op jit(solution)/shard_map/ppermute | solution.py:495
  69.5 6.7 %collective-permute-start.18 = (bf16[256,128]{1,0:T(8,128)(2,1)S(1)}, bf16[256,128]{1,0:T(8,128)(2,1)S(1)}, u32[]{:S(2)}, u32[]{:S(2)}) collective-permute-start(bf16[256,128]{1,0:T(8,128)(2,1)S(1)} %get-tuple-element.98), channel_id=1, source_target_pairs={{0,2},{2,0},{4,6},{6,4},{8,10},{10,8},{12,14},{14,12},{16,18},{18,... | collective-permute-start | bytes 196616 | tf_op jit(solution)/shard_map/ppermute | solution.py:495
  69.6 6.6 %collective-permute-start.19 = (bf16[256,128]{1,0:T(8,128)(2,1)S(1)}, bf16[256,128]{1,0:T(8,128)(2,1)S(1)}, u32[]{:S(2)}, u32[]{:S(2)}) collective-permute-start(bf16[256,128]{1,0:T(8,128)(2,1)S(1)} %get-tuple-element.99), channel_id=1, source_target_pairs={{0,4},{2,6},{4,0},{6,2},{8,12},{10,14},{12,8},{14,10},{16,20},{18,... | collective-permute-start | bytes 196616 | tf_op jit(solution)/shard_map/ppermute | solution.py:495
  72.5 4.3 %collective-permute-start.20 = (bf16[256,128]{1,0:T(8,128)(2,1)S(1)}, bf16[256,128]{1,0:T(8,128)(2,1)S(1)}, u32[]{:S(2)}, u32[]{:S(2)}) collective-permute-start(bf16[256,128]{1,0:T(8,128)(2,1)S(1)} %get-tuple-element.100), channel_id=1, source_target_pairs={{0,6},{2,4},{4,2},{6,0},{8,14},{10,12},{12,10},{14,8},{16,22},{18,... | collective-permute-start | bytes 196616 | tf_op jit(solution)/shard_map/ppermute | solution.py:495
  77.9 10.7 %collective-permute-start.21 = (bf16[2,80,1024]{2,1,0:T(8,128)(2,1)S(1)}, bf16[2,80,1024]{2,1,0:T(8,128)(2,1)S(1)}, u32[]{:S(2)}, u32[]{:S(2)}) collective-permute-start(bf16[2,80,1024]{2,1,0:T(8,128)(2,1)S(1)} %get-tuple-element.102), channel_id=1, source_target_pairs={{0,32},{32,0},{64,96},{96,64},{1,33},{33,1},{65,97},{97,65},{2,34}... | collective-permute-start | bytes 983048 | tf_op jit(solution)/shard_map/ppermute | solution.py:488
  78.0 13.7 %collective-permute-start.22 = (bf16[2,80,1024]{2,1,0:T(8,128)(2,1)S(1)}, bf16[2,80,1024]{2,1,0:T(8,128)(2,1)S(1)}, u32[]{:S(2)}, u32[]{:S(2)}) collective-permute-start(bf16[2,80,1024]{2,1,0:T(8,128)(2,1)S(1)} %get-tuple-element.103), channel_id=1, source_target_pairs={{0,64},{32,96},{64,0},{96,32},{1,65},{33,97},{65,1},{97,33},{2,66}... | collective-permute-start | bytes 983048 | tf_op jit(solution)/shard_map/ppermute | solution.py:488
  80.7 15.8 %collective-permute-start.23 = (bf16[2,80,1024]{2,1,0:T(8,128)(2,1)S(1)}, bf16[2,80,1024]{2,1,0:T(8,128)(2,1)S(1)}, u32[]{:S(2)}, u32[]{:S(2)}) collective-permute-start(bf16[2,80,1024]{2,1,0:T(8,128)(2,1)S(1)} %get-tuple-element.104), channel_id=1, source_target_pairs={{0,96},{32,64},{64,32},{96,0},{1,97},{33,65},{65,33},{97,1},{2,98}... | collective-permute-start | bytes 983048 | tf_op jit(solution)/shard_map/ppermute | solution.py:488
  81.9 17.2 %collective-permute-start.24 = (bf16[2,80,1024]{2,1,0:T(8,128)(2,1)S(1)}, bf16[2,80,1024]{2,1,0:T(8,128)(2,1)S(1)}, u32[]{:S(2)}, u32[]{:S(2)}) collective-permute-start(bf16[2,80,1024]{2,1,0:T(8,128)(2,1)S(1)} %get-tuple-element.101.refs_0_), channel_id=1, source_target_pairs={{0,1},{1,0},{2,3},{3,2},{4,5},{5,4},{6,7},{7,6},{8,9},{9,8},{10,11... | collective-permute-start | bytes 983048 | tf_op jit(solution)/shard_map/ppermute | solution.py:500
  88.7 10.5 %collective-permute-start.25 = (bf16[2,80,1024]{2,1,0:T(8,128)(2,1)S(1)}, bf16[2,80,1024]{2,1,0:T(8,128)(2,1)S(1)}, u32[]{:S(2)}, u32[]{:S(2)}) collective-permute-start(bf16[2,80,1024]{2,1,0:T(8,128)(2,1)S(1)} %collective-permute-done.21.refs_1_), channel_id=1, source_target_pairs={{0,1},{1,0},{2,3},{3,2},{4,5},{5,4},{6,7},{7,6},{8,9},{9,8},{10,11... | collective-permute-start | bytes 983048 | tf_op jit(solution)/shard_map/ppermute | solution.py:500
  91.7 7.4 %collective-permute-start.26 = (bf16[2,80,1024]{2,1,0:T(8,128)(2,1)S(1)}, bf16[2,80,1024]{2,1,0:T(8,128)(2,1)S(1)}, u32[]{:S(2)}, u32[]{:S(2)}) collective-permute-start(bf16[2,80,1024]{2,1,0:T(8,128)(2,1)S(1)} %collective-permute-done.22.refs_2_), channel_id=1, source_target_pairs={{0,1},{1,0},{2,3},{3,2},{4,5},{5,4},{6,7},{7,6},{8,9},{9,8},{10,11... | collective-permute-start | bytes 983048 | tf_op jit(solution)/shard_map/ppermute | solution.py:500
  (13 other events, 98.8 us)

commit v5 on v4

--- a/solution.py
+++ b/solution.py
@@ -19,6 +19,7 @@
 EMPTY = 64.0
 PAD = 128
 PACKS = 4
+NEAR, FAR = (0, 1, 3), 2
 RING = 4
 PIECE = HALF // RING
 TAIL = 16
@@ -125,7 +126,7 @@
     route_ref, other_route_ref, query_ref, other_query_ref, rows_ref, router_ref, *out_refs
 ):
     owner, core = lax.axis_index("memory"), lax.axis_index("dp")
-    gates_ref = out_refs[OWNERS]
+    gates_ref, picks_ref = out_refs[OWNERS:]
     mine = pl.multiple_of(core * HALF, HALF)
     for side, (routes, queries) in enumerate(
         ((route_ref, query_ref), (other_route_ref, other_query_ref))
@@ -138,17 +139,23 @@
         for shift in range(OWNERS):
             out_refs[shift][core ^ side] = part[shift * CAP : (shift + 1) * CAP]
         if side == 0:
+            for shift in range(OWNERS):
+                picks_ref[shift] = one_hot(place, owner ^ shift, 128).T.astype(BF16)
             score = dot_rows(router_ref[...], rows_ref[...])
             chosen = jax.nn.sigmoid(score) * named[:OWNERS]
             gates = chosen / jnp.sum(chosen, axis=0, keepdims=True)
-            gates_ref[...] = jnp.concatenate(
-                [gates, jnp.zeros((128 - OWNERS, ROWS), F32)], axis=0
-            ).T
+            memory = iota((OWNERS, ROWS), 0)
+            by_shift = [
+                jnp.sum(jnp.where(memory == owner ^ shift, gates, 0.0), axis=0, keepdims=True)
+                for shift in range(OWNERS)
+            ]
+            by_shift.append(jnp.zeros((128 - OWNERS, ROWS), F32))
+            gates_ref[...] = jnp.concatenate(by_shift, axis=0).T
 
 
 def pack_queries(route, other_route, queries, other_queries, rows, router_weight):
     out = [near((2, CAP, HALF), BF16)] * OWNERS
-    out = out + [near((ROWS, 128), F32)]
+    out = out + [near((ROWS, 128), F32), near((OWNERS, ROWS, 128), BF16)]
     operands = (route, other_route, queries, other_queries, rows, router_weight)
     return kernel_call(
         pack_queries_kernel, "pack_queries", out, (), 12, *operands, moved=4 * MIB
@@ -288,7 +295,7 @@
         reach *= 2
     row_out[...] = total
     running = jnp.concatenate([total, jnp.zeros((128 - HEADS, SLOTS), F32)], axis=0).T
-    column_out[...] = running
+    column_out[...] = running.reshape(CHUNKS, CAP, 128)
     token_order(unit_refs, units)
     token_order(value_refs, values)
     last = running[SLOTS - 1 : SLOTS]
@@ -309,7 +316,7 @@
 
 def block_state(units, values, decays):
     out = [near((PIECE + 2 * TAIL, 128), BF16)] * RING + [
-        near((SLOTS, 128), F32),
+        near((CHUNKS, CAP, 128), F32),
         near((HEADS, SLOTS), F32),
         near((CHUNKS, CAP, HALF), BF16),
         near((CHUNKS, CAP, HALF), BF16),
@@ -384,88 +391,84 @@
     return kernel_call(entry_kernel, "entry_states", out, scratch, 8, *pieces, before, faded)
 
 
-def order_queries(query_refs, held):
+def inner_kernel(shifts, *refs):
+    units, values, column_ref, row_ref = refs[0:4]
+    query_refs, inner = refs[4:-1], refs[-1]
     owner = lax.axis_index("memory")
-    for shift in range(OWNERS):
-        for core in range(2):
-            held[core * OWNERS + (owner ^ shift)] = query_refs[shift][core]
-
-
-def inner_kernel(start, *refs):
-    units, values, column_ref, row_ref = refs[0:4]
-    if start == 0:
-        inner, queries = refs[8:10]
-        order_queries(refs[4:8], queries)
-    else:
-        queries, inner = refs[4:6]
-    tile = 2 * CAP
-    for head in range(start, start + HEADS // 2):
-        columns = head_columns(head)
-        running = column_ref[:, head : head + 1]
-        running_row = row_ref[head : head + 1]
-        unit = units[:, :, columns].reshape(SLOTS, HEAD_DIM)
-        value = values[:, :, columns].reshape(SLOTS, HEAD_DIM)
-        for block in range(SLOTS // tile):
-            reach = -(-((block + 1) * tile) // 128) * 128
-            query = queries[2 * block : 2 * block + 2, :, columns].reshape(tile, HEAD_DIM)
-            score = dot_rows(query, unit[:reach])
-            spread = running[block * tile : (block + 1) * tile] - running_row[:, :reach]
-            causal = iota((tile, reach), 0) + block * tile >= iota((tile, reach), 1)
-            score = (score * jnp.exp(jnp.where(causal, spread, -1e30))).astype(BF16)
-            result = dot(score, value[:reach])
-            inner[2 * block : 2 * block + 2, :, head_columns(head - start)] = result.reshape(2, CAP, HEAD_DIM)
-
-
-def inner_reads(start, units, values, column, row, *queries):
-    out = [near((CHUNKS, CAP, HALF // 2), F32)]
-    if start == 0:
-        out = out + [near((CHUNKS, CAP, HALF), BF16)]
-    kernel = functools.partial(inner_kernel, start)
-    operands = (units, values, column, row, *queries)
-    return kernel_call(kernel, f"inner_reads_{start}", out, (), 16, *operands)
+    count = len(shifts) * CAP
+    for core in range(2):
+        reach = -(-(core + 1) * OWNERS * CAP // 128) * 128
+        chunks = [core * OWNERS + (owner ^ shift) for shift in shifts]
+        running = jnp.concatenate([column_ref[chunk] for chunk in chunks], axis=0)
+        place = jnp.concatenate([iota((CAP, reach), 0) + chunk * CAP for chunk in chunks], axis=0)
+        causal = place >= iota((count, reach), 1)
+        for head in range(HEADS):
+            columns = head_columns(head)
+            query = jnp.concatenate([query[core, :, columns] for query in query_refs], axis=0)
+            unit = units[:, :, columns].reshape(SLOTS, HEAD_DIM)[:reach]
+            value = values[:, :, columns].reshape(SLOTS, HEAD_DIM)[:reach]
+            spread = running[:, head : head + 1] - row_ref[head : head + 1, :reach]
+            weight = jnp.exp(jnp.where(causal, spread, -1e30))
+            score = (dot_rows(query, unit) * weight).astype(BF16)
+            inner[:, core, :, columns] = dot(score, value).reshape(len(shifts), CAP, HEAD_DIM)
+
+
+def inner_reads(shifts, units, values, column, row, *queries):
+    out = near((len(shifts), 2, CAP, HALF), F32)
+    kernel = functools.partial(inner_kernel, shifts)
+    name = f"inner_reads_{len(shifts)}"
+    return kernel_call(kernel, name, out, (), 16, units, values, column, row, *queries)
 
 
 def read_kernel(*refs):
-    queries, inners, column_ref = refs[0], refs[1:3], refs[3]
-    out_refs, (reads, entries) = refs[8:12], refs[12:]
-    ring_order(refs[4:8], entries, place_in_context()[1])
+    query_refs, inner_near, inner_far, column_ref = refs[0:4], refs[4], refs[5], refs[6]
+    out_refs, entries = refs[11:15], refs[15]
+    ring_order(refs[7:11], entries, place_in_context()[1])
     owner = lax.axis_index("memory")
-    fade = jnp.exp(column_ref[...])
+    inners = {shift: inner_near.at[at] for at, shift in enumerate(NEAR)}
+    inners[FAR] = inner_far.at[0]
+    pairs = [(shift, core) for shift in range(OWNERS) for core in range(2)]
+    fade = jnp.concatenate([column_ref[c * OWNERS + (owner ^ s)] for s, c in pairs], axis=0)
+    fade = jnp.exp(fade)
     for head in range(HEADS):
         columns = head_columns(head)
-        carried = dot(queries[:, :, columns].reshape(SLOTS, HEAD_DIM), entries[head // 2, head % 2 * HEAD_DIM : (head % 2 + 1) * HEAD_DIM])
-        inner = inners[head // 4][:, :, head_columns(head % 4)]
-        result = inner.reshape(SLOTS, HEAD_DIM) + fade[:, head : head + 1] * carried
-        reads[:, :, columns] = result.astype(BF16).reshape(CHUNKS, CAP, HEAD_DIM)
-    for shift in range(OWNERS):
-        for core in range(2):
-            out_refs[shift][core] = reads[core * OWNERS + (owner ^ shift)]
-
-
-def read_out(queries, inners, column, entry):
+        query = jnp.concatenate([query_refs[s][c, :, columns] for s, c in pairs], axis=0)
+        entry = entries[head // 2, head % 2 * HEAD_DIM : (head % 2 + 1) * HEAD_DIM]
+        carried = fade[:, head : head + 1] * dot(query, entry)
+        for at, (s, c) in enumerate(pairs):
+            read = inners[s][c, :, columns] + carried[at * CAP : (at + 1) * CAP]
+            out_refs[s][c, :, columns] = read.astype(BF16)
+
+
+def read_out(queries, inner_near, inner_far, column, entry):
     out = [near((2, CAP, HALF), BF16)] * OWNERS
-    scratch = [pltpu.VMEM((CHUNKS, CAP, HALF), BF16), pltpu.VMEM((RING, PIECE, 128), BF16)]
-    return kernel_call(
-        read_kernel, "read_out", out, scratch, 12, queries, *inners, column, *entry
-    )
-
-
-def mix_kernel(route_ref, gates_ref, gain_ref, *refs):
-    own_refs, other_refs, out_ref = refs[0:4], refs[4:8], refs[8]
-    owner, core = lax.axis_index("memory"), lax.axis_index("dp")
-    place = membership(route_ref[...])[1]
-    picks, gates = [], []
-    lane = iota((ROWS, 128), 1)
-    for shift in range(OWNERS):
-        memory = owner ^ shift
-        picks.append(one_hot(place, memory, 128).T.astype(BF16)[:, :CAP])
-        gate = jnp.where(lane == memory, gates_ref[...], 0.0)
-        gates.append(jnp.sum(gate, axis=1, keepdims=True))
-    for side, reads in enumerate((own_refs, other_refs)):
+    scratch = [pltpu.VMEM((RING, PIECE, 128), BF16)]
+    operands = (*queries, inner_near, inner_far, column, *entry)
+    return kernel_call(read_kernel, "read_out", out, scratch, 12, *operands)
+
+
+def mix_near_kernel(gates_ref, picks_ref, *refs):
+    partial = refs[-1]
+    core = lax.axis_index("dp")
+    for side in range(2):
+        total = jnp.zeros((ROWS, HALF), F32)
+        for at, shift in enumerate(NEAR):
+            reads = refs[side * len(NEAR) + at][core]
+            total = total + gates_ref[:, shift : shift + 1] * dot(picks_ref[shift, :, :CAP], reads)
+        partial[side] = total
+
+
+def mix_near(gates, picks, own, other):
+    out = near((2, ROWS, HALF), F32)
+    return kernel_call(mix_near_kernel, "mix_near", out, (), 12, gates, picks, *own, *other)
+
+
+def mix_kernel(gates_ref, picks_ref, gain_ref, partial, own, other, out_ref):
+    core = lax.axis_index("dp")
+    for side, reads in enumerate((own, other)):
         start = (core ^ side) * HALF
-        mixture = jnp.zeros((ROWS, HALF), F32)
-        for shift in range(OWNERS):
-            mixture = mixture + gates[shift] * dot(picks[shift], reads[shift][core])
+        far = dot(picks_ref[FAR, :, :CAP], reads[core])
+        mixture = partial[side] + gates_ref[:, FAR : FAR + 1] * far
         for head in range(HEADS):
             columns = pl.ds(pl.multiple_of(start + head * HEAD_DIM, HEAD_DIM), HEAD_DIM)
             mix = mixture[:, head_columns(head)]
@@ -473,10 +476,10 @@
             out_ref[:, columns] = (mix * scale * gain_ref[:, columns]).astype(BF16)
 
 
-def mix_reads(route, gates, gain, own, other):
+def mix_reads(gates, picks, gain, partial, own, other):
     out = jax.ShapeDtypeStruct((ROWS, 2 * HALF), BF16)
     return kernel_call(
-        mix_kernel, "mix_reads", out, (), 12, route, gates, gain, *own, *other
+        mix_kernel, "mix_reads", out, (), 12, gates, picks, gain, partial, own, other
     )
 
 
@@ -525,7 +528,7 @@
     packed_query = pack_queries(
         after(route, first[2]), other_route, query_rows, other_query, rows, router_weight.T
     )
-    gates = packed_query[OWNERS]
+    gates, picks = packed_query[OWNERS:]
     for shift in (1, 3):
         arrived[shift] = after(arrived[shift], gates)
     arrived[2] = hop(after(packed[2], arrived[1], arrived[3]), 2)
@@ -534,23 +537,29 @@
     second = project([arrived[1], other[1], arrived[3], other[3]], *weights)
     arrived[2] = after(arrived[2], second[2])
     other[2] = swap(arrived[2])
+    query_in = {0: packed_query[0]}
+    for shift in (1, 3):
+        query_in[shift] = hop(after(packed_query[shift], arrived[2]), shift)
     third = project([arrived[2], other[2]], *weights)
     units, values, decays = zip(first[:3], second, third)
 
     *messages, column, row, units, values = block_state(units, values, decays)
-    query_in = [packed_query[0]]
-    query_in += [hop(after(packed_query[shift], second[2]), shift) for shift in (1, 2, 3)]
-    whole, before, faded = row_prefix(exchange(messages, 1))
+    pieces = exchange(messages, 1)
+    blocks = (units, values, column, row)
+    inner_near = inner_reads(NEAR, *blocks, *[query_in[shift] for shift in NEAR])
+    pieces[0] = after(pieces[0], inner_near)
+    whole, before, faded = row_prefix(pieces)
+    query_in[FAR] = hop(after(packed_query[FAR], whole), FAR)
     totals = exchange([whole] * RING, RING)
-    inner_low, ordered = inner_reads(0, units, values, column, row, *query_in)
-    totals[0] = after(totals[0], inner_low)
     entry = exchange(entry_states(totals, before, faded), 1)
-    (inner_high,) = inner_reads(HEADS // 2, units, values, column, row, ordered)
-    reads = read_out(ordered, (inner_low, inner_high), column, entry)
+    inner_far = inner_reads((FAR,), *blocks, query_in[FAR])
+    queries = [query_in[shift] for shift in range(OWNERS)]
+    reads = read_out(queries, inner_near, inner_far, column, entry)
 
     own = [reads[0]] + [hop(reads[shift], shift) for shift in (1, 2, 3)]
     paired = [swap(part) for part in own]
-    return mix_reads(route, gates, norm_gain[None], own, paired)[None]
+    partial = mix_near(gates, picks, [own[i] for i in NEAR], [paired[i] for i in NEAR])
+    return mix_reads(gates, picks, norm_gain[None], partial, own[FAR], paired[FAR])[None]
 
 
 def solution(mesh):

time: 102 us -> 98.9 us (0.970)
  starting transfers between devices: 48.1 us -> 42.5 us
  waiting for transfers between devices: 19.9 us -> 21 us
    ppermute x9, starting transfers between devices: 13.8 us -> 11.3 us  [exchange(): out.append(lax.ppermute(arrays[shift], 'context', pairs))]
    ppermute x10, starting transfers between devices: 22.5 us -> 20.7 us  [swap(): return lax.ppermute(array, 'dp', [(0, 1), (1, 0)])]
    ppermute x9, starting transfers between devices: 11.8 us -> 10.5 us  [hop(): lax.ppermute(array, 'memory', [(i, i ^ shift) for i in range(OWNERS)])]
    pallas_call x12 -> x13, Pallas kernels: 33.2 us -> 34.1 us  [kernel_call(): pl.pallas_call(kernel, out_shape=out_shape, in_specs=[pl.BlockSpec(memory...]
  transfers between devices with their start and end apart: 28 -> 28, of which waited for: 10 -> 11; matrix products, arithmetic and copies ran while one was open for 0% -> 0% of each run, Pallas kernels for 27% -> 30%
where the time goes in v5:
time: 98.9 us; the launch traced here: 98.7 us
  starting transfers between devices  42.5 us (43%)
  Pallas kernels  34.1 us (34%)
  waiting for transfers between devices  21 us (21%)
    pallas_call x13, Pallas kernels, kernel_call(): pl.pallas_call(kernel, out_shape=out_shape, in_specs=[pl.BlockSpec(memory...  34.1 us
    ppermute x10, starting transfers between devices, swap(): return lax.ppermute(array, 'dp', [(0, 1), (1, 0)])  20.7 us
    ppermute x9, waiting for transfers between devices, hop(): lax.ppermute(array, 'memory', [(i, i ^ shift) for i in range(OWNERS)])  11.3 us
    ppermute x9, starting transfers between devices, exchange(): out.append(lax.ppermute(arrays[shift], 'context', pairs))  11.3 us
    ppermute x9, starting transfers between devices, hop(): lax.ppermute(array, 'memory', [(i, i ^ shift) for i in range(OWNERS)])  10.5 us
    ppermute x9, waiting for transfers between devices, exchange(): out.append(lax.ppermute(arrays[shift], 'context', pairs))  5.58 us
    ppermute x10, waiting for transfers between devices, swap(): return lax.ppermute(array, 'dp', [(0, 1), (1, 0)])  4.12 us
  transfers between devices with their start and end apart: 28, of which 11 were waited for; matrix products, arithmetic and copies ran while one was open for 0% of the time, Pallas kernels for 30%

profile of v5, /device:TPU:1, one launch (start us, length us, event | category | flops | bytes accessed | tf_op | source)
XLA Modules:
  0.0 98.7 jit_solution(16260711672777374082)
XLA Ops:
  0.0 2.3 %pack_rows.1 = (bf16[80,4096]{1,0:T(8,128)(2,1)S(1)}, bf16[80,4096]{1,0:T(8,128)(2,1)S(1)}, bf16[80,4224]{1,0:T(8,128)(2,1)S(1)}, bf16[80,4096]{1,0:T(8,128)(2,1)S(1)}) custom-call(s32[2,128]{1,0:T(2,128)} %bitcast.22, bf16[128,4096]{1,0:T(8,128)(2,1)} %bitcast.13), custom_call_target="tpu_custom_call" | custom-call | flops 1 | bytes 1 | tf_op jit(solution)/shard_map/pack_rows/pallas_call | solution.py:70
  2.3 1.5 %collective-permute-start = (bf16[80,4096]{1,0:T(8,128)(2,1)S(1)}, bf16[80,4096]{1,0:T(8,128)(2,1)S(1)}, u32[]{:S(2)}, u32[]{:S(2)}) collective-permute-start(bf16[80,4096]{1,0:T(8,128)(2,1)S(1)} %get-tuple-element.54.refs_0_), channel_id=1, source_target_pairs={{0,1},{1,0},{2,3},{3,2},{4,5},{5,4},{6,7},{7,6},{8,9},{9,8},{10,11... | collective-permute-start | bytes 1966088 | tf_op jit(solution)/shard_map/ppermute | solution.py:503
  3.8 3.9 %collective-permute-start.4 = (bf16[80,4096]{1,0:T(8,128)(2,1)S(1)}, bf16[80,4096]{1,0:T(8,128)(2,1)S(1)}, u32[]{:S(2)}, u32[]{:S(2)}) collective-permute-start(bf16[80,4096]{1,0:T(8,128)(2,1)S(1)} %get-tuple-element.64), channel_id=1, source_target_pairs={{0,96},{32,64},{64,32},{96,0},{1,97},{33,65},{65,33},{97,1},{2,98}... | collective-permute-start | bytes 1966088 | tf_op jit(solution)/shard_map/ppermute | solution.py:491
  9.1 8.8 %project_2.2 = (bf16[2,80,1024]{2,1,0:T(8,128)(2,1)S(1)}, bf16[2,80,1024]{2,1,0:T(8,128)(2,1)S(1)}, f32[2,80,128]{2,1,0:T(8,128)S(1)}, bf16[4096,1024]{1,0:T(8,128)(2,1)S(1)}, bf16[4096,1024]{1,0:T(8,128)(2,1)S(1)}) custom-call(bf16[80,4096]{1,0:T(8,128)(2,1)} %copy-done.1, bf16[80,4096]{1,0:T(8,128)(2,1)} %copy-done.8, bf16[4096,1024]{1,0:T(8,128)(2,1)} %bitcast.25, ...), custom_call_target="tpu_custom_call" | custom-call | flops 1 | bytes 1 | tf_op jit(solution)/shard_map/project_2/pallas_call | solution.py:70
  19.0 3.6 %collective-permute-done.4.refs_2_ = bf16[80,4096]{1,0:T(8,128)(2,1)S(1)} collective-permute-done((bf16[80,4096]{1,0:T(8,128)(2,1)S(1)}, bf16[80,4096]{1,0:T(8,128)(2,1)S(1)}, u32[]{:S(2)}, u32[]{:S(2)}) %collective-permute-start.4) | collective-permute-done | bytes 655392 | tf_op jit(solution)/shard_map/ppermute | solution.py:491
  24.9 1.7 %collective-permute-done.6.refs_1_ = bf16[80,4096]{1,0:T(8,128)(2,1)S(1)} collective-permute-done((bf16[80,4096]{1,0:T(8,128)(2,1)S(1)}, bf16[80,4096]{1,0:T(8,128)(2,1)S(1)}, u32[]{:S(2)}, u32[]{:S(2)}) %collective-permute-start.6) | collective-permute-done | bytes 655392 | tf_op jit(solution)/shard_map/ppermute | solution.py:503
  27.6 6.3 %project_4.1 = (bf16[4,80,1024]{2,1,0:T(8,128)(2,1)S(1)}, bf16[4,80,1024]{2,1,0:T(8,128)(2,1)S(1)}, f32[4,80,128]{2,1,0:T(8,128)S(1)}) custom-call(bf16[80,4096]{1,0:T(8,128)(2,1)S(1)} %collective-permute-done.3.refs_0_, bf16[80,4096]{1,0:T(8,128)(2,1)S(1)} %collective-permute-done.6.refs_1_, bf16[80,4096]{1,0:T(8,128)(2,1)S(1)} %collective-permute-done.4.refs_2_, ...), custom_call_target="tpu_custom_call" | custom-call | flops 1 | bytes 1 | tf_op jit(solution)/shard_map/project_4/pallas_call | solution.py:70
  33.9 6.7 %collective-permute-done.5.refs_0_ = bf16[80,4224]{1,0:T(8,128)(2,1)S(1)} collective-permute-done((bf16[80,4224]{1,0:T(8,128)(2,1)S(1)}, bf16[80,4224]{1,0:T(8,128)(2,1)S(1)}, u32[]{:S(2)}, u32[]{:S(2)}) %collective-permute-start.5) | collective-permute-done | bytes 675872 | tf_op jit(solution)/shard_map/ppermute | solution.py:491
  40.6 2.1 %collective-permute-start.9 = (bf16[80,4224]{1,0:T(8,128)(2,1)S(1)}, bf16[80,4224]{1,0:T(8,128)(2,1)S(1)}, u32[]{:S(2)}, u32[]{:S(2)}) collective-permute-start(bf16[80,4224]{1,0:T(8,128)(2,1)S(1)} %collective-permute-done.5.refs_0_), channel_id=1, source_target_pairs={{0,1},{1,0},{2,3},{3,2},{4,5},{5,4},{6,7},{7,6},{8,9},{9,8},{10,11... | collective-permute-start | bytes 2027528 | tf_op jit(solution)/shard_map/ppermute | solution.py:503
  44.5 3.3 %project_2.3 = (bf16[2,80,1024]{2,1,0:T(8,128)(2,1)S(1)}, bf16[2,80,1024]{2,1,0:T(8,128)(2,1)S(1)}, f32[2,80,128]{2,1,0:T(8,128)S(1)}) custom-call(bf16[80,4224]{1,0:T(8,128)(2,1)S(1)} %collective-permute-done.5.refs_0_, bf16[80,4224]{1,0:T(8,128)(2,1)S(1)} %collective-permute-done.9.refs_1_, bf16[4096,1024]{1,0:T(8,128)(2,1)S(1)} %get-tuple-element.67.refs_4_.refs_2_, ...), custom_call_target="tpu_custom_call" | custom-call | flops 1 | bytes 1 | tf_op jit(solution)/shard_map/project_2/pallas_call | solution.py:70
  47.8 2.6 %block_state.1 = (bf16[288,128]{1,0:T(8,128)(2,1)S(1)}, bf16[288,128]{1,0:T(8,128)(2,1)S(1)}, bf16[288,128]{1,0:T(8,128)(2,1)S(1)}, bf16[288,128]{1,0:T(8,128)(2...) custom-call(bf16[2,80,1024]{2,1,0:T(8,128)(2,1)S(1)} %get-tuple-elem, ...), custom_call_target="tpu_custom_call" | custom-call | flops 1 | bytes 1 | tf_op jit(solution)/shard_map/block_state/pallas_call | solution.py:70
  50.3 1.4 %collective-permute-start.11 = (bf16[288,128]{1,0:T(8,128)(2,1)S(1)}, bf16[288,128]{1,0:T(8,128)(2,1)S(1)}, u32[]{:S(2)}, u32[]{:S(2)}) collective-permute-start(bf16[288,128]{1,0:T(8,128)(2,1)S(1)} %get-tuple-element.88), channel_id=1, source_target_pairs={{0,2},{2,0},{4,6},{6,4},{8,10},{10,8},{12,14},{14,12},{16,18},{18,... | collective-permute-start | bytes 221192 | tf_op jit(solution)/shard_map/ppermute | solution.py:498
  51.7 2.6 %collective-permute-start.12 = (bf16[288,128]{1,0:T(8,128)(2,1)S(1)}, bf16[288,128]{1,0:T(8,128)(2,1)S(1)}, u32[]{:S(2)}, u32[]{:S(2)}) collective-permute-start(bf16[288,128]{1,0:T(8,128)(2,1)S(1)} %get-tuple-element.89), channel_id=1, source_target_pairs={{0,4},{2,6},{4,0},{6,2},{8,12},{10,14},{12,8},{14,10},{16,20},{18,... | collective-permute-start | bytes 221192 | tf_op jit(solution)/shard_map/ppermute | solution.py:498
  54.4 3.8 %inner_reads_3.1.refs_4_ = f32[3,2,80,1024]{3,2,1,0:T(8,128)S(1)} custom-call(bf16[8,80,1024]{2,1,0:T(8,128)(2,1)S(1)} %get-tuple-element.81.refs_0_, bf16[8,80,1024]{2,1,0:T(8,128)(2,1)S(1)} %get-tuple-element.82.refs_1_, f32[8,80,128]{2,1,0:T(8,128)S(1)} %get-tuple-element.83.refs_2_.refs_6_, f32[8,640]{1,0:T(8,128)S(1)} %get-tuple-element.84.refs_3_, ...), custom_call_target="tpu_custom_call" | custom-call | flops 1 | bytes 1 | tf_op jit(solution)/shard_map/inner_reads_3/pallas_call | solution.py:70
  59.3 1.6 %collective-permute-start.14 = (bf16[2,80,1024]{2,1,0:T(8,128)(2,1)S(1)}, bf16[2,80,1024]{2,1,0:T(8,128)(2,1)S(1)}, u32[]{:S(2)}, u32[]{:S(2)}) collective-permute-start(bf16[2,80,1024]{2,1,0:T(8,128)(2,1)S(1)} %get-tuple-element.92), channel_id=1, source_target_pairs={{0,64},{32,96},{64,0},{96,32},{1,65},{33,97},{65,1},{97,33},{2,66}... | collective-permute-start | bytes 983048 | tf_op jit(solution)/shard_map/ppermute | solution.py:491
  60.9 2.5 %collective-permute-start.17 = (bf16[288,128]{1,0:T(8,128)(2,1)S(1)}, bf16[288,128]{1,0:T(8,128)(2,1)S(1)}, u32[]{:S(2)}, u32[]{:S(2)}) collective-permute-start(bf16[288,128]{1,0:T(8,128)(2,1)S(1)} %get-tuple-element.91.refs_0_), channel_id=1, source_target_pairs={{0,24},{2,26},{4,28},{6,30},{8,16},{10,18},{12,20},{14,22},{16,8},... | collective-permute-start | bytes 221192 | tf_op jit(solution)/shard_map/ppermute | solution.py:498
  65.3 3.1 %collective-permute-done.16.refs_2_ = bf16[288,128]{1,0:T(8,128)(2,1)S(1)} collective-permute-done((bf16[288,128]{1,0:T(8,128)(2,1)S(1)}, bf16[288,128]{1,0:T(8,128)(2,1)S(1)}, u32[]{:S(2)}, u32[]{:S(2)}) %collective-permute-start.16) | collective-permute-done | bytes 73760 | tf_op jit(solution)/shard_map/ppermute | solution.py:498
  68.7 2.8 %collective-permute-start.19 = (bf16[256,128]{1,0:T(8,128)(2,1)S(1)}, bf16[256,128]{1,0:T(8,128)(2,1)S(1)}, u32[]{:S(2)}, u32[]{:S(2)}) collective-permute-start(bf16[256,128]{1,0:T(8,128)(2,1)S(1)} %get-tuple-element.97), channel_id=1, source_target_pairs={{0,4},{2,6},{4,0},{6,2},{8,12},{10,14},{12,8},{14,10},{16,20},{18,... | collective-permute-start | bytes 196616 | tf_op jit(solution)/shard_map/ppermute | solution.py:498
  72.5 2.9 %inner_reads_1.1.refs_5_ = f32[1,2,80,1024]{3,2,1,0:T(8,128)S(1)} custom-call(bf16[8,80,1024]{2,1,0:T(8,128)(2,1)S(1)} %get-tuple-element.81.refs_0_, bf16[8,80,1024]{2,1,0:T(8,128)(2,1)S(1)} %get-tuple-element.82.refs_1_, f32[8,80,128]{2,1,0:T(8,128)S(1)} %get-tuple-element.83.refs_2_.refs_6_, f32[8,640]{1,0:T(8,128)S(1)} %get-tuple-element.84.refs_3_, ...), custom_call_target="tpu_custom_call" | custom-call | flops 1 | bytes 1 | tf_op jit(solution)/shard_map/inner_reads_1/pallas_call | solution.py:70
  78.4 1.6 %collective-permute-start.26 = (bf16[2,80,1024]{2,1,0:T(8,128)(2,1)S(1)}, bf16[2,80,1024]{2,1,0:T(8,128)(2,1)S(1)}, u32[]{:S(2)}, u32[]{:S(2)}) collective-permute-start(bf16[2,80,1024]{2,1,0:T(8,128)(2,1)S(1)} %get-tuple-element.102), channel_id=1, source_target_pairs={{0,64},{32,96},{64,0},{96,32},{1,65},{33,97},{65,1},{97,33},{2,66}... | collective-permute-start | bytes 983048 | tf_op jit(solution)/shard_map/ppermute | solution.py:491
  80.0 5.4 %collective-permute-start.23 = (bf16[2,80,1024]{2,1,0:T(8,128)(2,1)S(1)}, bf16[2,80,1024]{2,1,0:T(8,128)(2,1)S(1)}, u32[]{:S(2)}, u32[]{:S(2)}) collective-permute-start(bf16[2,80,1024]{2,1,0:T(8,128)(2,1)S(1)} %get-tuple-element.99.refs_0_), channel_id=1, source_target_pairs={{0,1},{1,0},{2,3},{3,2},{4,5},{5,4},{6,7},{7,6},{8,9},{9,8},{10,11... | collective-permute-start | bytes 983048 | tf_op jit(solution)/shard_map/ppermute | solution.py:503
  85.4 5.1 %collective-permute-start.24 = (bf16[2,80,1024]{2,1,0:T(8,128)(2,1)S(1)}, bf16[2,80,1024]{2,1,0:T(8,128)(2,1)S(1)}, u32[]{:S(2)}, u32[]{:S(2)}) collective-permute-start(bf16[2,80,1024]{2,1,0:T(8,128)(2,1)S(1)} %collective-permute-done.21.refs_1_), channel_id=1, source_target_pairs={{0,1},{1,0},{2,3},{3,2},{4,5},{5,4},{6,7},{7,6},{8,9},{9,8},{10,11... | collective-permute-start | bytes 983048 | tf_op jit(solution)/shard_map/ppermute | solution.py:503
  90.5 5.0 %collective-permute-start.25 = (bf16[2,80,1024]{2,1,0:T(8,128)(2,1)S(1)}, bf16[2,80,1024]{2,1,0:T(8,128)(2,1)S(1)}, u32[]{:S(2)}, u32[]{:S(2)}) collective-permute-start(bf16[2,80,1024]{2,1,0:T(8,128)(2,1)S(1)} %collective-permute-done.22.refs_2_), channel_id=1, source_target_pairs={{0,1},{1,0},{2,3},{3,2},{4,5},{5,4},{6,7},{7,6},{8,9},{9,8},{10,11... | collective-permute-start | bytes 983048 | tf_op jit(solution)/shard_map/ppermute | solution.py:503
  97.4 1.3 %mix_reads.1 = bf16[128,2048]{1,0:T(8,128)(2,1)} custom-call(f32[128,128]{1,0:T(8,128)S(1)} %get-tuple-element.57.gates_ref, bf16[4,128,128]{2,1,0:T(8,128)(2,1)S(1)} %get-tuple-element.58.picks_ref, f32[1,2048]{1,0:T(1,128)S(1)} %bitcast.21, f32[2,128,1024]{2,1,0:T(8,128)S(1)} %mix_near.1.partial, bf16[2,80,1024]{2,1,0:T(8,128)(2,1)S(1)} %collective-permute-done.26.own, ...), custom_call_target="tpu_custom_call" | custom-call | flops 1 | bytes 1 | tf_op jit(solution)/shard_map/mix_reads/pallas_call | solution.py:70
  (63 shorter events, 16.6 us)
Async XLA Ops:
  2.3 5.9 %collective-permute-start = (bf16[80,4096]{1,0:T(8,128)(2,1)S(1)}, bf16[80,4096]{1,0:T(8,128)(2,1)S(1)}, u32[]{:S(2)}, u32[]{:S(2)}) collective-permute-start(bf16[80,4096]{1,0:T(8,128)(2,1)S(1)} %get-tuple-element.54.refs_0_), channel_id=1, source_target_pairs={{0,1},{1,0},{2,3},{3,2},{4,5},{5,4},{6,7},{7,6},{8,9},{9,8},{10,11... | collective-permute-start | bytes 1966088 | tf_op jit(solution)/shard_map/ppermute | solution.py:503
  3.8 18.9 %collective-permute-start.4 = (bf16[80,4096]{1,0:T(8,128)(2,1)S(1)}, bf16[80,4096]{1,0:T(8,128)(2,1)S(1)}, u32[]{:S(2)}, u32[]{:S(2)}) collective-permute-start(bf16[80,4096]{1,0:T(8,128)(2,1)S(1)} %get-tuple-element.64), channel_id=1, source_target_pairs={{0,96},{32,64},{64,32},{96,0},{1,97},{33,65},{65,33},{97,1},{2,98}... | collective-permute-start | bytes 1966088 | tf_op jit(solution)/shard_map/ppermute | solution.py:491
  7.7 16.0 %collective-permute-start.3 = (bf16[80,4096]{1,0:T(8,128)(2,1)S(1)}, bf16[80,4096]{1,0:T(8,128)(2,1)S(1)}, u32[]{:S(2)}, u32[]{:S(2)}) collective-permute-start(bf16[80,4096]{1,0:T(8,128)(2,1)S(1)} %get-tuple-element.62), channel_id=1, source_target_pairs={{0,32},{32,0},{64,96},{96,64},{1,33},{33,1},{65,97},{97,65},{2,34}... | collective-permute-start | bytes 1966088 | tf_op jit(solution)/shard_map/ppermute | solution.py:491
  7.7 10.3 %collective-permute-start.2 = (bf16[128,2048]{1,0:T(8,128)(2,1)}, bf16[128,2048]{1,0:T(8,128)(2,1)S(1)}, u32[]{:S(2)}, u32[]{:S(2)}) collective-permute-start(bf16[128,2048]{1,0:T(8,128)(2,1)} %bitcast.18), channel_id=1, source_target_pairs={{0,1},{1,0},{2,3},{3,2},{4,5},{5,4},{6,7},{7,6},{8,9},{9,8},{10,11... | collective-permute-start | bytes 1572872 | tf_op jit(solution)/shard_map/ppermute | solution.py:503
  8.0 9.9 %collective-permute-start.1 = (s32[2,128]{1,0:T(2,128)}, s32[2,128]{1,0:T(2,128)S(1)}, u32[]{:S(2)}, u32[]{:S(2)}) collective-permute-start(s32[2,128]{1,0:T(2,128)} %bitcast.23), channel_id=1, source_target_pairs={{0,1},{1,0},{2,3},{3,2},{4,5},{5,4},{6,7},{7,6},{8,9},{9,8},{10,11... | collective-permute-start | bytes 3080 | tf_op jit(solution)/shard_map/ppermute | solution.py:503
  23.6 17.0 %collective-permute-start.5 = (bf16[80,4224]{1,0:T(8,128)(2,1)S(1)}, bf16[80,4224]{1,0:T(8,128)(2,1)S(1)}, u32[]{:S(2)}, u32[]{:S(2)}) collective-permute-start(bf16[80,4224]{1,0:T(8,128)(2,1)S(1)} %get-tuple-element.66), channel_id=1, source_target_pairs={{0,64},{32,96},{64,0},{96,32},{1,65},{33,97},{65,1},{97,33},{2,66}... | collective-permute-start | bytes 2027528 | tf_op jit(solution)/shard_map/ppermute | solution.py:491
  42.7 11.7 %collective-permute-start.8 = (bf16[2,80,1024]{2,1,0:T(8,128)(2,1)S(1)}, bf16[2,80,1024]{2,1,0:T(8,128)(2,1)S(1)}, u32[]{:S(2)}, u32[]{:S(2)}) collective-permute-start(bf16[2,80,1024]{2,1,0:T(8,128)(2,1)S(1)} %get-tuple-element.71), channel_id=1, source_target_pairs={{0,32},{32,0},{64,96},{96,64},{1,33},{33,1},{65,97},{97,65},{2,34}... | collective-permute-start | bytes 983048 | tf_op jit(solution)/shard_map/ppermute | solution.py:491
  43.0 11.4 %collective-permute-start.10 = (bf16[2,80,1024]{2,1,0:T(8,128)(2,1)S(1)}, bf16[2,80,1024]{2,1,0:T(8,128)(2,1)S(1)}, u32[]{:S(2)}, u32[]{:S(2)}) collective-permute-start(bf16[2,80,1024]{2,1,0:T(8,128)(2,1)S(1)} %get-tuple-element.86), channel_id=1, source_target_pairs={{0,96},{32,64},{64,32},{96,0},{1,97},{33,65},{65,33},{97,1},{2,98}... | collective-permute-start | bytes 983048 | tf_op jit(solution)/shard_map/ppermute | solution.py:491
  50.3 7.9 %collective-permute-start.11 = (bf16[288,128]{1,0:T(8,128)(2,1)S(1)}, bf16[288,128]{1,0:T(8,128)(2,1)S(1)}, u32[]{:S(2)}, u32[]{:S(2)}) collective-permute-start(bf16[288,128]{1,0:T(8,128)(2,1)S(1)} %get-tuple-element.88), channel_id=1, source_target_pairs={{0,2},{2,0},{4,6},{6,4},{8,10},{10,8},{12,14},{14,12},{16,18},{18,... | collective-permute-start | bytes 221192 | tf_op jit(solution)/shard_map/ppermute | solution.py:498
  51.7 6.5 %collective-permute-start.12 = (bf16[288,128]{1,0:T(8,128)(2,1)S(1)}, bf16[288,128]{1,0:T(8,128)(2,1)S(1)}, u32[]{:S(2)}, u32[]{:S(2)}) collective-permute-start(bf16[288,128]{1,0:T(8,128)(2,1)S(1)} %get-tuple-element.89), channel_id=1, source_target_pairs={{0,4},{2,6},{4,0},{6,2},{8,12},{10,14},{12,8},{14,10},{16,20},{18,... | collective-permute-start | bytes 221192 | tf_op jit(solution)/shard_map/ppermute | solution.py:498
  54.3 4.9 %collective-permute-start.13 = (bf16[288,128]{1,0:T(8,128)(2,1)S(1)}, bf16[288,128]{1,0:T(8,128)(2,1)S(1)}, u32[]{:S(2)}, u32[]{:S(2)}) collective-permute-start(bf16[288,128]{1,0:T(8,128)(2,1)S(1)} %get-tuple-element.90), channel_id=1, source_target_pairs={{0,6},{2,4},{4,2},{6,0},{8,14},{10,12},{12,10},{14,8},{16,22},{18,... | collective-permute-start | bytes 221192 | tf_op jit(solution)/shard_map/ppermute | solution.py:498
  59.3 13.2 %collective-permute-start.14 = (bf16[2,80,1024]{2,1,0:T(8,128)(2,1)S(1)}, bf16[2,80,1024]{2,1,0:T(8,128)(2,1)S(1)}, u32[]{:S(2)}, u32[]{:S(2)}) collective-permute-start(bf16[2,80,1024]{2,1,0:T(8,128)(2,1)S(1)} %get-tuple-element.92), channel_id=1, source_target_pairs={{0,64},{32,96},{64,0},{96,32},{1,65},{33,97},{65,1},{97,33},{2,66}... | collective-permute-start | bytes 983048 | tf_op jit(solution)/shard_map/ppermute | solution.py:491
  60.9 4.4 %collective-permute-start.17 = (bf16[288,128]{1,0:T(8,128)(2,1)S(1)}, bf16[288,128]{1,0:T(8,128)(2,1)S(1)}, u32[]{:S(2)}, u32[]{:S(2)}) collective-permute-start(bf16[288,128]{1,0:T(8,128)(2,1)S(1)} %get-tuple-element.91.refs_0_), channel_id=1, source_target_pairs={{0,24},{2,26},{4,28},{6,30},{8,16},{10,18},{12,20},{14,22},{16,8},... | collective-permute-start | bytes 221192 | tf_op jit(solution)/shard_map/ppermute | solution.py:498
  63.4 5.0 %collective-permute-start.16 = (bf16[288,128]{1,0:T(8,128)(2,1)S(1)}, bf16[288,128]{1,0:T(8,128)(2,1)S(1)}, u32[]{:S(2)}, u32[]{:S(2)}) collective-permute-start(bf16[288,128]{1,0:T(8,128)(2,1)S(1)} %get-tuple-element.91.refs_0_), channel_id=1, source_target_pairs={{0,16},{2,18},{4,20},{6,22},{8,24},{10,26},{12,28},{14,30},{16,0},... | collective-permute-start | bytes 221192 | tf_op jit(solution)/shard_map/ppermute | solution.py:498
  63.9 4.5 %collective-permute-start.15 = (bf16[288,128]{1,0:T(8,128)(2,1)S(1)}, bf16[288,128]{1,0:T(8,128)(2,1)S(1)}, u32[]{:S(2)}, u32[]{:S(2)}) collective-permute-start(bf16[288,128]{1,0:T(8,128)(2,1)S(1)} %get-tuple-element.91.refs_0_), channel_id=1, source_target_pairs={{0,8},{2,10},{4,12},{6,14},{8,0},{10,2},{12,4},{14,6},{16,24},{18,... | collective-permute-start | bytes 221192 | tf_op jit(solution)/shard_map/ppermute | solution.py:498
  68.6 6.9 %collective-permute-start.18 = (bf16[256,128]{1,0:T(8,128)(2,1)S(1)}, bf16[256,128]{1,0:T(8,128)(2,1)S(1)}, u32[]{:S(2)}, u32[]{:S(2)}) collective-permute-start(bf16[256,128]{1,0:T(8,128)(2,1)S(1)} %get-tuple-element.96), channel_id=1, source_target_pairs={{0,2},{2,0},{4,6},{6,4},{8,10},{10,8},{12,14},{14,12},{16,18},{18,... | collective-permute-start | bytes 196616 | tf_op jit(solution)/shard_map/ppermute | solution.py:498
  68.7 6.8 %collective-permute-start.19 = (bf16[256,128]{1,0:T(8,128)(2,1)S(1)}, bf16[256,128]{1,0:T(8,128)(2,1)S(1)}, u32[]{:S(2)}, u32[]{:S(2)}) collective-permute-start(bf16[256,128]{1,0:T(8,128)(2,1)S(1)} %get-tuple-element.97), channel_id=1, source_target_pairs={{0,4},{2,6},{4,0},{6,2},{8,12},{10,14},{12,8},{14,10},{16,20},{18,... | collective-permute-start | bytes 196616 | tf_op jit(solution)/shard_map/ppermute | solution.py:498
  71.5 4.3 %collective-permute-start.20 = (bf16[256,128]{1,0:T(8,128)(2,1)S(1)}, bf16[256,128]{1,0:T(8,128)(2,1)S(1)}, u32[]{:S(2)}, u32[]{:S(2)}) collective-permute-start(bf16[256,128]{1,0:T(8,128)(2,1)S(1)} %get-tuple-element.98), channel_id=1, source_target_pairs={{0,6},{2,4},{4,2},{6,0},{8,14},{10,12},{12,10},{14,8},{16,22},{18,... | collective-permute-start | bytes 196616 | tf_op jit(solution)/shard_map/ppermute | solution.py:498
  76.7 8.7 %collective-permute-start.21 = (bf16[2,80,1024]{2,1,0:T(8,128)(2,1)S(1)}, bf16[2,80,1024]{2,1,0:T(8,128)(2,1)S(1)}, u32[]{:S(2)}, u32[]{:S(2)}) collective-permute-start(bf16[2,80,1024]{2,1,0:T(8,128)(2,1)S(1)} %get-tuple-element.100), channel_id=1, source_target_pairs={{0,32},{32,0},{64,96},{96,64},{1,33},{33,1},{65,97},{97,65},{2,34}... | collective-permute-start | bytes 983048 | tf_op jit(solution)/shard_map/ppermute | solution.py:491
  77.1 13.4 %collective-permute-start.22 = (bf16[2,80,1024]{2,1,0:T(8,128)(2,1)S(1)}, bf16[2,80,1024]{2,1,0:T(8,128)(2,1)S(1)}, u32[]{:S(2)}, u32[]{:S(2)}) collective-permute-start(bf16[2,80,1024]{2,1,0:T(8,128)(2,1)S(1)} %get-tuple-element.101), channel_id=1, source_target_pairs={{0,96},{32,64},{64,32},{96,0},{1,97},{33,65},{65,33},{97,1},{2,98}... | collective-permute-start | bytes 983048 | tf_op jit(solution)/shard_map/ppermute | solution.py:491
  78.4 17.1 %collective-permute-start.26 = (bf16[2,80,1024]{2,1,0:T(8,128)(2,1)S(1)}, bf16[2,80,1024]{2,1,0:T(8,128)(2,1)S(1)}, u32[]{:S(2)}, u32[]{:S(2)}) collective-permute-start(bf16[2,80,1024]{2,1,0:T(8,128)(2,1)S(1)} %get-tuple-element.102), channel_id=1, source_target_pairs={{0,64},{32,96},{64,0},{96,32},{1,65},{33,97},{65,1},{97,33},{2,66}... | collective-permute-start | bytes 983048 | tf_op jit(solution)/shard_map/ppermute | solution.py:491
  80.0 15.5 %collective-permute-start.23 = (bf16[2,80,1024]{2,1,0:T(8,128)(2,1)S(1)}, bf16[2,80,1024]{2,1,0:T(8,128)(2,1)S(1)}, u32[]{:S(2)}, u32[]{:S(2)}) collective-permute-start(bf16[2,80,1024]{2,1,0:T(8,128)(2,1)S(1)} %get-tuple-element.99.refs_0_), channel_id=1, source_target_pairs={{0,1},{1,0},{2,3},{3,2},{4,5},{5,4},{6,7},{7,6},{8,9},{9,8},{10,11... | collective-permute-start | bytes 983048 | tf_op jit(solution)/shard_map/ppermute | solution.py:503
  85.4 10.1 %collective-permute-start.24 = (bf16[2,80,1024]{2,1,0:T(8,128)(2,1)S(1)}, bf16[2,80,1024]{2,1,0:T(8,128)(2,1)S(1)}, u32[]{:S(2)}, u32[]{:S(2)}) collective-permute-start(bf16[2,80,1024]{2,1,0:T(8,128)(2,1)S(1)} %collective-permute-done.21.refs_1_), channel_id=1, source_target_pairs={{0,1},{1,0},{2,3},{3,2},{4,5},{5,4},{6,7},{7,6},{8,9},{9,8},{10,11... | collective-permute-start | bytes 983048 | tf_op jit(solution)/shard_map/ppermute | solution.py:503
  90.5 6.3 %collective-permute-start.25 = (bf16[2,80,1024]{2,1,0:T(8,128)(2,1)S(1)}, bf16[2,80,1024]{2,1,0:T(8,128)(2,1)S(1)}, u32[]{:S(2)}, u32[]{:S(2)}) collective-permute-start(bf16[2,80,1024]{2,1,0:T(8,128)(2,1)S(1)} %collective-permute-done.22.refs_2_), channel_id=1, source_target_pairs={{0,1},{1,0},{2,3},{3,2},{4,5},{5,4},{6,7},{7,6},{8,9},{9,8},{10,11... | collective-permute-start | bytes 983048 | tf_op jit(solution)/shard_map/ppermute | solution.py:503
  (13 other events, 133.6 us)

commit v6 on v5

--- a/solution.py
+++ b/solution.py
@@ -20,6 +20,7 @@
 PAD = 128
 PACKS = 4
 NEAR, FAR = (0, 1, 3), 2
+AWAY = (1, 3, 2)
 RING = 4
 PIECE = HALF // RING
 TAIL = 16
@@ -79,41 +80,41 @@
     )(*operands)
 
 
+def select_columns(pick, rows_ref, columns, out_refs):
+    part = dot(pick.astype(BF16), rows_ref[:, columns])
+    if columns.start == 0:
+        empty = jnp.sum(pick, axis=1, keepdims=True) == 0.0
+        first_lane = iota((part.shape[0], HEAD_DIM), 1) == 0
+        marked = jnp.where(first_lane & empty, EMPTY, part[:, :HEAD_DIM])
+        part = jnp.concatenate([marked, part[:, HEAD_DIM:]], axis=1)
+    part = part.astype(BF16)
+    for to, out_ref in enumerate(out_refs):
+        out_ref[:, columns] = part[to * CAP : (to + 1) * CAP]
+
+
 def pack_rows_kernel(route_hbm, rows_hbm, *refs):
-    out_refs, (route_ref, rows_ref, sems) = refs[:OWNERS], refs[OWNERS:]
+    out_refs, (route_ref, rows_ref, sems) = refs[: len(AWAY)], refs[len(AWAY) :]
     owner = lax.axis_index("memory")
     width = D // PACKS
     route_copy = pltpu.make_async_copy(route_hbm, route_ref, sems.at[PACKS])
     route_copy.start()
-    copies = []
-    for at in range(PACKS):
-        columns = slice(at * width, (at + 1) * width)
+    parts, copies = [slice(at * width, (at + 1) * width) for at in range(PACKS)], []
+    for at, columns in enumerate(parts):
         copies.append(
             pltpu.make_async_copy(rows_hbm.at[:, columns], rows_ref.at[:, columns], sems.at[at])
         )
         copies[at].start()
     route_copy.wait()
     place = membership(route_ref[...])[1]
-    pick = jnp.concatenate([one_hot(place, owner ^ shift) for shift in range(OWNERS)], axis=0)
-    empty = jnp.sum(pick, axis=1, keepdims=True) == 0.0
-    pick = pick.astype(BF16)
-    first_lane = iota((OWNERS * CAP, HEAD_DIM), 1) == 0
-    for at in range(PACKS):
-        copies[at].wait()
-        part = dot(pick, rows_ref[:, at * width : (at + 1) * width])
-        if at == 0:
-            marked = jnp.where(first_lane & empty, EMPTY, part[:, :HEAD_DIM])
-            part = jnp.concatenate([marked, part[:, HEAD_DIM:]], axis=1)
-        part = part.astype(BF16)
-        for shift in range(OWNERS):
-            out_refs[shift][:, at * width : (at + 1) * width] = part[
-                shift * CAP : (shift + 1) * CAP
-            ]
-    out_refs[2][:, D:] = jnp.zeros((CAP, PAD), BF16)
+    pick = jnp.concatenate([one_hot(place, owner ^ shift) for shift in AWAY], axis=0)
+    for copy, columns in zip(copies, parts):
+        copy.wait()
+        select_columns(pick, rows_ref, columns, out_refs)
+    out_refs[AWAY.index(FAR)][:, D:] = jnp.zeros((CAP, PAD), BF16)
 
 
 def pack_rows(route, rows):
-    out = [near((CAP, D + PAD * (shift == 2)), BF16) for shift in range(OWNERS)]
+    out = [near((CAP, D + PAD * (shift == FAR)), BF16) for shift in AWAY]
     scratch = [
         pltpu.VMEM((2, ROWS), jnp.int32),
         pltpu.VMEM((ROWS, D), BF16),
@@ -184,9 +185,16 @@
         held[rows, :HEAD_DIM] = jnp.where(lives[at], head, 0.0).astype(BF16)
         held[rows, HEAD_DIM:] = row_refs[at][:, HEAD_DIM:D]
     decay = log_sigmoid(dot_rows(held[...], decay_ref[...]) + bias_ref[...])
-    decay_out[...] = jnp.zeros_like(decay_out)
+    upto = (iota((CAP, CAP), 0) >= iota((CAP, CAP), 1)).astype(F32).astype(BF16)
     for at in range(count):
-        decay_out[at, :, :HEADS] = jnp.where(lives[at], decay[at * CAP : (at + 1) * CAP], 0.0)
+        kept = jnp.where(lives[at], decay[at * CAP : (at + 1) * CAP], 0.0)
+        kept = jnp.concatenate([kept, jnp.zeros((CAP, 128 - HEADS), F32)], axis=1)
+        total = jnp.zeros((CAP, 128), F32)
+        for _ in range(3):
+            part = kept.astype(BF16)
+            kept = kept - part.astype(F32)
+            total = total + dot(upto, part)
+        decay_out[at] = total
     for start in range(0, HALF, WIDTH):
         ready(start // WIDTH)
         columns = slice(start, start + WIDTH)
@@ -201,24 +209,27 @@
         value_out[:, :, columns] = values.reshape(count, CAP, WIDTH)
 
 
-def project_first_kernel(count, *refs):
-    key_hbm, value_hbm, decay_ref, bias_ref = refs[count : count + 4]
-    outs, (key_ref, value_ref, held, sems) = refs[count + 4 : count + 7], refs[count + 7 :]
+def project_first_kernel(*refs):
+    route_ref, rows_ref, key_hbm, value_hbm, decay_ref, bias_ref = refs[:6]
+    outs, (key_ref, value_ref, packed, held, sems) = refs[6:9], refs[9:]
     copies = []
     for at, start in enumerate(range(0, HALF, WIDTH)):
         columns = slice(start, start + WIDTH)
-        for side, (far, near) in enumerate(((key_hbm, key_ref), (value_hbm, value_ref))):
+        for side, (far, close) in enumerate(((key_hbm, key_ref), (value_hbm, value_ref))):
             copies.append(
-                pltpu.make_async_copy(far.at[:, columns], near.at[:, columns], sems.at[side, at])
+                pltpu.make_async_copy(far.at[:, columns], close.at[:, columns], sems.at[side, at])
             )
     for copy in copies:
         copy.start()
+    pick = one_hot(membership(route_ref[...])[1], lax.axis_index("memory"))
+    for start in range(0, D, WIDTH):
+        select_columns(pick, rows_ref, slice(start, start + WIDTH), [packed])
 
     def ready(at):
         copies[2 * at].wait()
         copies[2 * at + 1].wait()
 
-    project_parts(refs[:count], decay_ref, bias_ref, outs, key_ref, value_ref, held, ready)
+    project_parts([packed], decay_ref, bias_ref, outs, key_ref, value_ref, held, ready)
 
 
 def project_next_kernel(count, *refs):
@@ -229,31 +240,27 @@
     )
 
 
-def project(row_parts, key_weight, value_weight, decay_weight, decay_bias, first=False):
+def projected(count):
+    out = [near((count, CAP, HALF), BF16)] * 2 + [near((count, CAP, 128), F32)]
+    return out, [pltpu.VMEM((count * CAP, D), BF16)]
+
+
+def project_first(route, rows, *weights):
+    out, scratch = projected(1)
+    out = out + [near((D, HALF), BF16)] * 2 + [near((CAP, D), BF16)]
+    scratch = scratch + [pltpu.SemaphoreType.DMA((2, HALF // WIDTH))]
+    operands = (route, rows, *weights)
+    return kernel_call(project_first_kernel, "project_first", out, scratch, 40, *operands, hbm=(2, 3))
+
+
+def project(row_parts, *weights):
     count = len(row_parts)
-    out = [near((count, CAP, HALF), BF16)] * 2
-    out = out + [near((count, CAP, 128), F32)]
-    scratch = [pltpu.VMEM((count * CAP, D), BF16)]
-    kernel = project_first_kernel if first else project_next_kernel
-    if first:
-        out = out + [near((D, HALF), BF16)] * 2
-        scratch = scratch + [pltpu.SemaphoreType.DMA((2, HALF // WIDTH))]
-    return kernel_call(
-        functools.partial(kernel, count),
-        f"project_{count}",
-        out,
-        scratch,
-        40 if first else 12,
-        *row_parts,
-        key_weight,
-        value_weight,
-        decay_weight,
-        decay_bias,
-        hbm=(count, count + 1) if first else (),
-    )
-
-
-GROUPS = (((0, 0), (0, 1)), ((1, 0), (1, 1), (3, 0), (3, 1)), ((2, 0), (2, 1)))
+    out, scratch = projected(count)
+    kernel = functools.partial(project_next_kernel, count)
+    return kernel_call(kernel, f"project_{count}", out, scratch, 12, *row_parts, *weights)
+
+
+GROUPS = (((0, 0),), ((0, 1), (1, 0), (1, 1), (3, 0), (3, 1)), ((2, 0), (2, 1)))
 
 
 def token_order(refs, held):
@@ -287,15 +294,13 @@
     messages = refs[9:13]
     column_out, row_out, units, values, decays, quarters = refs[13:]
     token_order(decay_refs, decays)
-    total = decays[...].reshape(SLOTS, 128).T[:HEADS]
-    lane = iota((HEADS, SLOTS), 1)
-    reach = 1
-    while reach < SLOTS:
-        total = total + jnp.where(lane >= reach, pltpu.roll(total, reach, 1), 0.0)
-        reach *= 2
-    row_out[...] = total
-    running = jnp.concatenate([total, jnp.zeros((128 - HEADS, SLOTS), F32)], axis=0).T
+    offset, chunks = jnp.zeros((1, 128), F32), []
+    for chunk in range(CHUNKS):
+        chunks.append(decays[chunk] + offset)
+        offset = chunks[chunk][CAP - 1 :]
+    running = jnp.concatenate(chunks, axis=0)
     column_out[...] = running.reshape(CHUNKS, CAP, 128)
+    row_out[...] = running.T[:HEADS]
     token_order(unit_refs, units)
     token_order(value_refs, values)
     last = running[SLOTS - 1 : SLOTS]
@@ -517,13 +522,11 @@
     rows, query_rows, route = hidden[0], queries[0], route_ids[0].T
     weights = (key_weight[0], value_weight[0], decay_weight[0].T, decay_bias)
 
-    packed = pack_rows(route, rows)
-    arrived = {0: packed[0]}
-    for shift in (1, 3):
-        arrived[shift] = hop(packed[shift], shift)
-    other = {0: swap(packed[0])}
+    packed = dict(zip(AWAY, pack_rows(route, rows)))
+    arrived = {shift: hop(packed[shift], shift) for shift in (1, 3)}
     other_route, other_query = swap(route), swap(query_rows)
-    first = project([arrived[0], other[0]], *weights, first=True)
+    first = project_first(route, rows, *weights)
+    other = {0: swap(first[5])}
     weights = (first[3], first[4], *weights[2:])
     packed_query = pack_queries(
         after(route, first[2]), other_route, query_rows, other_query, rows, router_weight.T
@@ -534,7 +537,8 @@
     arrived[2] = hop(after(packed[2], arrived[1], arrived[3]), 2)
     for shift in (1, 3):
         other[shift] = swap(arrived[shift])
-    second = project([arrived[1], other[1], arrived[3], other[3]], *weights)
+    near_rows = [other[0], arrived[1], other[1], arrived[3], other[3]]
+    second = project(near_rows, *weights)
     arrived[2] = after(arrived[2], second[2])
     other[2] = swap(arrived[2])
     query_in = {0: packed_query[0]}

time: 98.9 us -> 97.1 us (0.982)
  waiting for transfers between devices: 21 us -> 16.5 us
  Pallas kernels: 34.1 us -> 36.1 us
  starting transfers between devices: 42.5 us -> 44.2 us
    ppermute x9, waiting for transfers between devices: 11.3 us -> 6.28 us  [hop(): lax.ppermute(array, 'memory', [(i, i ^ shift) for i in range(OWNERS)])]
    pallas_call x13, Pallas kernels: 34.1 us -> 36.1 us  [kernel_call(): pl.pallas_call(kernel, out_shape=out_shape, in_specs=[pl.BlockSpec(memory...]
  transfers between devices with their start and end apart: 28 -> 28, of which waited for: 11 -> 12; matrix products, arithmetic and copies ran while one was open for 0% -> 0% of each run, Pallas kernels for 30% -> 33%
where the time goes in v6:
time: 97.1 us; the launch traced here: 97 us
  starting transfers between devices  44.2 us (46%)
  Pallas kernels  36.1 us (37%)
  waiting for transfers between devices  16.5 us (17%)
    pallas_call x13, Pallas kernels, kernel_call(): pl.pallas_call(kernel, out_shape=out_shape, in_specs=[pl.BlockSpec(memory...  36.1 us
    ppermute x10, starting transfers between devices, swap(): return lax.ppermute(array, 'dp', [(0, 1), (1, 0)])  21.6 us
    ppermute x9, starting transfers between devices, hop(): lax.ppermute(array, 'memory', [(i, i ^ shift) for i in range(OWNERS)])  11.4 us
    ppermute x9, starting transfers between devices, exchange(): out.append(lax.ppermute(arrays[shift], 'context', pairs))  11.2 us
    ppermute x9, waiting for transfers between devices, hop(): lax.ppermute(array, 'memory', [(i, i ^ shift) for i in range(OWNERS)])  6.28 us
    ppermute x9, waiting for transfers between devices, exchange(): out.append(lax.ppermute(arrays[shift], 'context', pairs))  5.64 us
    ppermute x10, waiting for transfers between devices, swap(): return lax.ppermute(array, 'dp', [(0, 1), (1, 0)])  4.55 us
  transfers between devices with their start and end apart: 28, of which 12 were waited for; matrix products, arithmetic and copies ran while one was open for 0% of the time, Pallas kernels for 33%

profile of v6, /device:TPU:1, one launch (start us, length us, event | category | flops | bytes accessed | tf_op | source)
XLA Modules:
  0.0 97.0 jit_solution(2876894688381131263)
XLA Ops:
  0.0 2.1 %pack_rows.1 = (bf16[80,4096]{1,0:T(8,128)(2,1)S(1)}, bf16[80,4096]{1,0:T(8,128)(2,1)S(1)}, bf16[80,4224]{1,0:T(8,128)(2,1)S(1)}) custom-call(s32[2,128]{1,0:T(2,128)} %bitcast.22, bf16[128,4096]{1,0:T(8,128)(2,1)} %bitcast.13), custom_call_target="tpu_custom_call" | custom-call | flops 1 | bytes 1 | tf_op jit(solution)/shard_map/pack_rows/pallas_call | solution.py:71
  2.1 4.7 %collective-permute-start.3 = (bf16[80,4096]{1,0:T(8,128)(2,1)S(1)}, bf16[80,4096]{1,0:T(8,128)(2,1)S(1)}, u32[]{:S(2)}, u32[]{:S(2)}) collective-permute-start(bf16[80,4096]{1,0:T(8,128)(2,1)S(1)} %get-tuple-element.63), channel_id=1, source_target_pairs={{0,96},{32,64},{64,32},{96,0},{1,97},{33,65},{65,33},{97,1},{2,98}... | collective-permute-start | bytes 1966088 | tf_op jit(solution)/shard_map/ppermute | solution.py:496
  7.8 9.0 %project_first.1 = (bf16[1,80,1024]{2,1,0:T(8,128)(2,1)S(1)}, bf16[1,80,1024]{2,1,0:T(8,128)(2,1)S(1)}, f32[1,80,128]{2,1,0:T(8,128)S(1)}, bf16[4096,1024]{1,0:T...) custom-call(s32[2,128]{1,0:T(2,128)} %bitcast.24, bf16[128,4096]{1,0:T(8,128)(2,1)} %bitcast.14, ...), custom_call_target="tpu_custom_call" | custom-call | flops 1 | bytes 1 | tf_op jit(solution)/shard_map/project_first/pallas_call | solution.py:71
  17.9 3.4 %collective-permute-done.3.refs_3_ = bf16[80,4096]{1,0:T(8,128)(2,1)S(1)} collective-permute-done((bf16[80,4096]{1,0:T(8,128)(2,1)S(1)}, bf16[80,4096]{1,0:T(8,128)(2,1)S(1)}, u32[]{:S(2)}, u32[]{:S(2)}) %collective-permute-start.3) | collective-permute-done | bytes 655392 | tf_op jit(solution)/shard_map/ppermute | solution.py:496
  22.3 1.8 %collective-permute-start.5 = (bf16[80,4096]{1,0:T(8,128)(2,1)S(1)}, bf16[80,4096]{1,0:T(8,128)(2,1)S(1)}, u32[]{:S(2)}, u32[]{:S(2)}) collective-permute-start(bf16[80,4096]{1,0:T(8,128)(2,1)S(1)} %get-tuple-element.66), channel_id=1, source_target_pairs={{0,1},{1,0},{2,3},{3,2},{4,5},{5,4},{6,7},{7,6},{8,9},{9,8},{10,11... | collective-permute-start | bytes 1966088 | tf_op jit(solution)/shard_map/ppermute | solution.py:508
  27.8 8.5 %project_5.1 = (bf16[5,80,1024]{2,1,0:T(8,128)(2,1)S(1)}, bf16[5,80,1024]{2,1,0:T(8,128)(2,1)S(1)}, f32[5,80,128]{2,1,0:T(8,128)S(1)}) custom-call(bf16[80,4096]{1,0:T(8,128)(2,1)S(1)} %collective-permute-done.5.refs_0_, bf16[80,4096]{1,0:T(8,128)(2,1)S(1)} %collective-permute-done.2.refs_1_, bf16[80,4096]{1,0:T(8,128)(2,1)S(1)} %collective-permute-done.6.refs_2_, ...), custom_call_target="tpu_custom_call" | custom-call | flops 1 | bytes 1 | tf_op jit(solution)/shard_map/project_5/pallas_call | solution.py:71
  36.3 2.1 %collective-permute-done.4.refs_0_ = bf16[80,4224]{1,0:T(8,128)(2,1)S(1)} collective-permute-done((bf16[80,4224]{1,0:T(8,128)(2,1)S(1)}, bf16[80,4224]{1,0:T(8,128)(2,1)S(1)}, u32[]{:S(2)}, u32[]{:S(2)}) %collective-permute-start.4) | collective-permute-done | bytes 675872 | tf_op jit(solution)/shard_map/ppermute | solution.py:496
  38.4 2.8 %collective-permute-start.9 = (bf16[80,4224]{1,0:T(8,128)(2,1)S(1)}, bf16[80,4224]{1,0:T(8,128)(2,1)S(1)}, u32[]{:S(2)}, u32[]{:S(2)}) collective-permute-start(bf16[80,4224]{1,0:T(8,128)(2,1)S(1)} %collective-permute-done.4.refs_0_), channel_id=1, source_target_pairs={{0,1},{1,0},{2,3},{3,2},{4,5},{5,4},{6,7},{7,6},{8,9},{9,8},{10,11... | collective-permute-start | bytes 2027528 | tf_op jit(solution)/shard_map/ppermute | solution.py:508
  42.9 3.7 %project_2.1 = (bf16[2,80,1024]{2,1,0:T(8,128)(2,1)S(1)}, bf16[2,80,1024]{2,1,0:T(8,128)(2,1)S(1)}, f32[2,80,128]{2,1,0:T(8,128)S(1)}) custom-call(bf16[80,4224]{1,0:T(8,128)(2,1)S(1)} %collective-permute-done.4.refs_0_, bf16[80,4224]{1,0:T(8,128)(2,1)S(1)} %collective-permute-done.9.refs_1_, bf16[4096,1024]{1,0:T(8,128)(2,1)S(1)} %get-tuple-element.67.refs_5_.refs_2_, ...), custom_call_target="tpu_custom_call" | custom-call | flops 1 | bytes 1 | tf_op jit(solution)/shard_map/project_2/pallas_call | solution.py:71
  46.7 1.9 %block_state.1 = (bf16[288,128]{1,0:T(8,128)(2,1)S(1)}, bf16[288,128]{1,0:T(8,128)(2,1)S(1)}, bf16[288,128]{1,0:T(8,128)(2,1)S(1)}, bf16[288,128]{1,0:T(8,128)(2...) custom-call(bf16[1,80,1024]{2,1,0:T(8,128)(2,1)S(1)} %get-tuple-elem, ...), custom_call_target="tpu_custom_call" | custom-call | flops 1 | bytes 1 | tf_op jit(solution)/shard_map/block_state/pallas_call | solution.py:71
  48.6 1.4 %collective-permute-start.11 = (bf16[288,128]{1,0:T(8,128)(2,1)S(1)}, bf16[288,128]{1,0:T(8,128)(2,1)S(1)}, u32[]{:S(2)}, u32[]{:S(2)}) collective-permute-start(bf16[288,128]{1,0:T(8,128)(2,1)S(1)} %get-tuple-element.88), channel_id=1, source_target_pairs={{0,2},{2,0},{4,6},{6,4},{8,10},{10,8},{12,14},{14,12},{16,18},{18,... | collective-permute-start | bytes 221192 | tf_op jit(solution)/shard_map/ppermute | solution.py:503
  50.0 2.6 %collective-permute-start.12 = (bf16[288,128]{1,0:T(8,128)(2,1)S(1)}, bf16[288,128]{1,0:T(8,128)(2,1)S(1)}, u32[]{:S(2)}, u32[]{:S(2)}) collective-permute-start(bf16[288,128]{1,0:T(8,128)(2,1)S(1)} %get-tuple-element.89), channel_id=1, source_target_pairs={{0,4},{2,6},{4,0},{6,2},{8,12},{10,14},{12,8},{14,10},{16,20},{18,... | collective-permute-start | bytes 221192 | tf_op jit(solution)/shard_map/ppermute | solution.py:503
  52.6 3.8 %inner_reads_3.1.refs_4_ = f32[3,2,80,1024]{3,2,1,0:T(8,128)S(1)} custom-call(bf16[8,80,1024]{2,1,0:T(8,128)(2,1)S(1)} %get-tuple-element.81.refs_0_, bf16[8,80,1024]{2,1,0:T(8,128)(2,1)S(1)} %get-tuple-element.82.refs_1_, f32[8,80,128]{2,1,0:T(8,128)S(1)} %get-tuple-element.83.refs_2_.refs_6_, f32[8,640]{1,0:T(8,128)S(1)} %get-tuple-element.84.refs_3_, ...), custom_call_target="tpu_custom_call" | custom-call | flops 1 | bytes 1 | tf_op jit(solution)/shard_map/inner_reads_3/pallas_call | solution.py:71
  57.6 1.6 %collective-permute-start.14 = (bf16[2,80,1024]{2,1,0:T(8,128)(2,1)S(1)}, bf16[2,80,1024]{2,1,0:T(8,128)(2,1)S(1)}, u32[]{:S(2)}, u32[]{:S(2)}) collective-permute-start(bf16[2,80,1024]{2,1,0:T(8,128)(2,1)S(1)} %get-tuple-element.92), channel_id=1, source_target_pairs={{0,64},{32,96},{64,0},{96,32},{1,65},{33,97},{65,1},{97,33},{2,66}... | collective-permute-start | bytes 983048 | tf_op jit(solution)/shard_map/ppermute | solution.py:496
  59.2 2.5 %collective-permute-start.17 = (bf16[288,128]{1,0:T(8,128)(2,1)S(1)}, bf16[288,128]{1,0:T(8,128)(2,1)S(1)}, u32[]{:S(2)}, u32[]{:S(2)}) collective-permute-start(bf16[288,128]{1,0:T(8,128)(2,1)S(1)} %get-tuple-element.91.refs_0_), channel_id=1, source_target_pairs={{0,24},{2,26},{4,28},{6,30},{8,16},{10,18},{12,20},{14,22},{16,8},... | collective-permute-start | bytes 221192 | tf_op jit(solution)/shard_map/ppermute | solution.py:503
  63.6 3.1 %collective-permute-done.16.refs_2_ = bf16[288,128]{1,0:T(8,128)(2,1)S(1)} collective-permute-done((bf16[288,128]{1,0:T(8,128)(2,1)S(1)}, bf16[288,128]{1,0:T(8,128)(2,1)S(1)}, u32[]{:S(2)}, u32[]{:S(2)}) %collective-permute-start.16) | collective-permute-done | bytes 73760 | tf_op jit(solution)/shard_map/ppermute | solution.py:503
  66.9 2.8 %collective-permute-start.19 = (bf16[256,128]{1,0:T(8,128)(2,1)S(1)}, bf16[256,128]{1,0:T(8,128)(2,1)S(1)}, u32[]{:S(2)}, u32[]{:S(2)}) collective-permute-start(bf16[256,128]{1,0:T(8,128)(2,1)S(1)} %get-tuple-element.97), channel_id=1, source_target_pairs={{0,4},{2,6},{4,0},{6,2},{8,12},{10,14},{12,8},{14,10},{16,20},{18,... | collective-permute-start | bytes 196616 | tf_op jit(solution)/shard_map/ppermute | solution.py:503
  70.8 2.9 %inner_reads_1.1.refs_5_ = f32[1,2,80,1024]{3,2,1,0:T(8,128)S(1)} custom-call(bf16[8,80,1024]{2,1,0:T(8,128)(2,1)S(1)} %get-tuple-element.81.refs_0_, bf16[8,80,1024]{2,1,0:T(8,128)(2,1)S(1)} %get-tuple-element.82.refs_1_, f32[8,80,128]{2,1,0:T(8,128)S(1)} %get-tuple-element.83.refs_2_.refs_6_, f32[8,640]{1,0:T(8,128)S(1)} %get-tuple-element.84.refs_3_, ...), custom_call_target="tpu_custom_call" | custom-call | flops 1 | bytes 1 | tf_op jit(solution)/shard_map/inner_reads_1/pallas_call | solution.py:71
  75.4 1.3 %collective-permute-start.22 = (bf16[2,80,1024]{2,1,0:T(8,128)(2,1)S(1)}, bf16[2,80,1024]{2,1,0:T(8,128)(2,1)S(1)}, u32[]{:S(2)}, u32[]{:S(2)}) collective-permute-start(bf16[2,80,1024]{2,1,0:T(8,128)(2,1)S(1)} %get-tuple-element.101), channel_id=1, source_target_pairs={{0,96},{32,64},{64,32},{96,0},{1,97},{33,65},{65,33},{97,1},{2,98}... | collective-permute-start | bytes 983048 | tf_op jit(solution)/shard_map/ppermute | solution.py:496
  76.7 1.6 %collective-permute-start.26 = (bf16[2,80,1024]{2,1,0:T(8,128)(2,1)S(1)}, bf16[2,80,1024]{2,1,0:T(8,128)(2,1)S(1)}, u32[]{:S(2)}, u32[]{:S(2)}) collective-permute-start(bf16[2,80,1024]{2,1,0:T(8,128)(2,1)S(1)} %get-tuple-element.102), channel_id=1, source_target_pairs={{0,64},{32,96},{64,0},{96,32},{1,65},{33,97},{65,1},{97,33},{2,66}... | collective-permute-start | bytes 983048 | tf_op jit(solution)/shard_map/ppermute | solution.py:496
  78.3 5.4 %collective-permute-start.23 = (bf16[2,80,1024]{2,1,0:T(8,128)(2,1)S(1)}, bf16[2,80,1024]{2,1,0:T(8,128)(2,1)S(1)}, u32[]{:S(2)}, u32[]{:S(2)}) collective-permute-start(bf16[2,80,1024]{2,1,0:T(8,128)(2,1)S(1)} %get-tuple-element.99.refs_0_), channel_id=1, source_target_pairs={{0,1},{1,0},{2,3},{3,2},{4,5},{5,4},{6,7},{7,6},{8,9},{9,8},{10,11... | collective-permute-start | bytes 983048 | tf_op jit(solution)/shard_map/ppermute | solution.py:508
  83.7 5.0 %collective-permute-start.24 = (bf16[2,80,1024]{2,1,0:T(8,128)(2,1)S(1)}, bf16[2,80,1024]{2,1,0:T(8,128)(2,1)S(1)}, u32[]{:S(2)}, u32[]{:S(2)}) collective-permute-start(bf16[2,80,1024]{2,1,0:T(8,128)(2,1)S(1)} %collective-permute-done.21.refs_1_), channel_id=1, source_target_pairs={{0,1},{1,0},{2,3},{3,2},{4,5},{5,4},{6,7},{7,6},{8,9},{9,8},{10,11... | collective-permute-start | bytes 983048 | tf_op jit(solution)/shard_map/ppermute | solution.py:508
  88.7 5.1 %collective-permute-start.25 = (bf16[2,80,1024]{2,1,0:T(8,128)(2,1)S(1)}, bf16[2,80,1024]{2,1,0:T(8,128)(2,1)S(1)}, u32[]{:S(2)}, u32[]{:S(2)}) collective-permute-start(bf16[2,80,1024]{2,1,0:T(8,128)(2,1)S(1)} %collective-permute-done.22.refs_2_), channel_id=1, source_target_pairs={{0,1},{1,0},{2,3},{3,2},{4,5},{5,4},{6,7},{7,6},{8,9},{9,8},{10,11... | collective-permute-start | bytes 983048 | tf_op jit(solution)/shard_map/ppermute | solution.py:508
  95.6 1.3 %mix_reads.1 = bf16[128,2048]{1,0:T(8,128)(2,1)} custom-call(f32[128,128]{1,0:T(8,128)S(1)} %get-tuple-element.56.gates_ref, bf16[4,128,128]{2,1,0:T(8,128)(2,1)S(1)} %get-tuple-element.57.picks_ref, f32[1,2048]{1,0:T(1,128)S(1)} %bitcast.26, f32[2,128,1024]{2,1,0:T(8,128)S(1)} %mix_near.1.partial, bf16[2,80,1024]{2,1,0:T(8,128)(2,1)S(1)} %collective-permute-done.26.own, ...), custom_call_target="tpu_custom_call" | custom-call | flops 1 | bytes 1 | tf_op jit(solution)/shard_map/mix_reads/pallas_call | solution.py:71
  (59 shorter events, 16.3 us)
Async XLA Ops:
  2.1 19.1 %collective-permute-start.3 = (bf16[80,4096]{1,0:T(8,128)(2,1)S(1)}, bf16[80,4096]{1,0:T(8,128)(2,1)S(1)}, u32[]{:S(2)}, u32[]{:S(2)}) collective-permute-start(bf16[80,4096]{1,0:T(8,128)(2,1)S(1)} %get-tuple-element.63), channel_id=1, source_target_pairs={{0,96},{32,64},{64,32},{96,0},{1,97},{33,65},{65,33},{97,1},{2,98}... | collective-permute-start | bytes 1966088 | tf_op jit(solution)/shard_map/ppermute | solution.py:496
  6.8 15.3 %collective-permute-start.2 = (bf16[80,4096]{1,0:T(8,128)(2,1)S(1)}, bf16[80,4096]{1,0:T(8,128)(2,1)S(1)}, u32[]{:S(2)}, u32[]{:S(2)}) collective-permute-start(bf16[80,4096]{1,0:T(8,128)(2,1)S(1)} %get-tuple-element.61), channel_id=1, source_target_pairs={{0,32},{32,0},{64,96},{96,64},{1,33},{33,1},{65,97},{97,65},{2,34}... | collective-permute-start | bytes 1966088 | tf_op jit(solution)/shard_map/ppermute | solution.py:496
  6.8 10.0 %collective-permute-start.1 = (bf16[128,2048]{1,0:T(8,128)(2,1)}, bf16[128,2048]{1,0:T(8,128)(2,1)S(1)}, u32[]{:S(2)}, u32[]{:S(2)}) collective-permute-start(bf16[128,2048]{1,0:T(8,128)(2,1)} %bitcast.19), channel_id=1, source_target_pairs={{0,1},{1,0},{2,3},{3,2},{4,5},{5,4},{6,7},{7,6},{8,9},{9,8},{10,11... | collective-permute-start | bytes 1572872 | tf_op jit(solution)/shard_map/ppermute | solution.py:508
  7.8 9.0 %collective-permute-start = (s32[2,128]{1,0:T(2,128)}, s32[2,128]{1,0:T(2,128)S(1)}, u32[]{:S(2)}, u32[]{:S(2)}) collective-permute-start(s32[2,128]{1,0:T(2,128)} %bitcast.23), channel_id=1, source_target_pairs={{0,1},{1,0},{2,3},{3,2},{4,5},{5,4},{6,7},{7,6},{8,9},{9,8},{10,11... | collective-permute-start | bytes 3080 | tf_op jit(solution)/shard_map/ppermute | solution.py:508
  22.1 16.3 %collective-permute-start.4 = (bf16[80,4224]{1,0:T(8,128)(2,1)S(1)}, bf16[80,4224]{1,0:T(8,128)(2,1)S(1)}, u32[]{:S(2)}, u32[]{:S(2)}) collective-permute-start(bf16[80,4224]{1,0:T(8,128)(2,1)S(1)} %get-tuple-element.65), channel_id=1, source_target_pairs={{0,64},{32,96},{64,0},{96,32},{1,65},{33,97},{65,1},{97,33},{2,66}... | collective-permute-start | bytes 2027528 | tf_op jit(solution)/shard_map/ppermute | solution.py:496
  38.4 4.5 %collective-permute-start.9 = (bf16[80,4224]{1,0:T(8,128)(2,1)S(1)}, bf16[80,4224]{1,0:T(8,128)(2,1)S(1)}, u32[]{:S(2)}, u32[]{:S(2)}) collective-permute-start(bf16[80,4224]{1,0:T(8,128)(2,1)S(1)} %collective-permute-done.4.refs_0_), channel_id=1, source_target_pairs={{0,1},{1,0},{2,3},{3,2},{4,5},{5,4},{6,7},{7,6},{8,9},{9,8},{10,11... | collective-permute-start | bytes 2027528 | tf_op jit(solution)/shard_map/ppermute | solution.py:508
  41.2 11.5 %collective-permute-start.8 = (bf16[2,80,1024]{2,1,0:T(8,128)(2,1)S(1)}, bf16[2,80,1024]{2,1,0:T(8,128)(2,1)S(1)}, u32[]{:S(2)}, u32[]{:S(2)}) collective-permute-start(bf16[2,80,1024]{2,1,0:T(8,128)(2,1)S(1)} %get-tuple-element.71), channel_id=1, source_target_pairs={{0,32},{32,0},{64,96},{96,64},{1,33},{33,1},{65,97},{97,65},{2,34}... | collective-permute-start | bytes 983048 | tf_op jit(solution)/shard_map/ppermute | solution.py:496
  41.5 11.1 %collective-permute-start.10 = (bf16[2,80,1024]{2,1,0:T(8,128)(2,1)S(1)}, bf16[2,80,1024]{2,1,0:T(8,128)(2,1)S(1)}, u32[]{:S(2)}, u32[]{:S(2)}) collective-permute-start(bf16[2,80,1024]{2,1,0:T(8,128)(2,1)S(1)} %get-tuple-element.86), channel_id=1, source_target_pairs={{0,96},{32,64},{64,32},{96,0},{1,97},{33,65},{65,33},{97,1},{2,98}... | collective-permute-start | bytes 983048 | tf_op jit(solution)/shard_map/ppermute | solution.py:496
  48.6 7.8 %collective-permute-start.11 = (bf16[288,128]{1,0:T(8,128)(2,1)S(1)}, bf16[288,128]{1,0:T(8,128)(2,1)S(1)}, u32[]{:S(2)}, u32[]{:S(2)}) collective-permute-start(bf16[288,128]{1,0:T(8,128)(2,1)S(1)} %get-tuple-element.88), channel_id=1, source_target_pairs={{0,2},{2,0},{4,6},{6,4},{8,10},{10,8},{12,14},{14,12},{16,18},{18,... | collective-permute-start | bytes 221192 | tf_op jit(solution)/shard_map/ppermute | solution.py:503
  50.0 6.5 %collective-permute-start.12 = (bf16[288,128]{1,0:T(8,128)(2,1)S(1)}, bf16[288,128]{1,0:T(8,128)(2,1)S(1)}, u32[]{:S(2)}, u32[]{:S(2)}) collective-permute-start(bf16[288,128]{1,0:T(8,128)(2,1)S(1)} %get-tuple-element.89), channel_id=1, source_target_pairs={{0,4},{2,6},{4,0},{6,2},{8,12},{10,14},{12,8},{14,10},{16,20},{18,... | collective-permute-start | bytes 221192 | tf_op jit(solution)/shard_map/ppermute | solution.py:503
  52.6 4.9 %collective-permute-start.13 = (bf16[288,128]{1,0:T(8,128)(2,1)S(1)}, bf16[288,128]{1,0:T(8,128)(2,1)S(1)}, u32[]{:S(2)}, u32[]{:S(2)}) collective-permute-start(bf16[288,128]{1,0:T(8,128)(2,1)S(1)} %get-tuple-element.90), channel_id=1, source_target_pairs={{0,6},{2,4},{4,2},{6,0},{8,14},{10,12},{12,10},{14,8},{16,22},{18,... | collective-permute-start | bytes 221192 | tf_op jit(solution)/shard_map/ppermute | solution.py:503
  57.6 13.2 %collective-permute-start.14 = (bf16[2,80,1024]{2,1,0:T(8,128)(2,1)S(1)}, bf16[2,80,1024]{2,1,0:T(8,128)(2,1)S(1)}, u32[]{:S(2)}, u32[]{:S(2)}) collective-permute-start(bf16[2,80,1024]{2,1,0:T(8,128)(2,1)S(1)} %get-tuple-element.92), channel_id=1, source_target_pairs={{0,64},{32,96},{64,0},{96,32},{1,65},{33,97},{65,1},{97,33},{2,66}... | collective-permute-start | bytes 983048 | tf_op jit(solution)/shard_map/ppermute | solution.py:496
  59.2 4.4 %collective-permute-start.17 = (bf16[288,128]{1,0:T(8,128)(2,1)S(1)}, bf16[288,128]{1,0:T(8,128)(2,1)S(1)}, u32[]{:S(2)}, u32[]{:S(2)}) collective-permute-start(bf16[288,128]{1,0:T(8,128)(2,1)S(1)} %get-tuple-element.91.refs_0_), channel_id=1, source_target_pairs={{0,24},{2,26},{4,28},{6,30},{8,16},{10,18},{12,20},{14,22},{16,8},... | collective-permute-start | bytes 221192 | tf_op jit(solution)/shard_map/ppermute | solution.py:503
  61.7 5.0 %collective-permute-start.16 = (bf16[288,128]{1,0:T(8,128)(2,1)S(1)}, bf16[288,128]{1,0:T(8,128)(2,1)S(1)}, u32[]{:S(2)}, u32[]{:S(2)}) collective-permute-start(bf16[288,128]{1,0:T(8,128)(2,1)S(1)} %get-tuple-element.91.refs_0_), channel_id=1, source_target_pairs={{0,16},{2,18},{4,20},{6,22},{8,24},{10,26},{12,28},{14,30},{16,0},... | collective-permute-start | bytes 221192 | tf_op jit(solution)/shard_map/ppermute | solution.py:503
  62.2 4.5 %collective-permute-start.15 = (bf16[288,128]{1,0:T(8,128)(2,1)S(1)}, bf16[288,128]{1,0:T(8,128)(2,1)S(1)}, u32[]{:S(2)}, u32[]{:S(2)}) collective-permute-start(bf16[288,128]{1,0:T(8,128)(2,1)S(1)} %get-tuple-element.91.refs_0_), channel_id=1, source_target_pairs={{0,8},{2,10},{4,12},{6,14},{8,0},{10,2},{12,4},{14,6},{16,24},{18,... | collective-permute-start | bytes 221192 | tf_op jit(solution)/shard_map/ppermute | solution.py:503
  66.9 6.9 %collective-permute-start.18 = (bf16[256,128]{1,0:T(8,128)(2,1)S(1)}, bf16[256,128]{1,0:T(8,128)(2,1)S(1)}, u32[]{:S(2)}, u32[]{:S(2)}) collective-permute-start(bf16[256,128]{1,0:T(8,128)(2,1)S(1)} %get-tuple-element.96), channel_id=1, source_target_pairs={{0,2},{2,0},{4,6},{6,4},{8,10},{10,8},{12,14},{14,12},{16,18},{18,... | collective-permute-start | bytes 196616 | tf_op jit(solution)/shard_map/ppermute | solution.py:503
  66.9 6.8 %collective-permute-start.19 = (bf16[256,128]{1,0:T(8,128)(2,1)S(1)}, bf16[256,128]{1,0:T(8,128)(2,1)S(1)}, u32[]{:S(2)}, u32[]{:S(2)}) collective-permute-start(bf16[256,128]{1,0:T(8,128)(2,1)S(1)} %get-tuple-element.97), channel_id=1, source_target_pairs={{0,4},{2,6},{4,0},{6,2},{8,12},{10,14},{12,8},{14,10},{16,20},{18,... | collective-permute-start | bytes 196616 | tf_op jit(solution)/shard_map/ppermute | solution.py:503
  69.7 4.3 %collective-permute-start.20 = (bf16[256,128]{1,0:T(8,128)(2,1)S(1)}, bf16[256,128]{1,0:T(8,128)(2,1)S(1)}, u32[]{:S(2)}, u32[]{:S(2)}) collective-permute-start(bf16[256,128]{1,0:T(8,128)(2,1)S(1)} %get-tuple-element.98), channel_id=1, source_target_pairs={{0,6},{2,4},{4,2},{6,0},{8,14},{10,12},{12,10},{14,8},{16,22},{18,... | collective-permute-start | bytes 196616 | tf_op jit(solution)/shard_map/ppermute | solution.py:503
  75.0 8.7 %collective-permute-start.21 = (bf16[2,80,1024]{2,1,0:T(8,128)(2,1)S(1)}, bf16[2,80,1024]{2,1,0:T(8,128)(2,1)S(1)}, u32[]{:S(2)}, u32[]{:S(2)}) collective-permute-start(bf16[2,80,1024]{2,1,0:T(8,128)(2,1)S(1)} %get-tuple-element.100), channel_id=1, source_target_pairs={{0,32},{32,0},{64,96},{96,64},{1,33},{33,1},{65,97},{97,65},{2,34}... | collective-permute-start | bytes 983048 | tf_op jit(solution)/shard_map/ppermute | solution.py:496
  75.4 13.4 %collective-permute-start.22 = (bf16[2,80,1024]{2,1,0:T(8,128)(2,1)S(1)}, bf16[2,80,1024]{2,1,0:T(8,128)(2,1)S(1)}, u32[]{:S(2)}, u32[]{:S(2)}) collective-permute-start(bf16[2,80,1024]{2,1,0:T(8,128)(2,1)S(1)} %get-tuple-element.101), channel_id=1, source_target_pairs={{0,96},{32,64},{64,32},{96,0},{1,97},{33,65},{65,33},{97,1},{2,98}... | collective-permute-start | bytes 983048 | tf_op jit(solution)/shard_map/ppermute | solution.py:496
  76.7 17.1 %collective-permute-start.26 = (bf16[2,80,1024]{2,1,0:T(8,128)(2,1)S(1)}, bf16[2,80,1024]{2,1,0:T(8,128)(2,1)S(1)}, u32[]{:S(2)}, u32[]{:S(2)}) collective-permute-start(bf16[2,80,1024]{2,1,0:T(8,128)(2,1)S(1)} %get-tuple-element.102), channel_id=1, source_target_pairs={{0,64},{32,96},{64,0},{96,32},{1,65},{33,97},{65,1},{97,33},{2,66}... | collective-permute-start | bytes 983048 | tf_op jit(solution)/shard_map/ppermute | solution.py:496
  78.3 15.5 %collective-permute-start.23 = (bf16[2,80,1024]{2,1,0:T(8,128)(2,1)S(1)}, bf16[2,80,1024]{2,1,0:T(8,128)(2,1)S(1)}, u32[]{:S(2)}, u32[]{:S(2)}) collective-permute-start(bf16[2,80,1024]{2,1,0:T(8,128)(2,1)S(1)} %get-tuple-element.99.refs_0_), channel_id=1, source_target_pairs={{0,1},{1,0},{2,3},{3,2},{4,5},{5,4},{6,7},{7,6},{8,9},{9,8},{10,11... | collective-permute-start | bytes 983048 | tf_op jit(solution)/shard_map/ppermute | solution.py:508
  83.7 10.1 %collective-permute-start.24 = (bf16[2,80,1024]{2,1,0:T(8,128)(2,1)S(1)}, bf16[2,80,1024]{2,1,0:T(8,128)(2,1)S(1)}, u32[]{:S(2)}, u32[]{:S(2)}) collective-permute-start(bf16[2,80,1024]{2,1,0:T(8,128)(2,1)S(1)} %collective-permute-done.21.refs_1_), channel_id=1, source_target_pairs={{0,1},{1,0},{2,3},{3,2},{4,5},{5,4},{6,7},{7,6},{8,9},{9,8},{10,11... | collective-permute-start | bytes 983048 | tf_op jit(solution)/shard_map/ppermute | solution.py:508
  88.7 6.3 %collective-permute-start.25 = (bf16[2,80,1024]{2,1,0:T(8,128)(2,1)S(1)}, bf16[2,80,1024]{2,1,0:T(8,128)(2,1)S(1)}, u32[]{:S(2)}, u32[]{:S(2)}) collective-permute-start(bf16[2,80,1024]{2,1,0:T(8,128)(2,1)S(1)} %collective-permute-done.22.refs_2_), channel_id=1, source_target_pairs={{0,1},{1,0},{2,3},{3,2},{4,5},{5,4},{6,7},{7,6},{8,9},{9,8},{10,11... | collective-permute-start | bytes 983048 | tf_op jit(solution)/shard_map/ppermute | solution.py:508
  (11 other events, 130.8 us)

commit v7 on v6

--- a/solution.py
+++ b/solution.py
@@ -172,6 +172,7 @@
 
 
 WIDTH = 512
+LONGEST = -128.0
 
 
 def project_parts(row_refs, decay_ref, bias_ref, outs, key_ref, value_ref, held, ready):
@@ -187,7 +188,8 @@
     decay = log_sigmoid(dot_rows(held[...], decay_ref[...]) + bias_ref[...])
     upto = (iota((CAP, CAP), 0) >= iota((CAP, CAP), 1)).astype(F32).astype(BF16)
     for at in range(count):
-        kept = jnp.where(lives[at], decay[at * CAP : (at + 1) * CAP], 0.0)
+        kept = jnp.maximum(decay[at * CAP : (at + 1) * CAP], LONGEST)
+        kept = jnp.where(lives[at], kept, 0.0)
         kept = jnp.concatenate([kept, jnp.zeros((CAP, 128 - HEADS), F32)], axis=1)
         total = jnp.zeros((CAP, 128), F32)
         for _ in range(3):
@@ -286,7 +288,8 @@
 
 
 def from_parts(rows):
-    return rows[:1].astype(F32) + rows[TAIL // 2 : TAIL // 2 + 1].astype(F32)
+    wide = rows.astype(F32)
+    return wide[:1] + wide[TAIL // 2 : TAIL // 2 + 1]
 
 
 def state_kernel(*refs):

time: 97.1 us -> 97.1 us (level)
  no operation moved by 1% of the time
where the time goes in v7:
time: 97.1 us; the launch traced here: 97 us
  starting transfers between devices  44.1 us (45%)
  Pallas kernels  36.1 us (37%)
  waiting for transfers between devices  16.5 us (17%)
    pallas_call x13, Pallas kernels, kernel_call(): pl.pallas_call(kernel, out_shape=out_shape, in_specs=[pl.BlockSpec(memory...  36.1 us
    ppermute x10, starting transfers between devices, swap(): return lax.ppermute(array, 'dp', [(0, 1), (1, 0)])  21.6 us
    ppermute x9, starting transfers between devices, hop(): lax.ppermute(array, 'memory', [(i, i ^ shift) for i in range(OWNERS)])  11.4 us
    ppermute x9, starting transfers between devices, exchange(): out.append(lax.ppermute(arrays[shift], 'context', pairs))  11.2 us
    ppermute x9, waiting for transfers between devices, hop(): lax.ppermute(array, 'memory', [(i, i ^ shift) for i in range(OWNERS)])  6.28 us
    ppermute x9, waiting for transfers between devices, exchange(): out.append(lax.ppermute(arrays[shift], 'context', pairs))  5.63 us
    ppermute x10, waiting for transfers between devices, swap(): return lax.ppermute(array, 'dp', [(0, 1), (1, 0)])  4.55 us
  transfers between devices with their start and end apart: 28, of which 12 were waited for; matrix products, arithmetic and copies ran while one was open for 0% of the time, Pallas kernels for 33%

profile of v7, /device:TPU:1, one launch (start us, length us, event | category | flops | bytes accessed | tf_op | source)
XLA Modules:
  0.0 97.0 jit_solution(14415216190184882401)
XLA Ops:
  0.0 2.1 %pack_rows.1 = (bf16[80,4096]{1,0:T(8,128)(2,1)S(1)}, bf16[80,4096]{1,0:T(8,128)(2,1)S(1)}, bf16[80,4224]{1,0:T(8,128)(2,1)S(1)}) custom-call(s32[2,128]{1,0:T(2,128)} %bitcast.22, bf16[128,4096]{1,0:T(8,128)(2,1)} %bitcast.13), custom_call_target="tpu_custom_call" | custom-call | flops 1 | bytes 1 | tf_op jit(solution)/shard_map/pack_rows/pallas_call | solution.py:71
  2.1 4.7 %collective-permute-start.3 = (bf16[80,4096]{1,0:T(8,128)(2,1)S(1)}, bf16[80,4096]{1,0:T(8,128)(2,1)S(1)}, u32[]{:S(2)}, u32[]{:S(2)}) collective-permute-start(bf16[80,4096]{1,0:T(8,128)(2,1)S(1)} %get-tuple-element.63), channel_id=1, source_target_pairs={{0,96},{32,64},{64,32},{96,0},{1,97},{33,65},{65,33},{97,1},{2,98}... | collective-permute-start | bytes 1966088 | tf_op jit(solution)/shard_map/ppermute | solution.py:499
  7.8 9.0 %project_first.1 = (bf16[1,80,1024]{2,1,0:T(8,128)(2,1)S(1)}, bf16[1,80,1024]{2,1,0:T(8,128)(2,1)S(1)}, f32[1,80,128]{2,1,0:T(8,128)S(1)}, bf16[4096,1024]{1,0:T...) custom-call(s32[2,128]{1,0:T(2,128)} %bitcast.24, bf16[128,4096]{1,0:T(8,128)(2,1)} %bitcast.14, ...), custom_call_target="tpu_custom_call" | custom-call | flops 1 | bytes 1 | tf_op jit(solution)/shard_map/project_first/pallas_call | solution.py:71
  17.9 3.4 %collective-permute-done.3.refs_3_ = bf16[80,4096]{1,0:T(8,128)(2,1)S(1)} collective-permute-done((bf16[80,4096]{1,0:T(8,128)(2,1)S(1)}, bf16[80,4096]{1,0:T(8,128)(2,1)S(1)}, u32[]{:S(2)}, u32[]{:S(2)}) %collective-permute-start.3) | collective-permute-done | bytes 655392 | tf_op jit(solution)/shard_map/ppermute | solution.py:499
  22.3 1.8 %collective-permute-start.5 = (bf16[80,4096]{1,0:T(8,128)(2,1)S(1)}, bf16[80,4096]{1,0:T(8,128)(2,1)S(1)}, u32[]{:S(2)}, u32[]{:S(2)}) collective-permute-start(bf16[80,4096]{1,0:T(8,128)(2,1)S(1)} %get-tuple-element.66), channel_id=1, source_target_pairs={{0,1},{1,0},{2,3},{3,2},{4,5},{5,4},{6,7},{7,6},{8,9},{9,8},{10,11... | collective-permute-start | bytes 1966088 | tf_op jit(solution)/shard_map/ppermute | solution.py:511
  27.8 8.5 %project_5.1 = (bf16[5,80,1024]{2,1,0:T(8,128)(2,1)S(1)}, bf16[5,80,1024]{2,1,0:T(8,128)(2,1)S(1)}, f32[5,80,128]{2,1,0:T(8,128)S(1)}) custom-call(bf16[80,4096]{1,0:T(8,128)(2,1)S(1)} %collective-permute-done.5.refs_0_, bf16[80,4096]{1,0:T(8,128)(2,1)S(1)} %collective-permute-done.2.refs_1_, bf16[80,4096]{1,0:T(8,128)(2,1)S(1)} %collective-permute-done.6.refs_2_, ...), custom_call_target="tpu_custom_call" | custom-call | flops 1 | bytes 1 | tf_op jit(solution)/shard_map/project_5/pallas_call | solution.py:71
  36.3 2.1 %collective-permute-done.4.refs_0_ = bf16[80,4224]{1,0:T(8,128)(2,1)S(1)} collective-permute-done((bf16[80,4224]{1,0:T(8,128)(2,1)S(1)}, bf16[80,4224]{1,0:T(8,128)(2,1)S(1)}, u32[]{:S(2)}, u32[]{:S(2)}) %collective-permute-start.4) | collective-permute-done | bytes 675872 | tf_op jit(solution)/shard_map/ppermute | solution.py:499
  38.4 2.8 %collective-permute-start.9 = (bf16[80,4224]{1,0:T(8,128)(2,1)S(1)}, bf16[80,4224]{1,0:T(8,128)(2,1)S(1)}, u32[]{:S(2)}, u32[]{:S(2)}) collective-permute-start(bf16[80,4224]{1,0:T(8,128)(2,1)S(1)} %collective-permute-done.4.refs_0_), channel_id=1, source_target_pairs={{0,1},{1,0},{2,3},{3,2},{4,5},{5,4},{6,7},{7,6},{8,9},{9,8},{10,11... | collective-permute-start | bytes 2027528 | tf_op jit(solution)/shard_map/ppermute | solution.py:511
  42.9 3.7 %project_2.1 = (bf16[2,80,1024]{2,1,0:T(8,128)(2,1)S(1)}, bf16[2,80,1024]{2,1,0:T(8,128)(2,1)S(1)}, f32[2,80,128]{2,1,0:T(8,128)S(1)}) custom-call(bf16[80,4224]{1,0:T(8,128)(2,1)S(1)} %collective-permute-done.4.refs_0_, bf16[80,4224]{1,0:T(8,128)(2,1)S(1)} %collective-permute-done.9.refs_1_, bf16[4096,1024]{1,0:T(8,128)(2,1)S(1)} %get-tuple-element.67.refs_5_.refs_2_, ...), custom_call_target="tpu_custom_call" | custom-call | flops 1 | bytes 1 | tf_op jit(solution)/shard_map/project_2/pallas_call | solution.py:71
  46.7 1.9 %block_state.1 = (bf16[288,128]{1,0:T(8,128)(2,1)S(1)}, bf16[288,128]{1,0:T(8,128)(2,1)S(1)}, bf16[288,128]{1,0:T(8,128)(2,1)S(1)}, bf16[288,128]{1,0:T(8,128)(2...) custom-call(bf16[1,80,1024]{2,1,0:T(8,128)(2,1)S(1)} %get-tuple-elem, ...), custom_call_target="tpu_custom_call" | custom-call | flops 1 | bytes 1 | tf_op jit(solution)/shard_map/block_state/pallas_call | solution.py:71
  48.6 1.4 %collective-permute-start.11 = (bf16[288,128]{1,0:T(8,128)(2,1)S(1)}, bf16[288,128]{1,0:T(8,128)(2,1)S(1)}, u32[]{:S(2)}, u32[]{:S(2)}) collective-permute-start(bf16[288,128]{1,0:T(8,128)(2,1)S(1)} %get-tuple-element.88), channel_id=1, source_target_pairs={{0,2},{2,0},{4,6},{6,4},{8,10},{10,8},{12,14},{14,12},{16,18},{18,... | collective-permute-start | bytes 221192 | tf_op jit(solution)/shard_map/ppermute | solution.py:506
  50.0 2.6 %collective-permute-start.12 = (bf16[288,128]{1,0:T(8,128)(2,1)S(1)}, bf16[288,128]{1,0:T(8,128)(2,1)S(1)}, u32[]{:S(2)}, u32[]{:S(2)}) collective-permute-start(bf16[288,128]{1,0:T(8,128)(2,1)S(1)} %get-tuple-element.89), channel_id=1, source_target_pairs={{0,4},{2,6},{4,0},{6,2},{8,12},{10,14},{12,8},{14,10},{16,20},{18,... | collective-permute-start | bytes 221192 | tf_op jit(solution)/shard_map/ppermute | solution.py:506
  52.6 3.8 %inner_reads_3.1.refs_4_ = f32[3,2,80,1024]{3,2,1,0:T(8,128)S(1)} custom-call(bf16[8,80,1024]{2,1,0:T(8,128)(2,1)S(1)} %get-tuple-element.81.refs_0_, bf16[8,80,1024]{2,1,0:T(8,128)(2,1)S(1)} %get-tuple-element.82.refs_1_, f32[8,80,128]{2,1,0:T(8,128)S(1)} %get-tuple-element.83.refs_2_.refs_6_, f32[8,640]{1,0:T(8,128)S(1)} %get-tuple-element.84.refs_3_, ...), custom_call_target="tpu_custom_call" | custom-call | flops 1 | bytes 1 | tf_op jit(solution)/shard_map/inner_reads_3/pallas_call | solution.py:71
  57.6 1.6 %collective-permute-start.14 = (bf16[2,80,1024]{2,1,0:T(8,128)(2,1)S(1)}, bf16[2,80,1024]{2,1,0:T(8,128)(2,1)S(1)}, u32[]{:S(2)}, u32[]{:S(2)}) collective-permute-start(bf16[2,80,1024]{2,1,0:T(8,128)(2,1)S(1)} %get-tuple-element.92), channel_id=1, source_target_pairs={{0,64},{32,96},{64,0},{96,32},{1,65},{33,97},{65,1},{97,33},{2,66}... | collective-permute-start | bytes 983048 | tf_op jit(solution)/shard_map/ppermute | solution.py:499
  59.2 2.5 %collective-permute-start.17 = (bf16[288,128]{1,0:T(8,128)(2,1)S(1)}, bf16[288,128]{1,0:T(8,128)(2,1)S(1)}, u32[]{:S(2)}, u32[]{:S(2)}) collective-permute-start(bf16[288,128]{1,0:T(8,128)(2,1)S(1)} %get-tuple-element.91.refs_0_), channel_id=1, source_target_pairs={{0,24},{2,26},{4,28},{6,30},{8,16},{10,18},{12,20},{14,22},{16,8},... | collective-permute-start | bytes 221192 | tf_op jit(solution)/shard_map/ppermute | solution.py:506
  63.6 3.1 %collective-permute-done.16.refs_2_ = bf16[288,128]{1,0:T(8,128)(2,1)S(1)} collective-permute-done((bf16[288,128]{1,0:T(8,128)(2,1)S(1)}, bf16[288,128]{1,0:T(8,128)(2,1)S(1)}, u32[]{:S(2)}, u32[]{:S(2)}) %collective-permute-start.16) | collective-permute-done | bytes 73760 | tf_op jit(solution)/shard_map/ppermute | solution.py:506
  66.9 2.8 %collective-permute-start.19 = (bf16[256,128]{1,0:T(8,128)(2,1)S(1)}, bf16[256,128]{1,0:T(8,128)(2,1)S(1)}, u32[]{:S(2)}, u32[]{:S(2)}) collective-permute-start(bf16[256,128]{1,0:T(8,128)(2,1)S(1)} %get-tuple-element.97), channel_id=1, source_target_pairs={{0,4},{2,6},{4,0},{6,2},{8,12},{10,14},{12,8},{14,10},{16,20},{18,... | collective-permute-start | bytes 196616 | tf_op jit(solution)/shard_map/ppermute | solution.py:506
  70.8 2.9 %inner_reads_1.1.refs_5_ = f32[1,2,80,1024]{3,2,1,0:T(8,128)S(1)} custom-call(bf16[8,80,1024]{2,1,0:T(8,128)(2,1)S(1)} %get-tuple-element.81.refs_0_, bf16[8,80,1024]{2,1,0:T(8,128)(2,1)S(1)} %get-tuple-element.82.refs_1_, f32[8,80,128]{2,1,0:T(8,128)S(1)} %get-tuple-element.83.refs_2_.refs_6_, f32[8,640]{1,0:T(8,128)S(1)} %get-tuple-element.84.refs_3_, ...), custom_call_target="tpu_custom_call" | custom-call | flops 1 | bytes 1 | tf_op jit(solution)/shard_map/inner_reads_1/pallas_call | solution.py:71
  75.4 1.3 %collective-permute-start.22 = (bf16[2,80,1024]{2,1,0:T(8,128)(2,1)S(1)}, bf16[2,80,1024]{2,1,0:T(8,128)(2,1)S(1)}, u32[]{:S(2)}, u32[]{:S(2)}) collective-permute-start(bf16[2,80,1024]{2,1,0:T(8,128)(2,1)S(1)} %get-tuple-element.101), channel_id=1, source_target_pairs={{0,96},{32,64},{64,32},{96,0},{1,97},{33,65},{65,33},{97,1},{2,98}... | collective-permute-start | bytes 983048 | tf_op jit(solution)/shard_map/ppermute | solution.py:499
  76.7 1.6 %collective-permute-start.26 = (bf16[2,80,1024]{2,1,0:T(8,128)(2,1)S(1)}, bf16[2,80,1024]{2,1,0:T(8,128)(2,1)S(1)}, u32[]{:S(2)}, u32[]{:S(2)}) collective-permute-start(bf16[2,80,1024]{2,1,0:T(8,128)(2,1)S(1)} %get-tuple-element.102), channel_id=1, source_target_pairs={{0,64},{32,96},{64,0},{96,32},{1,65},{33,97},{65,1},{97,33},{2,66}... | collective-permute-start | bytes 983048 | tf_op jit(solution)/shard_map/ppermute | solution.py:499
  78.3 5.3 %collective-permute-start.23 = (bf16[2,80,1024]{2,1,0:T(8,128)(2,1)S(1)}, bf16[2,80,1024]{2,1,0:T(8,128)(2,1)S(1)}, u32[]{:S(2)}, u32[]{:S(2)}) collective-permute-start(bf16[2,80,1024]{2,1,0:T(8,128)(2,1)S(1)} %get-tuple-element.99.refs_0_), channel_id=1, source_target_pairs={{0,1},{1,0},{2,3},{3,2},{4,5},{5,4},{6,7},{7,6},{8,9},{9,8},{10,11... | collective-permute-start | bytes 983048 | tf_op jit(solution)/shard_map/ppermute | solution.py:511
  83.7 5.1 %collective-permute-start.24 = (bf16[2,80,1024]{2,1,0:T(8,128)(2,1)S(1)}, bf16[2,80,1024]{2,1,0:T(8,128)(2,1)S(1)}, u32[]{:S(2)}, u32[]{:S(2)}) collective-permute-start(bf16[2,80,1024]{2,1,0:T(8,128)(2,1)S(1)} %collective-permute-done.21.refs_1_), channel_id=1, source_target_pairs={{0,1},{1,0},{2,3},{3,2},{4,5},{5,4},{6,7},{7,6},{8,9},{9,8},{10,11... | collective-permute-start | bytes 983048 | tf_op jit(solution)/shard_map/ppermute | solution.py:511
  88.8 5.0 %collective-permute-start.25 = (bf16[2,80,1024]{2,1,0:T(8,128)(2,1)S(1)}, bf16[2,80,1024]{2,1,0:T(8,128)(2,1)S(1)}, u32[]{:S(2)}, u32[]{:S(2)}) collective-permute-start(bf16[2,80,1024]{2,1,0:T(8,128)(2,1)S(1)} %collective-permute-done.22.refs_2_), channel_id=1, source_target_pairs={{0,1},{1,0},{2,3},{3,2},{4,5},{5,4},{6,7},{7,6},{8,9},{9,8},{10,11... | collective-permute-start | bytes 983048 | tf_op jit(solution)/shard_map/ppermute | solution.py:511
  95.6 1.4 %mix_reads.1 = bf16[128,2048]{1,0:T(8,128)(2,1)} custom-call(f32[128,128]{1,0:T(8,128)S(1)} %get-tuple-element.56.gates_ref, bf16[4,128,128]{2,1,0:T(8,128)(2,1)S(1)} %get-tuple-element.57.picks_ref, f32[1,2048]{1,0:T(1,128)S(1)} %bitcast.26, f32[2,128,1024]{2,1,0:T(8,128)S(1)} %mix_near.1.partial, bf16[2,80,1024]{2,1,0:T(8,128)(2,1)S(1)} %collective-permute-done.26.own, ...), custom_call_target="tpu_custom_call" | custom-call | flops 1 | bytes 1 | tf_op jit(solution)/shard_map/mix_reads/pallas_call | solution.py:71
  (59 shorter events, 16.3 us)
Async XLA Ops:
  2.1 19.1 %collective-permute-start.3 = (bf16[80,4096]{1,0:T(8,128)(2,1)S(1)}, bf16[80,4096]{1,0:T(8,128)(2,1)S(1)}, u32[]{:S(2)}, u32[]{:S(2)}) collective-permute-start(bf16[80,4096]{1,0:T(8,128)(2,1)S(1)} %get-tuple-element.63), channel_id=1, source_target_pairs={{0,96},{32,64},{64,32},{96,0},{1,97},{33,65},{65,33},{97,1},{2,98}... | collective-permute-start | bytes 1966088 | tf_op jit(solution)/shard_map/ppermute | solution.py:499
  6.8 15.3 %collective-permute-start.2 = (bf16[80,4096]{1,0:T(8,128)(2,1)S(1)}, bf16[80,4096]{1,0:T(8,128)(2,1)S(1)}, u32[]{:S(2)}, u32[]{:S(2)}) collective-permute-start(bf16[80,4096]{1,0:T(8,128)(2,1)S(1)} %get-tuple-element.61), channel_id=1, source_target_pairs={{0,32},{32,0},{64,96},{96,64},{1,33},{33,1},{65,97},{97,65},{2,34}... | collective-permute-start | bytes 1966088 | tf_op jit(solution)/shard_map/ppermute | solution.py:499
  6.8 10.0 %collective-permute-start.1 = (bf16[128,2048]{1,0:T(8,128)(2,1)}, bf16[128,2048]{1,0:T(8,128)(2,1)S(1)}, u32[]{:S(2)}, u32[]{:S(2)}) collective-permute-start(bf16[128,2048]{1,0:T(8,128)(2,1)} %bitcast.19), channel_id=1, source_target_pairs={{0,1},{1,0},{2,3},{3,2},{4,5},{5,4},{6,7},{7,6},{8,9},{9,8},{10,11... | collective-permute-start | bytes 1572872 | tf_op jit(solution)/shard_map/ppermute | solution.py:511
  7.8 9.0 %collective-permute-start = (s32[2,128]{1,0:T(2,128)}, s32[2,128]{1,0:T(2,128)S(1)}, u32[]{:S(2)}, u32[]{:S(2)}) collective-permute-start(s32[2,128]{1,0:T(2,128)} %bitcast.23), channel_id=1, source_target_pairs={{0,1},{1,0},{2,3},{3,2},{4,5},{5,4},{6,7},{7,6},{8,9},{9,8},{10,11... | collective-permute-start | bytes 3080 | tf_op jit(solution)/shard_map/ppermute | solution.py:511
  22.1 16.3 %collective-permute-start.4 = (bf16[80,4224]{1,0:T(8,128)(2,1)S(1)}, bf16[80,4224]{1,0:T(8,128)(2,1)S(1)}, u32[]{:S(2)}, u32[]{:S(2)}) collective-permute-start(bf16[80,4224]{1,0:T(8,128)(2,1)S(1)} %get-tuple-element.65), channel_id=1, source_target_pairs={{0,64},{32,96},{64,0},{96,32},{1,65},{33,97},{65,1},{97,33},{2,66}... | collective-permute-start | bytes 2027528 | tf_op jit(solution)/shard_map/ppermute | solution.py:499
  38.4 4.5 %collective-permute-start.9 = (bf16[80,4224]{1,0:T(8,128)(2,1)S(1)}, bf16[80,4224]{1,0:T(8,128)(2,1)S(1)}, u32[]{:S(2)}, u32[]{:S(2)}) collective-permute-start(bf16[80,4224]{1,0:T(8,128)(2,1)S(1)} %collective-permute-done.4.refs_0_), channel_id=1, source_target_pairs={{0,1},{1,0},{2,3},{3,2},{4,5},{5,4},{6,7},{7,6},{8,9},{9,8},{10,11... | collective-permute-start | bytes 2027528 | tf_op jit(solution)/shard_map/ppermute | solution.py:511
  41.2 11.4 %collective-permute-start.8 = (bf16[2,80,1024]{2,1,0:T(8,128)(2,1)S(1)}, bf16[2,80,1024]{2,1,0:T(8,128)(2,1)S(1)}, u32[]{:S(2)}, u32[]{:S(2)}) collective-permute-start(bf16[2,80,1024]{2,1,0:T(8,128)(2,1)S(1)} %get-tuple-element.71), channel_id=1, source_target_pairs={{0,32},{32,0},{64,96},{96,64},{1,33},{33,1},{65,97},{97,65},{2,34}... | collective-permute-start | bytes 983048 | tf_op jit(solution)/shard_map/ppermute | solution.py:499
  41.5 11.1 %collective-permute-start.10 = (bf16[2,80,1024]{2,1,0:T(8,128)(2,1)S(1)}, bf16[2,80,1024]{2,1,0:T(8,128)(2,1)S(1)}, u32[]{:S(2)}, u32[]{:S(2)}) collective-permute-start(bf16[2,80,1024]{2,1,0:T(8,128)(2,1)S(1)} %get-tuple-element.86), channel_id=1, source_target_pairs={{0,96},{32,64},{64,32},{96,0},{1,97},{33,65},{65,33},{97,1},{2,98}... | collective-permute-start | bytes 983048 | tf_op jit(solution)/shard_map/ppermute | solution.py:499
  48.6 7.9 %collective-permute-start.11 = (bf16[288,128]{1,0:T(8,128)(2,1)S(1)}, bf16[288,128]{1,0:T(8,128)(2,1)S(1)}, u32[]{:S(2)}, u32[]{:S(2)}) collective-permute-start(bf16[288,128]{1,0:T(8,128)(2,1)S(1)} %get-tuple-element.88), channel_id=1, source_target_pairs={{0,2},{2,0},{4,6},{6,4},{8,10},{10,8},{12,14},{14,12},{16,18},{18,... | collective-permute-start | bytes 221192 | tf_op jit(solution)/shard_map/ppermute | solution.py:506
  50.0 6.5 %collective-permute-start.12 = (bf16[288,128]{1,0:T(8,128)(2,1)S(1)}, bf16[288,128]{1,0:T(8,128)(2,1)S(1)}, u32[]{:S(2)}, u32[]{:S(2)}) collective-permute-start(bf16[288,128]{1,0:T(8,128)(2,1)S(1)} %get-tuple-element.89), channel_id=1, source_target_pairs={{0,4},{2,6},{4,0},{6,2},{8,12},{10,14},{12,8},{14,10},{16,20},{18,... | collective-permute-start | bytes 221192 | tf_op jit(solution)/shard_map/ppermute | solution.py:506
  52.6 4.9 %collective-permute-start.13 = (bf16[288,128]{1,0:T(8,128)(2,1)S(1)}, bf16[288,128]{1,0:T(8,128)(2,1)S(1)}, u32[]{:S(2)}, u32[]{:S(2)}) collective-permute-start(bf16[288,128]{1,0:T(8,128)(2,1)S(1)} %get-tuple-element.90), channel_id=1, source_target_pairs={{0,6},{2,4},{4,2},{6,0},{8,14},{10,12},{12,10},{14,8},{16,22},{18,... | collective-permute-start | bytes 221192 | tf_op jit(solution)/shard_map/ppermute | solution.py:506
  57.6 13.2 %collective-permute-start.14 = (bf16[2,80,1024]{2,1,0:T(8,128)(2,1)S(1)}, bf16[2,80,1024]{2,1,0:T(8,128)(2,1)S(1)}, u32[]{:S(2)}, u32[]{:S(2)}) collective-permute-start(bf16[2,80,1024]{2,1,0:T(8,128)(2,1)S(1)} %get-tuple-element.92), channel_id=1, source_target_pairs={{0,64},{32,96},{64,0},{96,32},{1,65},{33,97},{65,1},{97,33},{2,66}... | collective-permute-start | bytes 983048 | tf_op jit(solution)/shard_map/ppermute | solution.py:499
  59.2 4.4 %collective-permute-start.17 = (bf16[288,128]{1,0:T(8,128)(2,1)S(1)}, bf16[288,128]{1,0:T(8,128)(2,1)S(1)}, u32[]{:S(2)}, u32[]{:S(2)}) collective-permute-start(bf16[288,128]{1,0:T(8,128)(2,1)S(1)} %get-tuple-element.91.refs_0_), channel_id=1, source_target_pairs={{0,24},{2,26},{4,28},{6,30},{8,16},{10,18},{12,20},{14,22},{16,8},... | collective-permute-start | bytes 221192 | tf_op jit(solution)/shard_map/ppermute | solution.py:506
  61.7 5.0 %collective-permute-start.16 = (bf16[288,128]{1,0:T(8,128)(2,1)S(1)}, bf16[288,128]{1,0:T(8,128)(2,1)S(1)}, u32[]{:S(2)}, u32[]{:S(2)}) collective-permute-start(bf16[288,128]{1,0:T(8,128)(2,1)S(1)} %get-tuple-element.91.refs_0_), channel_id=1, source_target_pairs={{0,16},{2,18},{4,20},{6,22},{8,24},{10,26},{12,28},{14,30},{16,0},... | collective-permute-start | bytes 221192 | tf_op jit(solution)/shard_map/ppermute | solution.py:506
  62.2 4.5 %collective-permute-start.15 = (bf16[288,128]{1,0:T(8,128)(2,1)S(1)}, bf16[288,128]{1,0:T(8,128)(2,1)S(1)}, u32[]{:S(2)}, u32[]{:S(2)}) collective-permute-start(bf16[288,128]{1,0:T(8,128)(2,1)S(1)} %get-tuple-element.91.refs_0_), channel_id=1, source_target_pairs={{0,8},{2,10},{4,12},{6,14},{8,0},{10,2},{12,4},{14,6},{16,24},{18,... | collective-permute-start | bytes 221192 | tf_op jit(solution)/shard_map/ppermute | solution.py:506
  66.8 6.9 %collective-permute-start.18 = (bf16[256,128]{1,0:T(8,128)(2,1)S(1)}, bf16[256,128]{1,0:T(8,128)(2,1)S(1)}, u32[]{:S(2)}, u32[]{:S(2)}) collective-permute-start(bf16[256,128]{1,0:T(8,128)(2,1)S(1)} %get-tuple-element.96), channel_id=1, source_target_pairs={{0,2},{2,0},{4,6},{6,4},{8,10},{10,8},{12,14},{14,12},{16,18},{18,... | collective-permute-start | bytes 196616 | tf_op jit(solution)/shard_map/ppermute | solution.py:506
  66.9 6.8 %collective-permute-start.19 = (bf16[256,128]{1,0:T(8,128)(2,1)S(1)}, bf16[256,128]{1,0:T(8,128)(2,1)S(1)}, u32[]{:S(2)}, u32[]{:S(2)}) collective-permute-start(bf16[256,128]{1,0:T(8,128)(2,1)S(1)} %get-tuple-element.97), channel_id=1, source_target_pairs={{0,4},{2,6},{4,0},{6,2},{8,12},{10,14},{12,8},{14,10},{16,20},{18,... | collective-permute-start | bytes 196616 | tf_op jit(solution)/shard_map/ppermute | solution.py:506
  69.7 4.3 %collective-permute-start.20 = (bf16[256,128]{1,0:T(8,128)(2,1)S(1)}, bf16[256,128]{1,0:T(8,128)(2,1)S(1)}, u32[]{:S(2)}, u32[]{:S(2)}) collective-permute-start(bf16[256,128]{1,0:T(8,128)(2,1)S(1)} %get-tuple-element.98), channel_id=1, source_target_pairs={{0,6},{2,4},{4,2},{6,0},{8,14},{10,12},{12,10},{14,8},{16,22},{18,... | collective-permute-start | bytes 196616 | tf_op jit(solution)/shard_map/ppermute | solution.py:506
  75.0 8.7 %collective-permute-start.21 = (bf16[2,80,1024]{2,1,0:T(8,128)(2,1)S(1)}, bf16[2,80,1024]{2,1,0:T(8,128)(2,1)S(1)}, u32[]{:S(2)}, u32[]{:S(2)}) collective-permute-start(bf16[2,80,1024]{2,1,0:T(8,128)(2,1)S(1)} %get-tuple-element.100), channel_id=1, source_target_pairs={{0,32},{32,0},{64,96},{96,64},{1,33},{33,1},{65,97},{97,65},{2,34}... | collective-permute-start | bytes 983048 | tf_op jit(solution)/shard_map/ppermute | solution.py:499
  75.4 13.4 %collective-permute-start.22 = (bf16[2,80,1024]{2,1,0:T(8,128)(2,1)S(1)}, bf16[2,80,1024]{2,1,0:T(8,128)(2,1)S(1)}, u32[]{:S(2)}, u32[]{:S(2)}) collective-permute-start(bf16[2,80,1024]{2,1,0:T(8,128)(2,1)S(1)} %get-tuple-element.101), channel_id=1, source_target_pairs={{0,96},{32,64},{64,32},{96,0},{1,97},{33,65},{65,33},{97,1},{2,98}... | collective-permute-start | bytes 983048 | tf_op jit(solution)/shard_map/ppermute | solution.py:499
  76.7 17.1 %collective-permute-start.26 = (bf16[2,80,1024]{2,1,0:T(8,128)(2,1)S(1)}, bf16[2,80,1024]{2,1,0:T(8,128)(2,1)S(1)}, u32[]{:S(2)}, u32[]{:S(2)}) collective-permute-start(bf16[2,80,1024]{2,1,0:T(8,128)(2,1)S(1)} %get-tuple-element.102), channel_id=1, source_target_pairs={{0,64},{32,96},{64,0},{96,32},{1,65},{33,97},{65,1},{97,33},{2,66}... | collective-permute-start | bytes 983048 | tf_op jit(solution)/shard_map/ppermute | solution.py:499
  78.3 15.5 %collective-permute-start.23 = (bf16[2,80,1024]{2,1,0:T(8,128)(2,1)S(1)}, bf16[2,80,1024]{2,1,0:T(8,128)(2,1)S(1)}, u32[]{:S(2)}, u32[]{:S(2)}) collective-permute-start(bf16[2,80,1024]{2,1,0:T(8,128)(2,1)S(1)} %get-tuple-element.99.refs_0_), channel_id=1, source_target_pairs={{0,1},{1,0},{2,3},{3,2},{4,5},{5,4},{6,7},{7,6},{8,9},{9,8},{10,11... | collective-permute-start | bytes 983048 | tf_op jit(solution)/shard_map/ppermute | solution.py:511
  83.7 10.1 %collective-permute-start.24 = (bf16[2,80,1024]{2,1,0:T(8,128)(2,1)S(1)}, bf16[2,80,1024]{2,1,0:T(8,128)(2,1)S(1)}, u32[]{:S(2)}, u32[]{:S(2)}) collective-permute-start(bf16[2,80,1024]{2,1,0:T(8,128)(2,1)S(1)} %collective-permute-done.21.refs_1_), channel_id=1, source_target_pairs={{0,1},{1,0},{2,3},{3,2},{4,5},{5,4},{6,7},{7,6},{8,9},{9,8},{10,11... | collective-permute-start | bytes 983048 | tf_op jit(solution)/shard_map/ppermute | solution.py:511
  88.8 6.3 %collective-permute-start.25 = (bf16[2,80,1024]{2,1,0:T(8,128)(2,1)S(1)}, bf16[2,80,1024]{2,1,0:T(8,128)(2,1)S(1)}, u32[]{:S(2)}, u32[]{:S(2)}) collective-permute-start(bf16[2,80,1024]{2,1,0:T(8,128)(2,1)S(1)} %collective-permute-done.22.refs_2_), channel_id=1, source_target_pairs={{0,1},{1,0},{2,3},{3,2},{4,5},{5,4},{6,7},{7,6},{8,9},{9,8},{10,11... | collective-permute-start | bytes 983048 | tf_op jit(solution)/shard_map/ppermute | solution.py:511
  (11 other events, 130.8 us)

commit v8 on v7

--- a/solution.py
+++ b/solution.py
@@ -403,22 +403,25 @@
     units, values, column_ref, row_ref = refs[0:4]
     query_refs, inner = refs[4:-1], refs[-1]
     owner = lax.axis_index("memory")
-    count = len(shifts) * CAP
-    for core in range(2):
-        reach = -(-(core + 1) * OWNERS * CAP // 128) * 128
-        chunks = [core * OWNERS + (owner ^ shift) for shift in shifts]
+    cores = [(0, 1)] if shifts == (FAR,) else [(0,), (1,)]
+    for group in cores:
+        reach = -(-(group[-1] + 1) * OWNERS * CAP // 128) * 128
+        tiles = [(at, shift, core) for core in group for at, shift in enumerate(shifts)]
+        chunks = [core * OWNERS + (owner ^ shift) for _, shift, core in tiles]
         running = jnp.concatenate([column_ref[chunk] for chunk in chunks], axis=0)
         place = jnp.concatenate([iota((CAP, reach), 0) + chunk * CAP for chunk in chunks], axis=0)
-        causal = place >= iota((count, reach), 1)
+        causal = place >= iota(place.shape, 1)
         for head in range(HEADS):
             columns = head_columns(head)
-            query = jnp.concatenate([query[core, :, columns] for query in query_refs], axis=0)
+            query = jnp.concatenate([query_refs[at][c, :, columns] for at, _, c in tiles], axis=0)
             unit = units[:, :, columns].reshape(SLOTS, HEAD_DIM)[:reach]
             value = values[:, :, columns].reshape(SLOTS, HEAD_DIM)[:reach]
             spread = running[:, head : head + 1] - row_ref[head : head + 1, :reach]
             weight = jnp.exp(jnp.where(causal, spread, -1e30))
             score = (dot_rows(query, unit) * weight).astype(BF16)
-            inner[:, core, :, columns] = dot(score, value).reshape(len(shifts), CAP, HEAD_DIM)
+            result = dot(score, value)
+            for row, (at, _, core) in enumerate(tiles):
+                inner[at, core, :, columns] = result[row * CAP : (row + 1) * CAP]
 
 
 def inner_reads(shifts, units, values, column, row, *queries):

time: 97.1 us -> 97.1 us (level)
  Pallas kernels: 36.1 us -> 35 us
  waiting for transfers between devices: 16.5 us -> 17.6 us
    pallas_call x13, Pallas kernels: 36.1 us -> 35 us  [kernel_call(): pl.pallas_call(kernel, out_shape=out_shape, in_specs=[pl.BlockSpec(memory...]
    ppermute x9, waiting for transfers between devices: 5.63 us -> 6.74 us  [exchange(): out.append(lax.ppermute(arrays[shift], 'context', pairs))]
  transfers between devices with their start and end apart: 28 -> 28, of which waited for: 12 -> 12; matrix products, arithmetic and copies ran while one was open for 0% -> 0% of each run, Pallas kernels for 33% -> 31%
where the time goes in v8:
time: 97.1 us; the launch traced here: 97 us
  starting transfers between devices  44.1 us (45%)
  Pallas kernels  35 us (36%)
  waiting for transfers between devices  17.6 us (18%)
    pallas_call x13, Pallas kernels, kernel_call(): pl.pallas_call(kernel, out_shape=out_shape, in_specs=[pl.BlockSpec(memory...  35 us
    ppermute x10, starting transfers between devices, swap(): return lax.ppermute(array, 'dp', [(0, 1), (1, 0)])  21.6 us
    ppermute x9, starting transfers between devices, hop(): lax.ppermute(array, 'memory', [(i, i ^ shift) for i in range(OWNERS)])  11.4 us
    ppermute x9, starting transfers between devices, exchange(): out.append(lax.ppermute(arrays[shift], 'context', pairs))  11.2 us
    ppermute x9, waiting for transfers between devices, exchange(): out.append(lax.ppermute(arrays[shift], 'context', pairs))  6.74 us
    ppermute x9, waiting for transfers between devices, hop(): lax.ppermute(array, 'memory', [(i, i ^ shift) for i in range(OWNERS)])  6.28 us
    ppermute x10, waiting for transfers between devices, swap(): return lax.ppermute(array, 'dp', [(0, 1), (1, 0)])  4.55 us
  transfers between devices with their start and end apart: 28, of which 12 were waited for; matrix products, arithmetic and copies ran while one was open for 0% of the time, Pallas kernels for 31%

profile of v8, /device:TPU:1, one launch (start us, length us, event | category | flops | bytes accessed | tf_op | source)
XLA Modules:
  0.0 97.0 jit_solution(2424283747604053745)
XLA Ops:
  0.0 2.1 %pack_rows.1 = (bf16[80,4096]{1,0:T(8,128)(2,1)S(1)}, bf16[80,4096]{1,0:T(8,128)(2,1)S(1)}, bf16[80,4224]{1,0:T(8,128)(2,1)S(1)}) custom-call(s32[2,128]{1,0:T(2,128)} %bitcast.22, bf16[128,4096]{1,0:T(8,128)(2,1)} %bitcast.13), custom_call_target="tpu_custom_call" | custom-call | flops 1 | bytes 1 | tf_op jit(solution)/shard_map/pack_rows/pallas_call | solution.py:71
  2.1 4.7 %collective-permute-start.3 = (bf16[80,4096]{1,0:T(8,128)(2,1)S(1)}, bf16[80,4096]{1,0:T(8,128)(2,1)S(1)}, u32[]{:S(2)}, u32[]{:S(2)}) collective-permute-start(bf16[80,4096]{1,0:T(8,128)(2,1)S(1)} %get-tuple-element.63), channel_id=1, source_target_pairs={{0,96},{32,64},{64,32},{96,0},{1,97},{33,65},{65,33},{97,1},{2,98}... | collective-permute-start | bytes 1966088 | tf_op jit(solution)/shard_map/ppermute | solution.py:502
  7.8 9.0 %project_first.1 = (bf16[1,80,1024]{2,1,0:T(8,128)(2,1)S(1)}, bf16[1,80,1024]{2,1,0:T(8,128)(2,1)S(1)}, f32[1,80,128]{2,1,0:T(8,128)S(1)}, bf16[4096,1024]{1,0:T...) custom-call(s32[2,128]{1,0:T(2,128)} %bitcast.24, bf16[128,4096]{1,0:T(8,128)(2,1)} %bitcast.14, ...), custom_call_target="tpu_custom_call" | custom-call | flops 1 | bytes 1 | tf_op jit(solution)/shard_map/project_first/pallas_call | solution.py:71
  17.9 3.4 %collective-permute-done.3.refs_3_ = bf16[80,4096]{1,0:T(8,128)(2,1)S(1)} collective-permute-done((bf16[80,4096]{1,0:T(8,128)(2,1)S(1)}, bf16[80,4096]{1,0:T(8,128)(2,1)S(1)}, u32[]{:S(2)}, u32[]{:S(2)}) %collective-permute-start.3) | collective-permute-done | bytes 655392 | tf_op jit(solution)/shard_map/ppermute | solution.py:502
  22.3 1.8 %collective-permute-start.5 = (bf16[80,4096]{1,0:T(8,128)(2,1)S(1)}, bf16[80,4096]{1,0:T(8,128)(2,1)S(1)}, u32[]{:S(2)}, u32[]{:S(2)}) collective-permute-start(bf16[80,4096]{1,0:T(8,128)(2,1)S(1)} %get-tuple-element.66), channel_id=1, source_target_pairs={{0,1},{1,0},{2,3},{3,2},{4,5},{5,4},{6,7},{7,6},{8,9},{9,8},{10,11... | collective-permute-start | bytes 1966088 | tf_op jit(solution)/shard_map/ppermute | solution.py:514
  27.8 8.5 %project_5.1 = (bf16[5,80,1024]{2,1,0:T(8,128)(2,1)S(1)}, bf16[5,80,1024]{2,1,0:T(8,128)(2,1)S(1)}, f32[5,80,128]{2,1,0:T(8,128)S(1)}) custom-call(bf16[80,4096]{1,0:T(8,128)(2,1)S(1)} %collective-permute-done.5.refs_0_, bf16[80,4096]{1,0:T(8,128)(2,1)S(1)} %collective-permute-done.2.refs_1_, bf16[80,4096]{1,0:T(8,128)(2,1)S(1)} %collective-permute-done.6.refs_2_, ...), custom_call_target="tpu_custom_call" | custom-call | flops 1 | bytes 1 | tf_op jit(solution)/shard_map/project_5/pallas_call | solution.py:71
  36.3 2.1 %collective-permute-done.4.refs_0_ = bf16[80,4224]{1,0:T(8,128)(2,1)S(1)} collective-permute-done((bf16[80,4224]{1,0:T(8,128)(2,1)S(1)}, bf16[80,4224]{1,0:T(8,128)(2,1)S(1)}, u32[]{:S(2)}, u32[]{:S(2)}) %collective-permute-start.4) | collective-permute-done | bytes 675872 | tf_op jit(solution)/shard_map/ppermute | solution.py:502
  38.4 2.8 %collective-permute-start.9 = (bf16[80,4224]{1,0:T(8,128)(2,1)S(1)}, bf16[80,4224]{1,0:T(8,128)(2,1)S(1)}, u32[]{:S(2)}, u32[]{:S(2)}) collective-permute-start(bf16[80,4224]{1,0:T(8,128)(2,1)S(1)} %collective-permute-done.4.refs_0_), channel_id=1, source_target_pairs={{0,1},{1,0},{2,3},{3,2},{4,5},{5,4},{6,7},{7,6},{8,9},{9,8},{10,11... | collective-permute-start | bytes 2027528 | tf_op jit(solution)/shard_map/ppermute | solution.py:514
  42.9 3.7 %project_2.1 = (bf16[2,80,1024]{2,1,0:T(8,128)(2,1)S(1)}, bf16[2,80,1024]{2,1,0:T(8,128)(2,1)S(1)}, f32[2,80,128]{2,1,0:T(8,128)S(1)}) custom-call(bf16[80,4224]{1,0:T(8,128)(2,1)S(1)} %collective-permute-done.4.refs_0_, bf16[80,4224]{1,0:T(8,128)(2,1)S(1)} %collective-permute-done.9.refs_1_, bf16[4096,1024]{1,0:T(8,128)(2,1)S(1)} %get-tuple-element.67.refs_5_.refs_2_, ...), custom_call_target="tpu_custom_call" | custom-call | flops 1 | bytes 1 | tf_op jit(solution)/shard_map/project_2/pallas_call | solution.py:71
  46.7 1.9 %block_state.1 = (bf16[288,128]{1,0:T(8,128)(2,1)S(1)}, bf16[288,128]{1,0:T(8,128)(2,1)S(1)}, bf16[288,128]{1,0:T(8,128)(2,1)S(1)}, bf16[288,128]{1,0:T(8,128)(2...) custom-call(bf16[1,80,1024]{2,1,0:T(8,128)(2,1)S(1)} %get-tuple-elem, ...), custom_call_target="tpu_custom_call" | custom-call | flops 1 | bytes 1 | tf_op jit(solution)/shard_map/block_state/pallas_call | solution.py:71
  48.6 1.4 %collective-permute-start.11 = (bf16[288,128]{1,0:T(8,128)(2,1)S(1)}, bf16[288,128]{1,0:T(8,128)(2,1)S(1)}, u32[]{:S(2)}, u32[]{:S(2)}) collective-permute-start(bf16[288,128]{1,0:T(8,128)(2,1)S(1)} %get-tuple-element.88), channel_id=1, source_target_pairs={{0,2},{2,0},{4,6},{6,4},{8,10},{10,8},{12,14},{14,12},{16,18},{18,... | collective-permute-start | bytes 221192 | tf_op jit(solution)/shard_map/ppermute | solution.py:509
  50.0 2.6 %collective-permute-start.12 = (bf16[288,128]{1,0:T(8,128)(2,1)S(1)}, bf16[288,128]{1,0:T(8,128)(2,1)S(1)}, u32[]{:S(2)}, u32[]{:S(2)}) collective-permute-start(bf16[288,128]{1,0:T(8,128)(2,1)S(1)} %get-tuple-element.89), channel_id=1, source_target_pairs={{0,4},{2,6},{4,0},{6,2},{8,12},{10,14},{12,8},{14,10},{16,20},{18,... | collective-permute-start | bytes 221192 | tf_op jit(solution)/shard_map/ppermute | solution.py:509
  52.6 3.8 %inner_reads_3.1.refs_4_ = f32[3,2,80,1024]{3,2,1,0:T(8,128)S(1)} custom-call(bf16[8,80,1024]{2,1,0:T(8,128)(2,1)S(1)} %get-tuple-element.81.refs_0_, bf16[8,80,1024]{2,1,0:T(8,128)(2,1)S(1)} %get-tuple-element.82.refs_1_, f32[8,80,128]{2,1,0:T(8,128)S(1)} %get-tuple-element.83.refs_2_.refs_6_, f32[8,640]{1,0:T(8,128)S(1)} %get-tuple-element.84.refs_3_, ...), custom_call_target="tpu_custom_call" | custom-call | flops 1 | bytes 1 | tf_op jit(solution)/shard_map/inner_reads_3/pallas_call | solution.py:71
  57.6 1.6 %collective-permute-start.14 = (bf16[2,80,1024]{2,1,0:T(8,128)(2,1)S(1)}, bf16[2,80,1024]{2,1,0:T(8,128)(2,1)S(1)}, u32[]{:S(2)}, u32[]{:S(2)}) collective-permute-start(bf16[2,80,1024]{2,1,0:T(8,128)(2,1)S(1)} %get-tuple-element.92), channel_id=1, source_target_pairs={{0,64},{32,96},{64,0},{96,32},{1,65},{33,97},{65,1},{97,33},{2,66}... | collective-permute-start | bytes 983048 | tf_op jit(solution)/shard_map/ppermute | solution.py:502
  59.2 2.5 %collective-permute-start.17 = (bf16[288,128]{1,0:T(8,128)(2,1)S(1)}, bf16[288,128]{1,0:T(8,128)(2,1)S(1)}, u32[]{:S(2)}, u32[]{:S(2)}) collective-permute-start(bf16[288,128]{1,0:T(8,128)(2,1)S(1)} %get-tuple-element.91.refs_0_), channel_id=1, source_target_pairs={{0,24},{2,26},{4,28},{6,30},{8,16},{10,18},{12,20},{14,22},{16,8},... | collective-permute-start | bytes 221192 | tf_op jit(solution)/shard_map/ppermute | solution.py:509
  63.6 3.1 %collective-permute-done.16.refs_2_ = bf16[288,128]{1,0:T(8,128)(2,1)S(1)} collective-permute-done((bf16[288,128]{1,0:T(8,128)(2,1)S(1)}, bf16[288,128]{1,0:T(8,128)(2,1)S(1)}, u32[]{:S(2)}, u32[]{:S(2)}) %collective-permute-start.16) | collective-permute-done | bytes 73760 | tf_op jit(solution)/shard_map/ppermute | solution.py:509
  66.9 2.8 %collective-permute-start.19 = (bf16[256,128]{1,0:T(8,128)(2,1)S(1)}, bf16[256,128]{1,0:T(8,128)(2,1)S(1)}, u32[]{:S(2)}, u32[]{:S(2)}) collective-permute-start(bf16[256,128]{1,0:T(8,128)(2,1)S(1)} %get-tuple-element.97), channel_id=1, source_target_pairs={{0,4},{2,6},{4,0},{6,2},{8,12},{10,14},{12,8},{14,10},{16,20},{18,... | collective-permute-start | bytes 196616 | tf_op jit(solution)/shard_map/ppermute | solution.py:509
  70.8 1.8 %inner_reads_1.1.refs_5_ = f32[1,2,80,1024]{3,2,1,0:T(8,128)S(1)} custom-call(bf16[8,80,1024]{2,1,0:T(8,128)(2,1)S(1)} %get-tuple-element.81.refs_0_, bf16[8,80,1024]{2,1,0:T(8,128)(2,1)S(1)} %get-tuple-element.82.refs_1_, f32[8,80,128]{2,1,0:T(8,128)S(1)} %get-tuple-element.83.refs_2_.refs_6_, f32[8,640]{1,0:T(8,128)S(1)} %get-tuple-element.84.refs_3_, ...), custom_call_target="tpu_custom_call" | custom-call | flops 1 | bytes 1 | tf_op jit(solution)/shard_map/inner_reads_1/pallas_call | solution.py:71
  72.6 1.5 %collective-permute-done.20.refs_10_ = bf16[256,128]{1,0:T(8,128)(2,1)S(1)} collective-permute-done((bf16[256,128]{1,0:T(8,128)(2,1)S(1)}, bf16[256,128]{1,0:T(8,128)(2,1)S(1)}, u32[]{:S(2)}, u32[]{:S(2)}) %collective-permute-start.20) | collective-permute-done | bytes 65568 | tf_op jit(solution)/shard_map/ppermute | solution.py:509
  76.7 1.6 %collective-permute-start.26 = (bf16[2,80,1024]{2,1,0:T(8,128)(2,1)S(1)}, bf16[2,80,1024]{2,1,0:T(8,128)(2,1)S(1)}, u32[]{:S(2)}, u32[]{:S(2)}) collective-permute-start(bf16[2,80,1024]{2,1,0:T(8,128)(2,1)S(1)} %get-tuple-element.102), channel_id=1, source_target_pairs={{0,64},{32,96},{64,0},{96,32},{1,65},{33,97},{65,1},{97,33},{2,66}... | collective-permute-start | bytes 983048 | tf_op jit(solution)/shard_map/ppermute | solution.py:502
  78.3 5.3 %collective-permute-start.23 = (bf16[2,80,1024]{2,1,0:T(8,128)(2,1)S(1)}, bf16[2,80,1024]{2,1,0:T(8,128)(2,1)S(1)}, u32[]{:S(2)}, u32[]{:S(2)}) collective-permute-start(bf16[2,80,1024]{2,1,0:T(8,128)(2,1)S(1)} %get-tuple-element.99.refs_0_), channel_id=1, source_target_pairs={{0,1},{1,0},{2,3},{3,2},{4,5},{5,4},{6,7},{7,6},{8,9},{9,8},{10,11... | collective-permute-start | bytes 983048 | tf_op jit(solution)/shard_map/ppermute | solution.py:514
  83.7 5.1 %collective-permute-start.24 = (bf16[2,80,1024]{2,1,0:T(8,128)(2,1)S(1)}, bf16[2,80,1024]{2,1,0:T(8,128)(2,1)S(1)}, u32[]{:S(2)}, u32[]{:S(2)}) collective-permute-start(bf16[2,80,1024]{2,1,0:T(8,128)(2,1)S(1)} %collective-permute-done.21.refs_1_), channel_id=1, source_target_pairs={{0,1},{1,0},{2,3},{3,2},{4,5},{5,4},{6,7},{7,6},{8,9},{9,8},{10,11... | collective-permute-start | bytes 983048 | tf_op jit(solution)/shard_map/ppermute | solution.py:514
  88.8 5.0 %collective-permute-start.25 = (bf16[2,80,1024]{2,1,0:T(8,128)(2,1)S(1)}, bf16[2,80,1024]{2,1,0:T(8,128)(2,1)S(1)}, u32[]{:S(2)}, u32[]{:S(2)}) collective-permute-start(bf16[2,80,1024]{2,1,0:T(8,128)(2,1)S(1)} %collective-permute-done.22.refs_2_), channel_id=1, source_target_pairs={{0,1},{1,0},{2,3},{3,2},{4,5},{5,4},{6,7},{7,6},{8,9},{9,8},{10,11... | collective-permute-start | bytes 983048 | tf_op jit(solution)/shard_map/ppermute | solution.py:514
  95.6 1.4 %mix_reads.1 = bf16[128,2048]{1,0:T(8,128)(2,1)} custom-call(f32[128,128]{1,0:T(8,128)S(1)} %get-tuple-element.56.gates_ref, bf16[4,128,128]{2,1,0:T(8,128)(2,1)S(1)} %get-tuple-element.57.picks_ref, f32[1,2048]{1,0:T(1,128)S(1)} %bitcast.26, f32[2,128,1024]{2,1,0:T(8,128)S(1)} %mix_near.1.partial, bf16[2,80,1024]{2,1,0:T(8,128)(2,1)S(1)} %collective-permute-done.26.own, ...), custom_call_target="tpu_custom_call" | custom-call | flops 1 | bytes 1 | tf_op jit(solution)/shard_map/mix_reads/pallas_call | solution.py:71
  (59 shorter events, 17.2 us)
Async XLA Ops:
  2.1 19.1 %collective-permute-start.3 = (bf16[80,4096]{1,0:T(8,128)(2,1)S(1)}, bf16[80,4096]{1,0:T(8,128)(2,1)S(1)}, u32[]{:S(2)}, u32[]{:S(2)}) collective-permute-start(bf16[80,4096]{1,0:T(8,128)(2,1)S(1)} %get-tuple-element.63), channel_id=1, source_target_pairs={{0,96},{32,64},{64,32},{96,0},{1,97},{33,65},{65,33},{97,1},{2,98}... | collective-permute-start | bytes 1966088 | tf_op jit(solution)/shard_map/ppermute | solution.py:502
  6.8 15.3 %collective-permute-start.2 = (bf16[80,4096]{1,0:T(8,128)(2,1)S(1)}, bf16[80,4096]{1,0:T(8,128)(2,1)S(1)}, u32[]{:S(2)}, u32[]{:S(2)}) collective-permute-start(bf16[80,4096]{1,0:T(8,128)(2,1)S(1)} %get-tuple-element.61), channel_id=1, source_target_pairs={{0,32},{32,0},{64,96},{96,64},{1,33},{33,1},{65,97},{97,65},{2,34}... | collective-permute-start | bytes 1966088 | tf_op jit(solution)/shard_map/ppermute | solution.py:502
  6.8 10.0 %collective-permute-start.1 = (bf16[128,2048]{1,0:T(8,128)(2,1)}, bf16[128,2048]{1,0:T(8,128)(2,1)S(1)}, u32[]{:S(2)}, u32[]{:S(2)}) collective-permute-start(bf16[128,2048]{1,0:T(8,128)(2,1)} %bitcast.19), channel_id=1, source_target_pairs={{0,1},{1,0},{2,3},{3,2},{4,5},{5,4},{6,7},{7,6},{8,9},{9,8},{10,11... | collective-permute-start | bytes 1572872 | tf_op jit(solution)/shard_map/ppermute | solution.py:514
  7.8 9.0 %collective-permute-start = (s32[2,128]{1,0:T(2,128)}, s32[2,128]{1,0:T(2,128)S(1)}, u32[]{:S(2)}, u32[]{:S(2)}) collective-permute-start(s32[2,128]{1,0:T(2,128)} %bitcast.23), channel_id=1, source_target_pairs={{0,1},{1,0},{2,3},{3,2},{4,5},{5,4},{6,7},{7,6},{8,9},{9,8},{10,11... | collective-permute-start | bytes 3080 | tf_op jit(solution)/shard_map/ppermute | solution.py:514
  22.1 16.3 %collective-permute-start.4 = (bf16[80,4224]{1,0:T(8,128)(2,1)S(1)}, bf16[80,4224]{1,0:T(8,128)(2,1)S(1)}, u32[]{:S(2)}, u32[]{:S(2)}) collective-permute-start(bf16[80,4224]{1,0:T(8,128)(2,1)S(1)} %get-tuple-element.65), channel_id=1, source_target_pairs={{0,64},{32,96},{64,0},{96,32},{1,65},{33,97},{65,1},{97,33},{2,66}... | collective-permute-start | bytes 2027528 | tf_op jit(solution)/shard_map/ppermute | solution.py:502
  38.4 4.5 %collective-permute-start.9 = (bf16[80,4224]{1,0:T(8,128)(2,1)S(1)}, bf16[80,4224]{1,0:T(8,128)(2,1)S(1)}, u32[]{:S(2)}, u32[]{:S(2)}) collective-permute-start(bf16[80,4224]{1,0:T(8,128)(2,1)S(1)} %collective-permute-done.4.refs_0_), channel_id=1, source_target_pairs={{0,1},{1,0},{2,3},{3,2},{4,5},{5,4},{6,7},{7,6},{8,9},{9,8},{10,11... | collective-permute-start | bytes 2027528 | tf_op jit(solution)/shard_map/ppermute | solution.py:514
  41.2 11.4 %collective-permute-start.8 = (bf16[2,80,1024]{2,1,0:T(8,128)(2,1)S(1)}, bf16[2,80,1024]{2,1,0:T(8,128)(2,1)S(1)}, u32[]{:S(2)}, u32[]{:S(2)}) collective-permute-start(bf16[2,80,1024]{2,1,0:T(8,128)(2,1)S(1)} %get-tuple-element.71), channel_id=1, source_target_pairs={{0,32},{32,0},{64,96},{96,64},{1,33},{33,1},{65,97},{97,65},{2,34}... | collective-permute-start | bytes 983048 | tf_op jit(solution)/shard_map/ppermute | solution.py:502
  41.5 11.1 %collective-permute-start.10 = (bf16[2,80,1024]{2,1,0:T(8,128)(2,1)S(1)}, bf16[2,80,1024]{2,1,0:T(8,128)(2,1)S(1)}, u32[]{:S(2)}, u32[]{:S(2)}) collective-permute-start(bf16[2,80,1024]{2,1,0:T(8,128)(2,1)S(1)} %get-tuple-element.86), channel_id=1, source_target_pairs={{0,96},{32,64},{64,32},{96,0},{1,97},{33,65},{65,33},{97,1},{2,98}... | collective-permute-start | bytes 983048 | tf_op jit(solution)/shard_map/ppermute | solution.py:502
  48.6 7.9 %collective-permute-start.11 = (bf16[288,128]{1,0:T(8,128)(2,1)S(1)}, bf16[288,128]{1,0:T(8,128)(2,1)S(1)}, u32[]{:S(2)}, u32[]{:S(2)}) collective-permute-start(bf16[288,128]{1,0:T(8,128)(2,1)S(1)} %get-tuple-element.88), channel_id=1, source_target_pairs={{0,2},{2,0},{4,6},{6,4},{8,10},{10,8},{12,14},{14,12},{16,18},{18,... | collective-permute-start | bytes 221192 | tf_op jit(solution)/shard_map/ppermute | solution.py:509
  50.0 6.5 %collective-permute-start.12 = (bf16[288,128]{1,0:T(8,128)(2,1)S(1)}, bf16[288,128]{1,0:T(8,128)(2,1)S(1)}, u32[]{:S(2)}, u32[]{:S(2)}) collective-permute-start(bf16[288,128]{1,0:T(8,128)(2,1)S(1)} %get-tuple-element.89), channel_id=1, source_target_pairs={{0,4},{2,6},{4,0},{6,2},{8,12},{10,14},{12,8},{14,10},{16,20},{18,... | collective-permute-start | bytes 221192 | tf_op jit(solution)/shard_map/ppermute | solution.py:509
  52.6 4.9 %collective-permute-start.13 = (bf16[288,128]{1,0:T(8,128)(2,1)S(1)}, bf16[288,128]{1,0:T(8,128)(2,1)S(1)}, u32[]{:S(2)}, u32[]{:S(2)}) collective-permute-start(bf16[288,128]{1,0:T(8,128)(2,1)S(1)} %get-tuple-element.90), channel_id=1, source_target_pairs={{0,6},{2,4},{4,2},{6,0},{8,14},{10,12},{12,10},{14,8},{16,22},{18,... | collective-permute-start | bytes 221192 | tf_op jit(solution)/shard_map/ppermute | solution.py:509
  57.6 13.2 %collective-permute-start.14 = (bf16[2,80,1024]{2,1,0:T(8,128)(2,1)S(1)}, bf16[2,80,1024]{2,1,0:T(8,128)(2,1)S(1)}, u32[]{:S(2)}, u32[]{:S(2)}) collective-permute-start(bf16[2,80,1024]{2,1,0:T(8,128)(2,1)S(1)} %get-tuple-element.92), channel_id=1, source_target_pairs={{0,64},{32,96},{64,0},{96,32},{1,65},{33,97},{65,1},{97,33},{2,66}... | collective-permute-start | bytes 983048 | tf_op jit(solution)/shard_map/ppermute | solution.py:502
  59.2 4.4 %collective-permute-start.17 = (bf16[288,128]{1,0:T(8,128)(2,1)S(1)}, bf16[288,128]{1,0:T(8,128)(2,1)S(1)}, u32[]{:S(2)}, u32[]{:S(2)}) collective-permute-start(bf16[288,128]{1,0:T(8,128)(2,1)S(1)} %get-tuple-element.91.refs_0_), channel_id=1, source_target_pairs={{0,24},{2,26},{4,28},{6,30},{8,16},{10,18},{12,20},{14,22},{16,8},... | collective-permute-start | bytes 221192 | tf_op jit(solution)/shard_map/ppermute | solution.py:509
  61.7 5.0 %collective-permute-start.16 = (bf16[288,128]{1,0:T(8,128)(2,1)S(1)}, bf16[288,128]{1,0:T(8,128)(2,1)S(1)}, u32[]{:S(2)}, u32[]{:S(2)}) collective-permute-start(bf16[288,128]{1,0:T(8,128)(2,1)S(1)} %get-tuple-element.91.refs_0_), channel_id=1, source_target_pairs={{0,16},{2,18},{4,20},{6,22},{8,24},{10,26},{12,28},{14,30},{16,0},... | collective-permute-start | bytes 221192 | tf_op jit(solution)/shard_map/ppermute | solution.py:509
  62.2 4.5 %collective-permute-start.15 = (bf16[288,128]{1,0:T(8,128)(2,1)S(1)}, bf16[288,128]{1,0:T(8,128)(2,1)S(1)}, u32[]{:S(2)}, u32[]{:S(2)}) collective-permute-start(bf16[288,128]{1,0:T(8,128)(2,1)S(1)} %get-tuple-element.91.refs_0_), channel_id=1, source_target_pairs={{0,8},{2,10},{4,12},{6,14},{8,0},{10,2},{12,4},{14,6},{16,24},{18,... | collective-permute-start | bytes 221192 | tf_op jit(solution)/shard_map/ppermute | solution.py:509
  66.8 5.7 %collective-permute-start.18 = (bf16[256,128]{1,0:T(8,128)(2,1)S(1)}, bf16[256,128]{1,0:T(8,128)(2,1)S(1)}, u32[]{:S(2)}, u32[]{:S(2)}) collective-permute-start(bf16[256,128]{1,0:T(8,128)(2,1)S(1)} %get-tuple-element.96), channel_id=1, source_target_pairs={{0,2},{2,0},{4,6},{6,4},{8,10},{10,8},{12,14},{14,12},{16,18},{18,... | collective-permute-start | bytes 196616 | tf_op jit(solution)/shard_map/ppermute | solution.py:509
  66.9 5.7 %collective-permute-start.19 = (bf16[256,128]{1,0:T(8,128)(2,1)S(1)}, bf16[256,128]{1,0:T(8,128)(2,1)S(1)}, u32[]{:S(2)}, u32[]{:S(2)}) collective-permute-start(bf16[256,128]{1,0:T(8,128)(2,1)S(1)} %get-tuple-element.97), channel_id=1, source_target_pairs={{0,4},{2,6},{4,0},{6,2},{8,12},{10,14},{12,8},{14,10},{16,20},{18,... | collective-permute-start | bytes 196616 | tf_op jit(solution)/shard_map/ppermute | solution.py:509
  69.7 4.3 %collective-permute-start.20 = (bf16[256,128]{1,0:T(8,128)(2,1)S(1)}, bf16[256,128]{1,0:T(8,128)(2,1)S(1)}, u32[]{:S(2)}, u32[]{:S(2)}) collective-permute-start(bf16[256,128]{1,0:T(8,128)(2,1)S(1)} %get-tuple-element.98), channel_id=1, source_target_pairs={{0,6},{2,4},{4,2},{6,0},{8,14},{10,12},{12,10},{14,8},{16,22},{18,... | collective-permute-start | bytes 196616 | tf_op jit(solution)/shard_map/ppermute | solution.py:509
  75.0 8.7 %collective-permute-start.21 = (bf16[2,80,1024]{2,1,0:T(8,128)(2,1)S(1)}, bf16[2,80,1024]{2,1,0:T(8,128)(2,1)S(1)}, u32[]{:S(2)}, u32[]{:S(2)}) collective-permute-start(bf16[2,80,1024]{2,1,0:T(8,128)(2,1)S(1)} %get-tuple-element.100), channel_id=1, source_target_pairs={{0,32},{32,0},{64,96},{96,64},{1,33},{33,1},{65,97},{97,65},{2,34}... | collective-permute-start | bytes 983048 | tf_op jit(solution)/shard_map/ppermute | solution.py:502
  75.4 13.4 %collective-permute-start.22 = (bf16[2,80,1024]{2,1,0:T(8,128)(2,1)S(1)}, bf16[2,80,1024]{2,1,0:T(8,128)(2,1)S(1)}, u32[]{:S(2)}, u32[]{:S(2)}) collective-permute-start(bf16[2,80,1024]{2,1,0:T(8,128)(2,1)S(1)} %get-tuple-element.101), channel_id=1, source_target_pairs={{0,96},{32,64},{64,32},{96,0},{1,97},{33,65},{65,33},{97,1},{2,98}... | collective-permute-start | bytes 983048 | tf_op jit(solution)/shard_map/ppermute | solution.py:502
  76.7 17.1 %collective-permute-start.26 = (bf16[2,80,1024]{2,1,0:T(8,128)(2,1)S(1)}, bf16[2,80,1024]{2,1,0:T(8,128)(2,1)S(1)}, u32[]{:S(2)}, u32[]{:S(2)}) collective-permute-start(bf16[2,80,1024]{2,1,0:T(8,128)(2,1)S(1)} %get-tuple-element.102), channel_id=1, source_target_pairs={{0,64},{32,96},{64,0},{96,32},{1,65},{33,97},{65,1},{97,33},{2,66}... | collective-permute-start | bytes 983048 | tf_op jit(solution)/shard_map/ppermute | solution.py:502
  78.3 15.5 %collective-permute-start.23 = (bf16[2,80,1024]{2,1,0:T(8,128)(2,1)S(1)}, bf16[2,80,1024]{2,1,0:T(8,128)(2,1)S(1)}, u32[]{:S(2)}, u32[]{:S(2)}) collective-permute-start(bf16[2,80,1024]{2,1,0:T(8,128)(2,1)S(1)} %get-tuple-element.99.refs_0_), channel_id=1, source_target_pairs={{0,1},{1,0},{2,3},{3,2},{4,5},{5,4},{6,7},{7,6},{8,9},{9,8},{10,11... | collective-permute-start | bytes 983048 | tf_op jit(solution)/shard_map/ppermute | solution.py:514
  83.7 10.1 %collective-permute-start.24 = (bf16[2,80,1024]{2,1,0:T(8,128)(2,1)S(1)}, bf16[2,80,1024]{2,1,0:T(8,128)(2,1)S(1)}, u32[]{:S(2)}, u32[]{:S(2)}) collective-permute-start(bf16[2,80,1024]{2,1,0:T(8,128)(2,1)S(1)} %collective-permute-done.21.refs_1_), channel_id=1, source_target_pairs={{0,1},{1,0},{2,3},{3,2},{4,5},{5,4},{6,7},{7,6},{8,9},{9,8},{10,11... | collective-permute-start | bytes 983048 | tf_op jit(solution)/shard_map/ppermute | solution.py:514
  88.8 6.3 %collective-permute-start.25 = (bf16[2,80,1024]{2,1,0:T(8,128)(2,1)S(1)}, bf16[2,80,1024]{2,1,0:T(8,128)(2,1)S(1)}, u32[]{:S(2)}, u32[]{:S(2)}) collective-permute-start(bf16[2,80,1024]{2,1,0:T(8,128)(2,1)S(1)} %collective-permute-done.22.refs_2_), channel_id=1, source_target_pairs={{0,1},{1,0},{2,3},{3,2},{4,5},{5,4},{6,7},{7,6},{8,9},{9,8},{10,11... | collective-permute-start | bytes 983048 | tf_op jit(solution)/shard_map/ppermute | solution.py:514
  (11 other events, 130.8 us)
